TPU v7x, 256 devices: a whole 4x4x8 slice. The times are simulated.
256 devices in a mesh: tm: 16 (over z, y_hi), az: 2 (over y_lo), rg: 8 (over x, core).
Axes of the slice: x: 4, y: 4 (y_hi: 2, y_lo: 2; y = y_hi * 2 + y_lo), z: 8, core: 2. Of those that a mesh axis runs over, the one named last changes fastest.
Arguments:
- slc: bfloat16 [16, 2, 128, 4096], P('tm', None, 'az', 'rg')
- pairs: int32 [16, 3], P('tm'), may hold values from 0 to 15, as said below
Outputs:
- filtered: float32 [16, 3, 2, 32, 256], P('tm', None, None, 'az', 'rg')
- coherence: float32 [16, 3, 32, 256], P('tm', None, 'az', 'rg')
Inputs may be any that keep to these rules, and one draw needn't show every extreme that they name: `pairs`: row a holds 3 different acquisitions, each between 1 and 3 away from a.
All inputs are finite; a program needn't handle non-finite values.
Results may differ from a plain program's by a relative error of at most 0.0003.
Values may be sent and summed in bfloat16 or wider, within the bound.
No kernel may reach another device: no remote copies, remote signals or barrier semaphores. Data moves between devices by JAX's collectives and lax.ppermute only.
A program may use at most 128 MiB of HBM per device.

v0:
```python
import math

import jax
import jax.numpy as jnp
from jax import lax
from jax.sharding import PartitionSpec as P


def passed_along(value, axis, by):
    count = lax.axis_size(axis)
    pairs = [(i, i + by) for i in range(count) if 0 <= i + by < count]
    return lax.ppermute(value, axis, pairs)


def extended(value, sides, width):
    for axis, dim in sides:
        count, length = (lax.axis_size(axis), value.shape[dim])
        up = [(i, (i + 1) % count) for i in range(count - 1)]
        down = [(j, i) for i, j in up]
        last = lax.slice_in_dim(value, length - width, length, axis=dim)
        initial = lax.slice_in_dim(value, 0, width, axis=dim)
        before = lax.ppermute(last, axis, up)
        after = lax.ppermute(initial, axis, down)
        value = jnp.concatenate([before, value, after], axis=dim)
    return value


def multilook(values):
    lines = values.shape[-2]
    columns = values.shape[-1]
    shaped = values.reshape(values.shape[:-2] + (lines // 4, 4, columns // 16, 16))
    return jnp.sum(shaped, axis=(-3, -1)) / 64.0


def pair_fields(own_tile, remote_tiles):
    own_real = own_tile[0].astype(jnp.float32)
    own_imag = own_tile[1].astype(jnp.float32)
    far_real = remote_tiles[:, 0].astype(jnp.float32)
    far_imag = remote_tiles[:, 1].astype(jnp.float32)
    cross_real = multilook(own_real * far_real + own_imag * far_imag)
    cross_imag = multilook(own_imag * far_real - own_real * far_imag)
    far_power = multilook(far_real * far_real + far_imag * far_imag)
    own_power = multilook(own_real * own_real + own_imag * own_imag)[None]
    return jnp.concatenate([cross_real, cross_imag, far_power, own_power], axis=0)


def cut_patches(values):
    lines = values.shape[-2]
    columns = values.shape[-1]
    leading = values.shape[:-2]
    blocks = values.reshape(leading + (lines // 16, 16, columns // 16, 16))
    by_rows = jnp.concatenate([blocks[..., :-1, :, :, :], blocks[..., 1:, :, :, :]], axis=-3)
    return jnp.concatenate([by_rows[..., :-1, :], by_rows[..., 1:, :]], axis=-1)


def add_patches(patches):
    by_rows = patches[..., :-1, 16:, :, :] + patches[..., 1:, :16, :, :]
    joined = by_rows[..., :-1, 16:] + by_rows[..., 1:, :16]
    shape = joined.shape
    return joined.reshape(shape[:-4] + (shape[-4] * 16, shape[-2] * 16))


def taper_weights():
    steps = jnp.arange(32, dtype=jnp.float32)
    single = jnp.sin(math.pi * (steps + 0.5) / 32.0) ** 2
    return single[:, None, None] * single


def smooth_response(spectral_amplitude):
    smoothed = jnp.zeros_like(spectral_amplitude)
    for shift_a in (-1, 0, 1):
        for shift_b in (-1, 0, 1):
            smoothed = smoothed + jnp.roll(spectral_amplitude, (shift_a, shift_b), axis=(-3, -1))
    response = jnp.sqrt(smoothed / 9.0)
    largest = jnp.max(response, axis=(-3, -1), keepdims=True)
    return response / (largest + 1e-06)


def mix_along(pattern, table, values):
    return jnp.einsum(pattern, table, values, precision=lax.Precision.HIGHEST)


def transform(values_real, values_imag, cos_table, sin_table):
    first = "ua,...arb->...urb"
    second_image = "dk,...cmk->...cmd"
    step_real = mix_along(first, cos_table, values_real) - mix_along(first, sin_table, values_imag)
    step_imag = mix_along(first, cos_table, values_imag) + mix_along(first, sin_table, values_real)
    out_real = mix_along(second_image, cos_table, step_real) - mix_along(
        second_image, sin_table, step_imag
    )
    out_imag = mix_along(second_image, cos_table, step_imag) + mix_along(
        second_image, sin_table, step_real
    )
    return (out_real, out_imag)


def goldstein(field_real, field_imag):
    counter = jnp.arange(32, dtype=jnp.int32)
    product = counter[:, None] * counter[None, :] % 32
    angle = product.astype(jnp.float32) * (2.0 * math.pi / 32.0)
    cos_table = jnp.cos(angle)
    sin_table = -jnp.sin(angle)
    spec_real, spec_imag = transform(
        cut_patches(field_real), cut_patches(field_imag), cos_table, sin_table
    )
    weights = smooth_response(jnp.sqrt(spec_real * spec_real + spec_imag * spec_imag))
    back_real, returned_imaginary = transform(
        spec_real * weights, spec_imag * weights, cos_table, -sin_table
    )
    taper_window = taper_weights() / 1024.0
    return (add_patches(back_real * taper_window), add_patches(returned_imaginary * taper_window))


def window_sum(values, lines, columns):
    total = jnp.zeros(values.shape[:-2] + (lines, columns), values.dtype)
    for shift_a in range(5):
        for shift_b in range(5):
            total = total + values[..., shift_a : shift_a + lines, shift_b : shift_b + columns]
    return total


def coherence_of(fields):
    lines = fields.shape[-2] - 32
    columns = fields.shape[-1] - 32
    inner = fields[:, 14 : 18 + lines, 14 : 18 + columns]
    real_total_sum = window_sum(inner[0:3], lines, columns)
    sum_imag = window_sum(inner[3:6], lines, columns)
    far_sum = window_sum(inner[6:9], lines, columns)
    own_sum = window_sum(inner[9:10], lines, columns)
    return jnp.sqrt(real_total_sum * real_total_sum + sum_imag * sum_imag) / jnp.sqrt(
        own_sum * far_sum
    )


def neighbour(tile_block, steps):
    return passed_along(tile_block, "tm", steps)


def fetch(tile_block, partner_ids, position):
    arrived = []
    for offset in (1, 2, 3, -1, -2, -3):
        arrived.append((offset, neighbour(tile_block, -offset)))
    collected = []
    for slot_index in range(3):
        chosen = jnp.zeros_like(tile_block)
        for offset, shifted in arrived:
            chosen = jnp.where(partner_ids[slot_index] - position == offset, shifted, chosen)
        collected.append(chosen)
    return jnp.stack(collected, axis=0)


def tile_fields(tile_block, pair_rows, position):
    return pair_fields(tile_block, fetch(tile_block, pair_rows[0], position))


def per_device(slc, pairs):
    own_tile = slc[0]
    position = lax.axis_index("tm")
    widened = extended(own_tile, (("az", 1),), 64)
    widened = extended(widened, (("rg", 2),), 256)
    fields = tile_fields(widened, pairs, position)
    filt_real, filt_imag = goldstein(fields[0:3], fields[3:6])
    filtered = jnp.stack([filt_real, filt_imag], axis=1)[None]
    coherence = coherence_of(fields)[None]
    return (filtered, coherence)


def solution(mesh):
    placed = (P("tm", None, "az", "rg"), P("tm", None))
    return jax.shard_map(
        per_device,
        mesh=mesh,
        in_specs=placed,
        out_specs=(P("tm", None, None, "az", "rg"), P("tm", None, "az", "rg")),
        check_vma=False,
    )
```

profile of v0, /device:TPU:99, one launch (start us, length us, event | category | flops | bytes accessed | tf_op | source)
XLA Modules:
  0.0 178.7 jit_solution(7113926745857873453)
XLA Ops:
  0.6 3.2 %collective-permute-start = (bf16[2,64,512]{2,1,0:T(8,128)(2,1)}, bf16[2,64,512]{2,1,0:T(8,128)(2,1)S(1)}, u32[]{:S(2)}, u32[]{:S(2)}) collective-permute-start(bf16[2,64,512]{2,1,0:T(8,128)(2,1)} %bitcast.85), channel_id=1, source_target_pairs={{0,8},{1,9},{2,10},{3,11},{4,12},{5,13},{6,14},{7,15},{16,24},{17,... | collective-permute-start | bytes 393224 | tf_op jit(solution)/shard_map/ppermute | solution.py:22
  3.9 1.3 collective-permute-start.1
  5.2 1.2 collective-permute-done
  6.3 3.5 %collective-permute-done.1 = bf16[2,64,512]{2,1,0:T(8,128)(2,1)S(1)} collective-permute-done((bf16[2,64,512]{2,1,0:T(8,128)(2,1)}, bf16[2,64,512]{2,1,0:T(8,128)(2,1)S(1)}, u32[]{:S(2)}, u32[]{:S(2)}) %collective-permute-start.1) | collective-permute-done | bytes 131104 | tf_op jit(solution)/shard_map/ppermute | solution.py:23
  9.8 0.9 pad_maximum_fusion.4
  10.8 5.1 %collective-permute-start.2 = (bf16[2,192,256]{2,1,0:T(8,128)(2,1)S(1)}, bf16[2,192,256]{2,1,0:T(8,128)(2,1)S(1)}, u32[]{:S(2)}, u32[]{:S(2)}) collective-permute-start(bf16[2,192,256]{2,1,0:T(8,128)(2,1)S(1)} %get-tuple-element.15), channel_id=1, source_target_pairs={{0,1},{1,2},{2,3},{3,4},{4,5},{5,6},{6,7},{8,9},{9,10},{10,11},{11... | collective-permute-start | bytes 589832 | tf_op jit(solution)/shard_map/ppermute | solution.py:22
  15.9 1.9 %collective-permute-start.3 = (bf16[2,192,256]{2,1,0:T(8,128)(2,1)S(1)}, bf16[2,192,256]{2,1,0:T(8,128)(2,1)S(1)}, u32[]{:S(2)}, u32[]{:S(2)}) collective-permute-start(bf16[2,192,256]{2,1,0:T(8,128)(2,1)S(1)} %get-tuple-element.16), channel_id=1, source_target_pairs={{1,0},{2,1},{3,2},{4,3},{5,4},{6,5},{7,6},{9,8},{10,9},{11,10},{12... | collective-permute-start | bytes 589832 | tf_op jit(solution)/shard_map/ppermute | solution.py:23
  17.8 0.7 collective-permute-done.2
  18.5 4.4 %collective-permute-done.3 = bf16[2,192,256]{2,1,0:T(8,128)(2,1)S(1)} collective-permute-done((bf16[2,192,256]{2,1,0:T(8,128)(2,1)S(1)}, bf16[2,192,256]{2,1,0:T(8,128)(2,1)S(1)}, u32[]{:S(2)}, u32[]{:S(2)}) %collective-permute-start.3) | collective-permute-done | bytes 196640 | tf_op jit(solution)/shard_map/ppermute | solution.py:23
  22.9 1.0 pad_maximum_fusion.3
  23.9 7.1 %collective-permute-start.4 = (bf16[2,192,1024]{2,1,0:T(8,128)(2,1)S(1)}, bf16[2,192,1024]{2,1,0:T(8,128)(2,1)S(1)}, u32[]{:S(2)}, u32[]{:S(2)}) collective-permute-start(bf16[2,192,1024]{2,1,0:T(8,128)(2,1)S(1)} %pad_maximum_fusion.3), channel_id=1, source_target_pairs={{0,48},{16,64},{32,80},{48,96},{64,112},{80,128},{96,144},{112,160... | collective-permute-start | bytes 2359304 | tf_op jit(solution)/shard_map/ppermute | solution.py:12
  31.0 0.6 fusion.174
  33.7 2.6 %collective-permute-start.5 = (bf16[2,192,1024]{2,1,0:T(8,128)(2,1)S(1)}, bf16[2,192,1024]{2,1,0:T(8,128)(2,1)}, u32[]{:S(2)}, u32[]{:S(2)}) collective-permute-start(bf16[2,192,1024]{2,1,0:T(8,128)(2,1)S(1)} %pad_maximum_fusion.3), channel_id=1, source_target_pairs={{0,32},{16,48},{32,64},{48,80},{64,96},{80,112},{96,128},{112,144}... | collective-permute-start | bytes 2359304 | tf_op jit(solution)/shard_map/ppermute | solution.py:12
  36.4 2.7 %collective-permute-start.6 = (bf16[2,192,1024]{2,1,0:T(8,128)(2,1)S(1)}, bf16[2,192,1024]{2,1,0:T(8,128)(2,1)}, u32[]{:S(2)}, u32[]{:S(2)}) collective-permute-start(bf16[2,192,1024]{2,1,0:T(8,128)(2,1)S(1)} %pad_maximum_fusion.3), channel_id=1, source_target_pairs={{0,16},{16,32},{32,48},{48,64},{64,80},{80,96},{96,112},{112,128},... | collective-permute-start | bytes 2359304 | tf_op jit(solution)/shard_map/ppermute | solution.py:12
  39.1 5.4 %collective-permute-start.7 = (bf16[2,192,1024]{2,1,0:T(8,128)(2,1)S(1)}, bf16[2,192,1024]{2,1,0:T(8,128)(2,1)}, u32[]{:S(2)}, u32[]{:S(2)}) collective-permute-start(bf16[2,192,1024]{2,1,0:T(8,128)(2,1)S(1)} %pad_maximum_fusion.3), channel_id=1, source_target_pairs={{48,0},{64,16},{80,32},{96,48},{112,64},{128,80},{144,96},{160,112... | collective-permute-start | bytes 2359304 | tf_op jit(solution)/shard_map/ppermute | solution.py:12
  44.5 1.9 %collective-permute-start.8 = (bf16[2,192,1024]{2,1,0:T(8,128)(2,1)S(1)}, bf16[2,192,1024]{2,1,0:T(8,128)(2,1)}, u32[]{:S(2)}, u32[]{:S(2)}) collective-permute-start(bf16[2,192,1024]{2,1,0:T(8,128)(2,1)S(1)} %pad_maximum_fusion.3), channel_id=1, source_target_pairs={{32,0},{48,16},{64,32},{80,48},{96,64},{112,80},{128,96},{144,112}... | collective-permute-start | bytes 2359304 | tf_op jit(solution)/shard_map/ppermute | solution.py:12
  46.4 34.0 %collective-permute-done.4 = bf16[2,192,1024]{2,1,0:T(8,128)(2,1)S(1)} collective-permute-done((bf16[2,192,1024]{2,1,0:T(8,128)(2,1)S(1)}, bf16[2,192,1024]{2,1,0:T(8,128)(2,1)S(1)}, u32[]{:S(2)}, u32[]{:S(2)}) %collective-permute-start.4) | collective-permute-done | bytes 786464 | tf_op jit(solution)/shard_map/ppermute | solution.py:12
  80.4 1.9 %collective-permute-start.9 = (bf16[2,192,1024]{2,1,0:T(8,128)(2,1)S(1)}, bf16[2,192,1024]{2,1,0:T(8,128)(2,1)}, u32[]{:S(2)}, u32[]{:S(2)}) collective-permute-start(bf16[2,192,1024]{2,1,0:T(8,128)(2,1)S(1)} %pad_maximum_fusion.3), channel_id=1, source_target_pairs={{16,0},{32,16},{48,32},{64,48},{80,64},{96,80},{112,96},{128,112},... | collective-permute-start | bytes 2359304 | tf_op jit(solution)/shard_map/ppermute | solution.py:12
  82.4 0.2 slice_convert_fusion.3
  82.5 4.1 %reshape.128 = f32[48,4,64,16]{3,2,1,0:T(8,128)} reshape(f32[1,192,1024]{2,1,0:T(8,128)S(1)} %get-tuple-element.13) | data formatting | bytes 1572864 | tf_op jit(solution)/shard_map/mul | solution.py:40
  86.6 4.1 %reshape.130 = f32[48,4,64,16]{3,2,1,0:T(8,128)} reshape(f32[1,192,1024]{2,1,0:T(8,128)S(1)} %get-tuple-element.14) | data formatting | bytes 1572864 | tf_op jit(solution)/shard_map/mul | solution.py:40
  90.7 0.1 multiply_add_fusion
  90.9 4.1 %add.509 = f32[48,4,64,16]{3,2,1,0:T(8,128)} reshape(f32[1,192,1024]{2,1,0:T(8,128)S(1)} %multiply_add_fusion) | data formatting | bytes 1572864 | tf_op jit(solution)/shard_map/add | solution.py:43
  95.0 3.3 %reduce_sum.38 = f32[48,64]{1,0:T(8,128)S(1)} reduce(f32[48,4,64,16]{3,2,1,0:T(8,128)} %add.509, f32[]{:T(128)} %constant.51.clone.1), dimensions={1,3}, to_apply=%region_3.4 | reduce | flops 193536 | bytes 798724 | tf_op jit(solution)/shard_map/reduce_sum | solution.py:32
  98.4 1.5 collective-permute-done.6
  99.9 16.9 %collective-permute-done.9 = bf16[2,192,1024]{2,1,0:T(8,128)(2,1)} collective-permute-done((bf16[2,192,1024]{2,1,0:T(8,128)(2,1)S(1)}, bf16[2,192,1024]{2,1,0:T(8,128)(2,1)}, u32[]{:S(2)}, u32[]{:S(2)}) %collective-permute-start.9) | collective-permute-done | bytes 786464 | tf_op jit(solution)/shard_map/ppermute | solution.py:12
  116.9 1.3 select_bitcast_fusion.1
  118.2 2.4 %select_bitcast_fusion.2 = (bf16[1,2,192,1024]{3,2,1,0:T(8,128)(2,1)S(1)}, bf16[1,2,192,1024]{3,2,1,0:T(8,128)(2,1)S(1)}) fusion(bf16[2,192,1024]{2,1,0:T(8,128)(2,1)S(1)} %collective-permute-done.4, bf16[2,192,1024]{2,1,0:T(8,128)(2,1)} %collective-permute-done.5, bf16[2,192,1024]{2,1,0:T(8,128)(2,1)} %collective-permute-done.6, ...), kind=kLoop, calls=%fused_computation.34 | loop fusion | flops 4718592 | bytes 6291468 | tf_op jit(solution)/shard_map/stack | solution.py:149
  120.6 0.3 pad_maximum_fusion
  120.9 1.9 %slice_convert_fusion.1 = (f32[3,1,192,1024]{3,2,1,0:T(8,128)}, f32[3,1,192,1024]{3,2,1,0:T(8,128)S(1)}) fusion(bf16[3,2,192,1024]{3,2,1,0:T(8,128)(2,1)S(1)} %pad_maximum_fusion), kind=kLoop, calls=%fused_computation.5 | loop fusion | flops 1179648 | bytes 7077888 | tf_op jit(solution)/shard_map/convert_element_type | solution.py:38
  122.8 11.5 %reshape.129 = f32[3,48,4,64,16]{4,3,2,1,0:T(8,128)} reshape(f32[3,1,192,1024]{3,2,1,0:T(8,128)} %get-tuple-element.11) | data formatting | bytes 4718592 | tf_op jit(solution)/shard_map/convert_element_type | solution.py:38
  134.3 10.2 %reshape.131 = f32[3,48,4,64,16]{4,3,2,1,0:T(8,128)} reshape(f32[3,1,192,1024]{3,2,1,0:T(8,128)S(1)} %get-tuple-element.12) | data formatting | bytes 4718592 | tf_op jit(solution)/shard_map/convert_element_type | solution.py:39
  144.5 18.8 %add_reduce_fusion.1 = (f32[3,48,64]{2,1,0:T(8,128)S(1)}, f32[3,48,64]{2,1,0:T(8,128)S(1)}, f32[3,48,64]{2,1,0:T(8,128)S(1)}) fusion(f32[3,48,4,64,16]{4,3,2,1,0:T(8,128)} %reshape.131, f32[3,48,4,64,16]{4,3,2,1,0:T(8,128)} %reshape.129, f32[48,4,64,16]{3,2,1,0:T(8,128)} %reshape.130, f32[48,4,64,16]{3,2,1,0:T(8,128)} %reshape.128), kind=kLoop, calls=%fused_computation.2 | loop fusion | flops 7050240 | bytes 6402048 | tf_op jit(solution)/shard_map/reduce_sum | solution.py:32
  163.3 0.2 div.57
  163.6 0.1 copy.52
  163.7 0.1 copy.53
  163.9 0.5 fusion.37
  164.4 0.2 div.55
  164.7 0.1 copy.50
  164.8 0.1 copy.51
  165.0 0.5 fusion.35
  165.5 0.5 fusion.4
  166.0 0.5 fusion.5
  166.5 0.6 fusion.68
  167.1 0.6 fusion.65
  167.8 0.6 convolution_subtract_fusion.2
  168.4 0.7 add_sqrt_fusion
  169.2 0.2 fusion.21
  169.3 0.2 fusion.20
  169.5 0.2 fusion.11
  169.7 0.2 fusion.10
  169.9 0.1 fusion.170
  170.0 0.1 fusion.171
  170.2 0.7 fusion.165
  170.9 0.7 fusion.32
  171.6 0.7 fusion.28
  172.4 0.7 fusion.3
  173.1 0.6 fusion.62
  173.7 0.7 fusion.2
  174.5 0.6 fusion.59
  175.1 0.6 fusion.1
  176.0 0.6 fusion
  176.9 0.6 copy.34
  177.5 1.2 fusion.43
  (28 shorter events, 1.1 us)
Async XLA Ops:
  0.6 30.3 %copy-start = (s32[1,3]{1,0:T(1,128)S(1)}, s32[1,3]{1,0:T(1,128)}, u32[]{:S(2)}) copy-start(s32[1,3]{1,0:T(1,128)} %param.3) | copy-start | bytes 40
  0.6 5.7 %collective-permute-start = (bf16[2,64,512]{2,1,0:T(8,128)(2,1)}, bf16[2,64,512]{2,1,0:T(8,128)(2,1)S(1)}, u32[]{:S(2)}, u32[]{:S(2)}) collective-permute-start(bf16[2,64,512]{2,1,0:T(8,128)(2,1)} %bitcast.85), channel_id=1, source_target_pairs={{0,8},{1,9},{2,10},{3,11},{4,12},{5,13},{6,14},{7,15},{16,24},{17,... | collective-permute-start | bytes 393224 | tf_op jit(solution)/shard_map/ppermute | solution.py:22
  3.9 5.9 %collective-permute-start.1 = (bf16[2,64,512]{2,1,0:T(8,128)(2,1)}, bf16[2,64,512]{2,1,0:T(8,128)(2,1)S(1)}, u32[]{:S(2)}, u32[]{:S(2)}) collective-permute-start(bf16[2,64,512]{2,1,0:T(8,128)(2,1)} %bitcast.86), channel_id=1, source_target_pairs={{8,0},{9,1},{10,2},{11,3},{12,4},{13,5},{14,6},{15,7},{24,16},{25,... | collective-permute-start | bytes 393224 | tf_op jit(solution)/shard_map/ppermute | solution.py:23
  10.8 7.7 %collective-permute-start.2 = (bf16[2,192,256]{2,1,0:T(8,128)(2,1)S(1)}, bf16[2,192,256]{2,1,0:T(8,128)(2,1)S(1)}, u32[]{:S(2)}, u32[]{:S(2)}) collective-permute-start(bf16[2,192,256]{2,1,0:T(8,128)(2,1)S(1)} %get-tuple-element.15), channel_id=1, source_target_pairs={{0,1},{1,2},{2,3},{3,4},{4,5},{5,6},{6,7},{8,9},{9,10},{10,11},{11... | collective-permute-start | bytes 589832 | tf_op jit(solution)/shard_map/ppermute | solution.py:22
  15.9 7.0 %collective-permute-start.3 = (bf16[2,192,256]{2,1,0:T(8,128)(2,1)S(1)}, bf16[2,192,256]{2,1,0:T(8,128)(2,1)S(1)}, u32[]{:S(2)}, u32[]{:S(2)}) collective-permute-start(bf16[2,192,256]{2,1,0:T(8,128)(2,1)S(1)} %get-tuple-element.16), channel_id=1, source_target_pairs={{1,0},{2,1},{3,2},{4,3},{5,4},{6,5},{7,6},{9,8},{10,9},{11,10},{12... | collective-permute-start | bytes 589832 | tf_op jit(solution)/shard_map/ppermute | solution.py:23
  23.9 56.6 %collective-permute-start.4 = (bf16[2,192,1024]{2,1,0:T(8,128)(2,1)S(1)}, bf16[2,192,1024]{2,1,0:T(8,128)(2,1)S(1)}, u32[]{:S(2)}, u32[]{:S(2)}) collective-permute-start(bf16[2,192,1024]{2,1,0:T(8,128)(2,1)S(1)} %pad_maximum_fusion.3), channel_id=1, source_target_pairs={{0,48},{16,64},{32,80},{48,96},{64,112},{80,128},{96,144},{112,160... | collective-permute-start | bytes 2359304 | tf_op jit(solution)/shard_map/ppermute | solution.py:12
  33.7 64.7 %collective-permute-start.5 = (bf16[2,192,1024]{2,1,0:T(8,128)(2,1)S(1)}, bf16[2,192,1024]{2,1,0:T(8,128)(2,1)}, u32[]{:S(2)}, u32[]{:S(2)}) collective-permute-start(bf16[2,192,1024]{2,1,0:T(8,128)(2,1)S(1)} %pad_maximum_fusion.3), channel_id=1, source_target_pairs={{0,32},{16,48},{32,64},{48,80},{64,96},{80,112},{96,128},{112,144}... | collective-permute-start | bytes 2359304 | tf_op jit(solution)/shard_map/ppermute | solution.py:12
  36.4 63.5 %collective-permute-start.6 = (bf16[2,192,1024]{2,1,0:T(8,128)(2,1)S(1)}, bf16[2,192,1024]{2,1,0:T(8,128)(2,1)}, u32[]{:S(2)}, u32[]{:S(2)}) collective-permute-start(bf16[2,192,1024]{2,1,0:T(8,128)(2,1)S(1)} %pad_maximum_fusion.3), channel_id=1, source_target_pairs={{0,16},{16,32},{32,48},{48,64},{64,80},{80,96},{96,112},{112,128},... | collective-permute-start | bytes 2359304 | tf_op jit(solution)/shard_map/ppermute | solution.py:12
  39.1 60.8 %collective-permute-start.7 = (bf16[2,192,1024]{2,1,0:T(8,128)(2,1)S(1)}, bf16[2,192,1024]{2,1,0:T(8,128)(2,1)}, u32[]{:S(2)}, u32[]{:S(2)}) collective-permute-start(bf16[2,192,1024]{2,1,0:T(8,128)(2,1)S(1)} %pad_maximum_fusion.3), channel_id=1, source_target_pairs={{48,0},{64,16},{80,32},{96,48},{112,64},{128,80},{144,96},{160,112... | collective-permute-start | bytes 2359304 | tf_op jit(solution)/shard_map/ppermute | solution.py:12
  44.5 55.4 %collective-permute-start.8 = (bf16[2,192,1024]{2,1,0:T(8,128)(2,1)S(1)}, bf16[2,192,1024]{2,1,0:T(8,128)(2,1)}, u32[]{:S(2)}, u32[]{:S(2)}) collective-permute-start(bf16[2,192,1024]{2,1,0:T(8,128)(2,1)S(1)} %pad_maximum_fusion.3), channel_id=1, source_target_pairs={{32,0},{48,16},{64,32},{80,48},{96,64},{112,80},{128,96},{144,112}... | collective-permute-start | bytes 2359304 | tf_op jit(solution)/shard_map/ppermute | solution.py:12
  80.4 36.4 %collective-permute-start.9 = (bf16[2,192,1024]{2,1,0:T(8,128)(2,1)S(1)}, bf16[2,192,1024]{2,1,0:T(8,128)(2,1)}, u32[]{:S(2)}, u32[]{:S(2)}) collective-permute-start(bf16[2,192,1024]{2,1,0:T(8,128)(2,1)S(1)} %pad_maximum_fusion.3), channel_id=1, source_target_pairs={{16,0},{32,16},{48,32},{64,48},{80,64},{96,80},{112,96},{128,112},... | collective-permute-start | bytes 2359304 | tf_op jit(solution)/shard_map/ppermute | solution.py:12
where the time goes:
time: 179 us
  waiting for transfers between devices  62.1 us (35%)
  local copies, waits for them, and re-layouts  36.9 us (21%)
  other arithmetic  33.5 us (19%)
  starting transfers between devices  33.2 us (19%)
  matrix products  9.91 us (6%)
  between operations  3.06 us (2%)
    ppermute x6, waiting for transfers between devices, passed_along(): return lax.ppermute(value, axis, pairs)  52.4 us
    reduce_sum x2, other arithmetic, multilook(): return jnp.sum(shaped, axis=(-3, -1)) / 64.0  22.1 us
    ppermute x6, starting transfers between devices, passed_along(): return lax.ppermute(value, axis, pairs)  21.7 us
    convert_element_type x1, local copies, waits for them, and re-layouts, pair_fields(): far_real = remote_tiles[:, 0].astype(jnp.float32)  11.5 us
    convert_element_type x1, local copies, waits for them, and re-layouts, pair_fields(): far_imag = remote_tiles[:, 1].astype(jnp.float32)  10.2 us
    dot_general x16, matrix products, mix_along(): return jnp.einsum(pattern, table, values, precision=lax.Precision.HIGHEST)  9.91 us
    ppermute x2, starting transfers between devices, extended(): before = lax.ppermute(last, axis, up)  8.32 us
    mul x2, local copies, waits for them, and re-layouts, pair_fields(): cross_real = multilook(own_real * far_real + own_imag * far_imag)  8.21 us
  transfers between devices with their start and end apart: 10, of which 7 were waited for; matrix products, arithmetic and copies ran while one was open for 9% of the time, Pallas kernels for 0%

commit v1 on v0

v1 whole, which is shorter than its diff:
```python
import math

import jax
import jax.numpy as jnp
import ml_dtypes
import numpy as np
from jax import lax
from jax.experimental import pallas as pl
from jax.experimental.pallas import tpu as pltpu
from jax.sharding import Mesh, PartitionSpec as P

F32 = jnp.float32
BF16 = jnp.bfloat16
EVERY = ("tm", "az", "rg")


def split_table(table):
    high = table.astype(ml_dtypes.bfloat16)
    low = (table - high.astype(np.float64)).astype(ml_dtypes.bfloat16)
    return high, low


def column_tables():
    forward = np.zeros((256, 384))
    back = np.zeros((256, 256))
    steps = np.arange(32)
    taper = np.sin(math.pi * (steps + 0.5) / 32.0) ** 2

    def row_of(field, column):
        if column < 16:
            return 128 + field * 32 + 16 + column
        if column < 48:
            return field * 32 + column - 16
        return 128 + field * 32 + column - 48

    for patch in range(3):
        for j in range(32):
            angle = 2.0 * math.pi * (j * steps % 32) / 32.0
            real, imag = row_of(0, patch * 16 + j), row_of(1, patch * 16 + j)
            at = patch * 32 + steps
            forward[real, at] = np.cos(angle)
            forward[imag, at] = np.sin(angle)
            forward[real, 128 + at] = -np.sin(angle)
            forward[imag, 128 + at] = np.cos(angle)
            column = patch * 16 + j - 16
            if 0 <= column < 32:
                scale = taper[j] / 32.0
                back[at, column] = np.cos(angle) * scale
                back[128 + at, column] = -np.sin(angle) * scale
                back[at, 128 + column] = np.sin(angle) * scale
                back[128 + at, 128 + column] = np.cos(angle) * scale
    for field in range(4):
        for cell in range(32):
            for column in range(cell + 14, cell + 19):
                forward[row_of(field, column), 256 + field * 32 + cell] = 1.0
    return forward, back


def line_tables():
    forward = np.zeros((2, 128, 64))
    window = np.zeros((2, 16, 32))
    back = np.zeros((32, 128))
    steps = np.arange(32)
    taper = np.sin(math.pi * (steps + 0.5) / 32.0) ** 2
    for side in range(2):
        places = {}
        for line in range(16):
            places[16 + line] = line
            places[(32 if side == 0 else 0) + line] = 16 + line
        for patch in range(2):
            for j in range(32):
                row = places.get(patch * 16 + j)
                if row is None:
                    continue
                angle = 2.0 * math.pi * (j * steps % 32) / 32.0
                at = patch * 32 + steps
                forward[side, at, row] = np.cos(angle)
                forward[side, at, 32 + row] = np.sin(angle)
                forward[side, 64 + at, row] = -np.sin(angle)
                forward[side, 64 + at, 32 + row] = np.cos(angle)
        for cell in range(16):
            for line in range(cell + 14, cell + 19):
                if line in places:
                    window[side, cell, places[line]] = 1.0
    for patch in range(2):
        for j in range(32):
            cell = patch * 16 + j - 16
            if 0 <= cell < 16:
                angle = 2.0 * math.pi * (j * steps % 32) / 32.0
                scale = taper[j] / 32.0
                at = patch * 32 + steps
                back[cell, at] = np.cos(angle) * scale
                back[cell, 64 + at] = -np.sin(angle) * scale
                back[16 + cell, at] = np.sin(angle) * scale
                back[16 + cell, 64 + at] = np.cos(angle) * scale
    return forward, window, back


def tables():
    column_forward, column_back = column_tables()
    line_forward, window, line_back = line_tables()
    cf_high, cf_low = split_table(column_forward)
    cb_high, cb_low = split_table(column_back)
    lf_high, lf_low = split_table(line_forward)
    lb_high, lb_low = split_table(line_back)
    return (
        cf_high,
        cf_low,
        np.concatenate([lf_high, lf_high, lf_low], axis=2),
        np.concatenate([window, window], axis=2).astype(ml_dtypes.bfloat16),
        np.concatenate([lb_high, lb_high, lb_low], axis=1),
        cb_high,
        cb_low,
    )


def look_table():
    table = np.zeros((512, 128))
    columns = np.arange(512)
    table[columns, columns // 16] = 1.0 / 64.0
    return table.astype(ml_dtypes.bfloat16)


def halves(values):
    high = values.astype(BF16)
    low = (values - high.astype(F32)).astype(BF16)
    return high, low


def dot(left, right):
    return jnp.dot(left, right, preferred_element_type=F32)


def cross_kernel(own, other, up, down, far, look, own_out, other_out, wide, sums):
    tiles = (own, other, up, down, far)
    for index, tile in enumerate(tiles):
        for part in range(2):
            for chunk in range(4):
                wide[index * 2 + part, chunk] = tile[part, :, chunk * 128 : chunk * 128 + 128].astype(F32)
    couples = ((0, 1), (0, 2), (0, 3), (1, 2), (1, 3), (1, 4))
    for chunk in range(4):
        at = slice(chunk * 128, chunk * 128 + 128)
        totals = [None] * 17
        for line in range(4):
            real = [wide[2 * i, chunk, pl.ds(line, 16, stride=4), :] for i in range(5)]
            imag = [wide[2 * i + 1, chunk, pl.ds(line, 16, stride=4), :] for i in range(5)]
            terms = []
            for u, v in couples:
                terms.append(real[u] * real[v] + imag[u] * imag[v])
            for u, v in couples:
                terms.append(imag[u] * real[v] - real[u] * imag[v])
            for u in range(5):
                terms.append(real[u] * real[u] + imag[u] * imag[u])
            totals = [t if s is None else s + t for s, t in zip(totals, terms)]
        for index, total in enumerate(totals):
            sums[index * 16 : index * 16 + 16, at] = total
    high, low = halves(sums[...])
    table = look[...]
    looked = dot(high, table) + dot(low, table)
    fields = [looked[i * 16 : i * 16 + 16] for i in range(17)]
    far_power = [pltpu.roll(fields[12 + i], 64, 1) for i in range(5)]
    own_power = [pltpu.roll(fields[12 + i], 96, 1) for i in range(2)]
    for index, (u, v) in enumerate(couples):
        row = fields[index] + pltpu.roll(fields[6 + index], 32, 1) + far_power[v] + own_power[u]
        if u == 0:
            own_out[index] = row
        else:
            other_out[index - 3] = row


def choose_kernel(meta, own, swapped, own_beside, swapped_beside, out):
    position = meta[0]
    odd = position % 2
    for slot in range(3):
        offset = meta[4 + slot] - position
        flipped = jnp.where(odd == 1, -offset, offset)
        near = jnp.where(flipped == 1, 0, jnp.where(offset == 2, 1, 2))
        third = jnp.where(odd == 1, 4, 3)
        first = jnp.where(odd == 1, 3, 4)
        away = jnp.where(flipped == 3, third, jnp.where(flipped == -1, first, 5)) - 3
        is_near = (flipped == 1) | (offset == 2) | (offset == -2)
        near = jnp.where(is_near, near, 0)
        away = jnp.where(is_near, 0, away)
        out[slot, 0:16] = jnp.where(is_near, own[near], swapped[away])
        out[slot, 16:32] = jnp.where(is_near, own_beside[near], swapped_beside[away])


def finish_kernel(
    meta, fields, core_halo, chip_halo, cf_high, cf_low, lf, window, lb, cb_high, cb_low, filtered, coherence
):
    side = meta[1]
    core = meta[2]
    lane = lax.broadcasted_iota(jnp.int32, (1, 128), 1)
    place = lane % 32
    from_core = (place >= 16) == (core == 1)
    halo = jnp.where(from_core, core_halo[...].reshape(96, 128), chip_halo[...].reshape(96, 128))
    values = jnp.concatenate([fields[...].reshape(96, 128), halo], axis=1)
    high, low = halves(values)
    table = cf_high[...]
    mixed = dot(high, table) + dot(low, table) + dot(high, cf_low[...])
    rows = [mixed[32 * s : 32 * s + 32] for s in range(3)]
    real = jnp.concatenate([r[:, 0:128] for r in rows], axis=1)
    imag = jnp.concatenate([r[:, 128:256] for r in rows], axis=1)
    sums = jnp.concatenate([r[:, 256:384] for r in rows], axis=1)
    high, low = halves(jnp.concatenate([real, imag], axis=0))
    spectrum = dot(lf[side], jnp.concatenate([high, low, high], axis=0))
    spec_real, spec_imag = spectrum[0:64], spectrum[64:128]
    power = jnp.sqrt(spec_real * spec_real + spec_imag * spec_imag)

    def turned(block, by):
        away = pltpu.roll(block, by % 128, 1)
        wrapped = pltpu.roll(block, (by - 32) % 128, 1)
        if by > 0:
            return jnp.where(place < by, wrapped, away)
        wrapped = pltpu.roll(block, (by + 32) % 128, 1)
        return jnp.where(place >= 32 + by, wrapped, away)

    smoothed = []
    for patch in range(2):
        for slot in range(3):
            block = power[32 * patch : 32 * patch + 32, 128 * slot : 128 * slot + 128]
            block = block + pltpu.roll(block, 1, 0) + pltpu.roll(block, 31, 0)
            block = block + turned(block, 1) + turned(block, -1)
            smoothed.append(block / 9.0)
    largest = jnp.concatenate([jnp.max(b, axis=0, keepdims=True) for b in smoothed] + [jnp.zeros((2, 128), F32)], axis=0)
    for by in (1, 2, 4, 8, 16):
        largest = jnp.maximum(largest, turned(largest, by))
    scale = 1.0 / (jnp.sqrt(largest) + 1e-06)
    weights = [jnp.sqrt(b) * scale[i : i + 1] for i, b in enumerate(smoothed)]
    weights = jnp.concatenate(
        [jnp.concatenate(weights[0:3], axis=1), jnp.concatenate(weights[3:6], axis=1)], axis=0
    )
    high, low = halves(jnp.concatenate([spec_real * weights, spec_imag * weights], axis=0))
    lines = dot(lb[...], jnp.concatenate([high, low, high], axis=0))
    stacked = jnp.concatenate(
        [
            jnp.concatenate([lines[0:16, 128 * s : 128 * s + 128], lines[16:32, 128 * s : 128 * s + 128]], axis=1)
            for s in range(3)
        ],
        axis=0,
    )
    high, low = halves(stacked)
    table = cb_high[...]
    result = dot(high, table) + dot(low, table) + dot(high, cb_low[...])
    for slot in range(3):
        filtered[slot, 0] = result[16 * slot : 16 * slot + 16, 0:32]
        filtered[slot, 1] = result[16 * slot : 16 * slot + 16, 128:160]

    high, low = halves(sums)
    totals = dot(window[side], jnp.concatenate([high, low], axis=0))
    for slot in range(3):
        total = totals[:, 128 * slot : 128 * slot + 128]
        square = total * total
        square = square + pltpu.roll(square, 96, 1)
        product = total * pltpu.roll(total, 96, 1)
        product = pltpu.roll(product, 64, 1)
        coherence[slot] = (jnp.sqrt(square) / jnp.sqrt(product))[:, 0:32]


VMEM = pl.BlockSpec(memory_space=pltpu.VMEM)
SMEM = pl.BlockSpec(memory_space=pltpu.SMEM)


def moved(value, where):
    pairs = []
    for z in range(8):
        for yh in range(2):
            for yl in range(2):
                for r in range(8):
                    target = where(z, yh, yl, r)
                    if target is None:
                        continue
                    tz, th, tl, tr = target
                    if not (0 <= tz < 8 and 0 <= tr < 8):
                        continue
                    pairs.append((((z * 2 + yh) * 2 + yl) * 8 + r, ((tz * 2 + th) * 2 + tl) * 8 + tr))
    return lax.ppermute(value, EVERY, pairs)


def per_device(slc, pairs):
    tile = slc[0]
    position = lax.axis_index("tm")
    side = lax.axis_index("az")
    column = lax.axis_index("rg")
    meta = jnp.stack([position, side, column % 2, 0, pairs[0, 0], pairs[0, 1], pairs[0, 2], 0]).astype(jnp.int32)

    def even_pair(z, h, l, r):
        return (z ^ 1, h, l, r)

    def odd_pair(z, h, l, r):
        return (((z + 1) ^ 1) - 1, h, l, r)

    def far_pair(z, h, l, r):
        return (z - 2, h, l, r) if h == 0 else (z + 2, h, l, r)

    swap_even = moved(tile, even_pair)
    swap_odd = moved(tile, odd_pair)
    far = moved(tile, far_pair)
    other = moved(tile, lambda z, h, l, r: (z, 1 - h, l, r))
    odd_z = (position // 2) % 2 == 1
    up = jnp.where(odd_z, swap_odd, swap_even)
    down = jnp.where(odd_z, swap_even, swap_odd)

    record = jax.ShapeDtypeStruct((3, 16, 128), F32)
    own_fields, other_fields = pl.pallas_call(
        cross_kernel,
        out_shape=(record, record),
        in_specs=[VMEM] * 6,
        out_specs=(VMEM, VMEM),
        scratch_shapes=[pltpu.VMEM((10, 4, 64, 128), F32), pltpu.VMEM((272, 512), F32)],
        compiler_params=pltpu.CompilerParams(vmem_limit_bytes=24 * 2**20),
        name="cross",
    )(tile, other, up, down, far, jnp.asarray(look_table()))

    swapped = moved(other_fields, lambda z, h, l, r: (z, 1 - h, l, r))
    own_beside = moved(own_fields, lambda z, h, l, r: (z, h, 1 - l, r))
    swapped_beside = moved(other_fields, lambda z, h, l, r: (z, 1 - h, 1 - l, r))
    fields = pl.pallas_call(
        choose_kernel,
        out_shape=jax.ShapeDtypeStruct((3, 32, 128), F32),
        in_specs=[SMEM] + [VMEM] * 4,
        out_specs=VMEM,
        name="choose",
    )(meta, own_fields, swapped, own_beside, swapped_beside)

    core_halo = moved(fields, lambda z, h, l, r: (z, h, l, r ^ 1))
    chip_halo = moved(fields, lambda z, h, l, r: (z, h, l, ((r + 1) ^ 1) - 1))
    filtered, coherence = pl.pallas_call(
        finish_kernel,
        out_shape=(jax.ShapeDtypeStruct((3, 2, 16, 32), F32), jax.ShapeDtypeStruct((3, 16, 32), F32)),
        in_specs=[SMEM] + [VMEM] * 10,
        out_specs=(VMEM, VMEM),
        compiler_params=pltpu.CompilerParams(vmem_limit_bytes=24 * 2**20),
        name="finish",
    )(meta, fields, core_halo, chip_halo, *[jnp.asarray(t) for t in tables()])
    return (filtered[None], coherence[None])


def solution(mesh):
    placed = (P("tm", None, "az", "rg"), P("tm", None))
    return jax.shard_map(
        per_device,
        mesh=mesh,
        in_specs=placed,
        out_specs=(P("tm", None, None, "az", "rg"), P("tm", None, "az", "rg")),
        check_vma=False,
    )
```

time: 179 us -> 43 us (0.24)
  the two profiles are of different devices: /device:TPU:99 before, /device:TPU:1 now
where the time goes in v1:
time: 43 us; the launch traced here: 42.7 us
  starting transfers between devices  17.9 us (42%)
  waiting for transfers between devices  14.1 us (33%)
  local copies, waits for them, and re-layouts  5.17 us (12%)
  Pallas kernels  4.6 us (11%)
  between operations  0.89 us (2%)
    ppermute x9, starting transfers between devices, moved(): return lax.ppermute(value, EVERY, pairs)  17.9 us
    ppermute x9, waiting for transfers between devices, moved(): return lax.ppermute(value, EVERY, pairs)  14.1 us
    pallas_call x1, Pallas kernels, per_device(): pl.pallas_call(finish_kernel, out_shape=(jax.ShapeDtypeStruct((3, 2, 16,...  2.5 us
    another operation x1, local copies, waits for them, and re-layouts, per_device(): jnp.stack([position, side, column % 2, 0, pairs[0, 0], pairs[0, 1], pairs...  2.5 us
    unnamed x32, local copies, waits for them, and re-layouts  2.06 us
    pallas_call x1, Pallas kernels, per_device(): pl.pallas_call(choose_kernel, out_shape=jax.ShapeDtypeStruct((3, 32, 128)...  1.45 us
  transfers between devices with their start and end apart: 9, of which 3 were waited for; matrix products, arithmetic and copies ran while one was open for 7% of the time, Pallas kernels for 0%

profile of v1, /device:TPU:1, one launch (start us, length us, event | category | flops | bytes accessed | tf_op | source)
XLA Modules:
  0.0 42.7 jit_solution(4254633587811905652)
XLA Ops:
  0.6 0.7 %collective-permute-start.1 = (bf16[2,64,512]{2,1,0:T(8,128)(2,1)}, bf16[2,64,512]{2,1,0:T(8,128)(2,1)S(1)}, u32[]{:S(2)}, u32[]{:S(2)}) collective-permute-start(bf16[2,64,512]{2,1,0:T(8,128)(2,1)} %bitcast.9), channel_id=1, source_target_pairs={{32,64},{33,65},{34,66},{35,67},{36,68},{37,69},{38,70},{39,71},{4... | collective-permute-start | bytes 393224 | tf_op jit(solution)/shard_map/ppermute | solution.py:277
  1.3 5.4 %collective-permute-start.2 = (bf16[2,64,512]{2,1,0:T(8,128)(2,1)}, bf16[2,64,512]{2,1,0:T(8,128)(2,1)S(1)}, u32[]{:S(2)}, u32[]{:S(2)}) collective-permute-start(bf16[2,64,512]{2,1,0:T(8,128)(2,1)} %bitcast.10), channel_id=1, source_target_pairs={{0,32},{1,33},{2,34},{3,35},{4,36},{5,37},{6,38},{7,39},{8,40},{9,... | collective-permute-start | bytes 393224 | tf_op jit(solution)/shard_map/ppermute | solution.py:277
  6.7 2.9 %collective-permute-start = (bf16[2,64,512]{2,1,0:T(8,128)(2,1)}, bf16[2,64,512]{2,1,0:T(8,128)(2,1)S(1)}, u32[]{:S(2)}, u32[]{:S(2)}) collective-permute-start(bf16[2,64,512]{2,1,0:T(8,128)(2,1)} %bitcast.11), channel_id=1, source_target_pairs={{0,16},{1,17},{2,18},{3,19},{4,20},{5,21},{6,22},{7,23},{8,24},{9,... | collective-permute-start | bytes 393224 | tf_op jit(solution)/shard_map/ppermute | solution.py:277
  9.7 1.3 %collective-permute-start.3 = (bf16[2,64,512]{2,1,0:T(8,128)(2,1)}, bf16[2,64,512]{2,1,0:T(8,128)(2,1)S(1)}, u32[]{:S(2)}, u32[]{:S(2)}) collective-permute-start(bf16[2,64,512]{2,1,0:T(8,128)(2,1)} %bitcast.12), channel_id=1, source_target_pairs={{16,80},{17,81},{18,82},{19,83},{20,84},{21,85},{22,86},{23,87},{2... | collective-permute-start | bytes 393224 | tf_op jit(solution)/shard_map/ppermute | solution.py:277
  11.0 0.0 copy-start.6
  11.0 0.0 copy-start.7
  11.0 0.0 collective-permute-done.1
  11.0 0.0 collective-permute-done.2
  11.0 1.2 %collective-permute-done.other = bf16[2,64,512]{2,1,0:T(8,128)(2,1)S(1)} collective-permute-done((bf16[2,64,512]{2,1,0:T(8,128)(2,1)}, bf16[2,64,512]{2,1,0:T(8,128)(2,1)S(1)}, u32[]{:S(2)}, u32[]{:S(2)}) %collective-permute-start) | collective-permute-done | bytes 131104 | tf_op jit(solution)/shard_map/ppermute | solution.py:277
  12.3 10.2 %collective-permute-done.3.far = bf16[2,64,512]{2,1,0:T(8,128)(2,1)S(1)} collective-permute-done((bf16[2,64,512]{2,1,0:T(8,128)(2,1)}, bf16[2,64,512]{2,1,0:T(8,128)(2,1)S(1)}, u32[]{:S(2)}, u32[]{:S(2)}) %collective-permute-start.3) | collective-permute-done | bytes 131104 | tf_op jit(solution)/shard_map/ppermute | solution.py:277
  22.5 0.0 copy-done.6
  22.5 0.0 copy-done.7
  22.5 0.0 copy-start.15
  22.5 0.0 copy-start.2
  22.5 0.0 copy-start.3
  22.6 0.0 copy-start.4
  22.6 0.0 copy-start.5
  22.6 0.0 copy-start.9
  22.6 0.6 %cross.1 = (f32[3,16,128]{2,1,0:T(8,128)S(1)}, f32[3,16,128]{2,1,0:T(8,128)S(1)}) custom-call(bf16[2,64,512]{2,1,0:T(8,128)(2,1)S(1)} %bitcast.13, bf16[2,64,512]{2,1,0:T(8,128)(2,1)S(1)} %collective-permute-done.other, bf16[2,64,512]{2,1,0:T(8,128)(2,1)S(1)} %get-tuple-element.11.up, bf16[2,64,512]{2,1,0:T(8,128)(2,1)S(1)} %get-tuple-element.10.down, ...), custom_call_target="tpu_custom_call" | custom-call | tf_op jit(solution)/shard_map/cross/pallas_call | solution.py:305
  23.2 0.0 copy-start.8
  23.3 0.0 copy-start.1
  23.3 0.1 collective-permute-start.4
  23.4 2.8 %collective-permute-start.6 = (f32[3,16,128]{2,1,0:T(8,128)S(1)}, f32[3,16,128]{2,1,0:T(8,128)S(1)}, u32[]{:S(2)}, u32[]{:S(2)}) collective-permute-start(f32[3,16,128]{2,1,0:T(8,128)S(1)} %get-tuple-element.7), channel_id=1, source_target_pairs={{0,24},{1,25},{2,26},{3,27},{4,28},{5,29},{6,30},{7,31},{8,16},{9,... | collective-permute-start | bytes 73736 | tf_op jit(solution)/shard_map/ppermute | solution.py:277
  26.2 0.0 collective-permute-start.5
  26.2 0.0 copy-done.15
  26.2 0.6 %fusion = (s32[1,1]{1,0:T(1,128)}, s32[1,1]{1,0:T(1,128)}, s32[1,1]{1,0:T(1,128)}) fusion(s32[1,3]{1,0:T(1,128)S(1)} %copy-done.15), kind=kLoop, calls=%fused_computation.2 | loop fusion | bytes 24 | tf_op jit(solution)/shard_map/slice | solution.py:285
  26.8 0.0 copy-done.8
  26.8 2.5 %stack.15.meta = s32[8]{0:T(128)} concatenate(s32[1]{0:T(128)} %bitcast, s32[1]{0:T(128)} %bitcast.1, s32[1]{0:T(128)} %bitcast.2, s32[1]{0:T(128)} %constant.59.clone.1, s32[1]{0:T(128)} %bitcast.3, s32[1]{0:T(128)} %bitcast.4, s32[1]{0:T(128)} %bitcast.5, s32[1]{0:T(128)} %constant.59.clone.1), dimensions={0} | concatenate | bytes 64 | tf_op jit(solution)/shard_map/stack | solution.py:285
  29.3 0.0 copy-start.10
  29.3 0.0 copy-start.11
  29.3 0.0 collective-permute-done.4.swapped
  29.3 0.0 copy-start.12
  29.3 0.0 collective-permute-done.5.own_beside
  29.3 0.0 copy-start.14
  29.3 0.0 collective-permute-done.6.swapped_beside
  29.3 0.6 %copy-done.12 = f32[3,16,128]{2,1,0:T(8,128)} copy-done((f32[3,16,128]{2,1,0:T(8,128)}, f32[3,16,128]{2,1,0:T(8,128)S(1)}, u32[]{:S(2)}) %copy-start.12) | copy-done | bytes 24600
  29.9 0.0 copy-done.14
  29.9 0.0 copy-start.13
  29.9 0.6 %copy-done.13 = f32[3,16,128]{2,1,0:T(8,128)} copy-done((f32[3,16,128]{2,1,0:T(8,128)}, f32[3,16,128]{2,1,0:T(8,128)S(1)}, u32[]{:S(2)}) %copy-start.13) | copy-done | bytes 24600
  30.5 1.5 %choose.1.fields = f32[3,32,128]{2,1,0:T(8,128)} custom-call(s32[8]{0:T(128)} %stack.15.meta, f32[3,16,128]{2,1,0:T(8,128)} %copy-done.8, f32[3,16,128]{2,1,0:T(8,128)} %copy-done.12, f32[3,16,128]{2,1,0:T(8,128)} %copy-done.14, f32[3,16,128]{2,1,0:T(8,128)} %copy-done.13), custom_call_target="tpu_custom_call" | custom-call | tf_op jit(solution)/shard_map/choose/pallas_call | solution.py:318
  32.0 1.7 %collective-permute-start.7 = (f32[3,32,128]{2,1,0:T(8,128)}, f32[3,32,128]{2,1,0:T(8,128)S(1)}, u32[]{:S(2)}, u32[]{:S(2)}) collective-permute-start(f32[3,32,128]{2,1,0:T(8,128)} %choose.1.fields), channel_id=1, source_target_pairs={{0,1},{1,0},{2,3},{3,2},{4,5},{5,4},{6,7},{7,6},{8,9},{9,8},{10,11... | collective-permute-start | bytes 147464 | tf_op jit(solution)/shard_map/ppermute | solution.py:277
  33.7 3.0 %collective-permute-start.8 = (f32[3,32,128]{2,1,0:T(8,128)}, f32[3,32,128]{2,1,0:T(8,128)S(1)}, u32[]{:S(2)}, u32[]{:S(2)}) collective-permute-start(f32[3,32,128]{2,1,0:T(8,128)} %choose.1.fields), channel_id=1, source_target_pairs={{1,2},{2,1},{3,4},{4,3},{5,6},{6,5},{9,10},{10,9},{11,12},{12,11},... | collective-permute-start | bytes 147464 | tf_op jit(solution)/shard_map/ppermute | solution.py:277
  36.7 0.0 collective-permute-done.7.core_halo
  36.7 2.6 %collective-permute-done.8.chip_halo = f32[3,32,128]{2,1,0:T(8,128)S(1)} collective-permute-done((f32[3,32,128]{2,1,0:T(8,128)}, f32[3,32,128]{2,1,0:T(8,128)S(1)}, u32[]{:S(2)}, u32[]{:S(2)}) %collective-permute-start.8) | collective-permute-done | bytes 49184 | tf_op jit(solution)/shard_map/ppermute | solution.py:277
  39.3 0.0 copy-done.2
  39.3 0.0 copy-done.3
  39.3 0.0 copy-done.4
  39.3 0.0 copy-done.5
  39.3 0.0 copy-done.9
  39.3 0.0 copy-done.1
  39.4 0.0 copy-done.10
  39.4 0.0 copy-done.11
  39.4 0.0 copy-start
  39.4 0.8 %copy-done = f32[3,32,128]{2,1,0:T(8,128)S(1)} copy-done((f32[3,32,128]{2,1,0:T(8,128)S(1)}, f32[3,32,128]{2,1,0:T(8,128)}, u32[]{:S(2)}) %copy-start) | copy-done | bytes 49176
  40.2 2.5 %finish.1 = (f32[3,2,16,32]{3,2,1,0:T(8,128)}, f32[3,16,32]{2,1,0:T(8,128)}) custom-call(s32[8]{0:T(128)S(1)} %copy-done.11, f32[3,32,128]{2,1,0:T(8,128)S(1)} %copy-done, f32[3,32,128]{2,1,0:T(8,128)S(1)} %collective-permute-done.7.core_halo, f32[3,32,128]{2,1,0:T(8,128)S(1)} %collective-permute-done.8.chip_halo, bf16[256,384]{1,0:T(8,128)(2,1)S(1)} %copy-done.1, ...), custom_call_target="tpu_custom_call" | custom-call | tf_op jit(solution)/shard_map/finish/pallas_call | solution.py:328
  (1 shorter events, 0.0 us)
Async XLA Ops:
  0.6 10.4 %collective-permute-start.1 = (bf16[2,64,512]{2,1,0:T(8,128)(2,1)}, bf16[2,64,512]{2,1,0:T(8,128)(2,1)S(1)}, u32[]{:S(2)}, u32[]{:S(2)}) collective-permute-start(bf16[2,64,512]{2,1,0:T(8,128)(2,1)} %bitcast.9), channel_id=1, source_target_pairs={{32,64},{33,65},{34,66},{35,67},{36,68},{37,69},{38,70},{39,71},{4... | collective-permute-start | bytes 393224 | tf_op jit(solution)/shard_map/ppermute | solution.py:277
  1.3 9.7 %collective-permute-start.2 = (bf16[2,64,512]{2,1,0:T(8,128)(2,1)}, bf16[2,64,512]{2,1,0:T(8,128)(2,1)S(1)}, u32[]{:S(2)}, u32[]{:S(2)}) collective-permute-start(bf16[2,64,512]{2,1,0:T(8,128)(2,1)} %bitcast.10), channel_id=1, source_target_pairs={{0,32},{1,33},{2,34},{3,35},{4,36},{5,37},{6,38},{7,39},{8,40},{9,... | collective-permute-start | bytes 393224 | tf_op jit(solution)/shard_map/ppermute | solution.py:277
  6.7 5.6 %collective-permute-start = (bf16[2,64,512]{2,1,0:T(8,128)(2,1)}, bf16[2,64,512]{2,1,0:T(8,128)(2,1)S(1)}, u32[]{:S(2)}, u32[]{:S(2)}) collective-permute-start(bf16[2,64,512]{2,1,0:T(8,128)(2,1)} %bitcast.11), channel_id=1, source_target_pairs={{0,16},{1,17},{2,18},{3,19},{4,20},{5,21},{6,22},{7,23},{8,24},{9,... | collective-permute-start | bytes 393224 | tf_op jit(solution)/shard_map/ppermute | solution.py:277
  9.7 12.9 %collective-permute-start.3 = (bf16[2,64,512]{2,1,0:T(8,128)(2,1)}, bf16[2,64,512]{2,1,0:T(8,128)(2,1)S(1)}, u32[]{:S(2)}, u32[]{:S(2)}) collective-permute-start(bf16[2,64,512]{2,1,0:T(8,128)(2,1)} %bitcast.12), channel_id=1, source_target_pairs={{16,80},{17,81},{18,82},{19,83},{20,84},{21,85},{22,86},{23,87},{2... | collective-permute-start | bytes 393224 | tf_op jit(solution)/shard_map/ppermute | solution.py:277
  11.0 11.6 %copy-start.6 = (bf16[1,2,64,512]{3,2,1,0:T(8,128)(2,1)S(1)}, bf16[1,2,64,512]{3,2,1,0:T(8,128)(2,1)}, u32[]{:S(2)}) copy-start(bf16[1,2,64,512]{3,2,1,0:T(8,128)(2,1)} %param.10) | copy-start | bytes 393220
  11.0 11.6 %copy-start.7 = (bf16[512,128]{1,0:T(8,128)(2,1)S(1)}, bf16[512,128]{1,0:T(8,128)(2,1)}, u32[]{:S(2)}) copy-start(bf16[512,128]{1,0:T(8,128)(2,1)} %constant.61.clone.look) | copy-start | bytes 393220
  22.5 3.6 %copy-start.15 = (s32[1,3]{1,0:T(1,128)S(1)}, s32[1,3]{1,0:T(1,128)}, u32[]{:S(2)}) copy-start(s32[1,3]{1,0:T(1,128)} %param.11) | copy-start | bytes 40
  22.5 16.8 %copy-start.2 = (bf16[256,384]{1,0:T(8,128)(2,1)S(1)}, bf16[256,384]{1,0:T(8,128)(2,1)}, u32[]{:S(2)}) copy-start(bf16[256,384]{1,0:T(8,128)(2,1)} %constant.63.clone.cf_low) | copy-start | bytes 589828
  22.5 16.8 %copy-start.3 = (bf16[2,128,192]{2,1,0:T(8,128)(2,1)S(1)}, bf16[2,128,192]{2,1,0:T(8,128)(2,1)}, u32[]{:S(2)}) copy-start(bf16[2,128,192]{2,1,0:T(8,128)(2,1)} %constant.64.clone.lf) | copy-start | bytes 294916
  22.6 16.8 %copy-start.4 = (bf16[256,256]{1,0:T(8,128)(2,1)S(1)}, bf16[256,256]{1,0:T(8,128)(2,1)}, u32[]{:S(2)}) copy-start(bf16[256,256]{1,0:T(8,128)(2,1)} %constant.67.clone.cb_high) | copy-start | bytes 393220
  22.6 16.8 %copy-start.5 = (bf16[256,256]{1,0:T(8,128)(2,1)S(1)}, bf16[256,256]{1,0:T(8,128)(2,1)}, u32[]{:S(2)}) copy-start(bf16[256,256]{1,0:T(8,128)(2,1)} %constant.68.clone.cb_low) | copy-start | bytes 393220
  22.6 16.7 %copy-start.9 = (bf16[32,384]{1,0:T(8,128)(2,1)S(1)}, bf16[32,384]{1,0:T(8,128)(2,1)}, u32[]{:S(2)}) copy-start(bf16[32,384]{1,0:T(8,128)(2,1)} %constant.66.clone.lb) | copy-start | bytes 73732
  23.2 3.5 %copy-start.8 = (f32[3,16,128]{2,1,0:T(8,128)}, f32[3,16,128]{2,1,0:T(8,128)S(1)}, u32[]{:S(2)}) copy-start(f32[3,16,128]{2,1,0:T(8,128)S(1)} %get-tuple-element.6.own) | copy-start | bytes 73732
  23.3 16.1 %copy-start.1 = (bf16[256,384]{1,0:T(8,128)(2,1)S(1)}, bf16[256,384]{1,0:T(8,128)(2,1)}, u32[]{:S(2)}) copy-start(bf16[256,384]{1,0:T(8,128)(2,1)} %constant.62.clone.cf_high) | copy-start | bytes 589828
  23.3 6.0 %collective-permute-start.4 = (f32[3,16,128]{2,1,0:T(8,128)S(1)}, f32[3,16,128]{2,1,0:T(8,128)S(1)}, u32[]{:S(2)}, u32[]{:S(2)}) collective-permute-start(f32[3,16,128]{2,1,0:T(8,128)S(1)} %get-tuple-element.7), channel_id=1, source_target_pairs={{0,16},{1,17},{2,18},{3,19},{4,20},{5,21},{6,22},{7,23},{8,24},{9,... | collective-permute-start | bytes 73736 | tf_op jit(solution)/shard_map/ppermute | solution.py:277
  23.4 5.9 %collective-permute-start.6 = (f32[3,16,128]{2,1,0:T(8,128)S(1)}, f32[3,16,128]{2,1,0:T(8,128)S(1)}, u32[]{:S(2)}, u32[]{:S(2)}) collective-permute-start(f32[3,16,128]{2,1,0:T(8,128)S(1)} %get-tuple-element.7), channel_id=1, source_target_pairs={{0,24},{1,25},{2,26},{3,27},{4,28},{5,29},{6,30},{7,31},{8,16},{9,... | collective-permute-start | bytes 73736 | tf_op jit(solution)/shard_map/ppermute | solution.py:277
  26.2 3.1 %collective-permute-start.5 = (f32[3,16,128]{2,1,0:T(8,128)S(1)}, f32[3,16,128]{2,1,0:T(8,128)S(1)}, u32[]{:S(2)}, u32[]{:S(2)}) collective-permute-start(f32[3,16,128]{2,1,0:T(8,128)S(1)} %get-tuple-element.6.own), channel_id=1, source_target_pairs={{0,8},{1,9},{2,10},{3,11},{4,12},{5,13},{6,14},{7,15},{8,0},{9,1},... | collective-permute-start | bytes 73736 | tf_op jit(solution)/shard_map/ppermute | solution.py:277
  29.3 10.1 %copy-start.10 = (bf16[2,16,64]{2,1,0:T(8,128)(2,1)S(1)}, bf16[2,16,64]{2,1,0:T(8,128)(2,1)}, u32[]{:S(2)}) copy-start(bf16[2,16,64]{2,1,0:T(8,128)(2,1)} %constant.65.clone.window) | copy-start | bytes 12292
  29.3 10.1 %copy-start.11 = (s32[8]{0:T(128)S(1)}, s32[8]{0:T(128)}, u32[]{:S(2)}) copy-start(s32[8]{0:T(128)} %stack.15.meta) | copy-start | bytes 100
  29.3 0.6 %copy-start.12 = (f32[3,16,128]{2,1,0:T(8,128)}, f32[3,16,128]{2,1,0:T(8,128)S(1)}, u32[]{:S(2)}) copy-start(f32[3,16,128]{2,1,0:T(8,128)S(1)} %collective-permute-done.4.swapped) | copy-start | bytes 73732
  29.3 0.6 %copy-start.14 = (f32[3,16,128]{2,1,0:T(8,128)}, f32[3,16,128]{2,1,0:T(8,128)S(1)}, u32[]{:S(2)}) copy-start(f32[3,16,128]{2,1,0:T(8,128)S(1)} %collective-permute-done.5.own_beside) | copy-start | bytes 73732
  29.9 0.6 %copy-start.13 = (f32[3,16,128]{2,1,0:T(8,128)}, f32[3,16,128]{2,1,0:T(8,128)S(1)}, u32[]{:S(2)}) copy-start(f32[3,16,128]{2,1,0:T(8,128)S(1)} %collective-permute-done.6.swapped_beside) | copy-start | bytes 73732
  32.0 4.7 %collective-permute-start.7 = (f32[3,32,128]{2,1,0:T(8,128)}, f32[3,32,128]{2,1,0:T(8,128)S(1)}, u32[]{:S(2)}, u32[]{:S(2)}) collective-permute-start(f32[3,32,128]{2,1,0:T(8,128)} %choose.1.fields), channel_id=1, source_target_pairs={{0,1},{1,0},{2,3},{3,2},{4,5},{5,4},{6,7},{7,6},{8,9},{9,8},{10,11... | collective-permute-start | bytes 147464 | tf_op jit(solution)/shard_map/ppermute | solution.py:277
  33.7 5.6 %collective-permute-start.8 = (f32[3,32,128]{2,1,0:T(8,128)}, f32[3,32,128]{2,1,0:T(8,128)S(1)}, u32[]{:S(2)}, u32[]{:S(2)}) collective-permute-start(f32[3,32,128]{2,1,0:T(8,128)} %choose.1.fields), channel_id=1, source_target_pairs={{1,2},{2,1},{3,4},{4,3},{5,6},{6,5},{9,10},{10,9},{11,12},{12,11},... | collective-permute-start | bytes 147464 | tf_op jit(solution)/shard_map/ppermute | solution.py:277
  39.4 0.8 %copy-start = (f32[3,32,128]{2,1,0:T(8,128)S(1)}, f32[3,32,128]{2,1,0:T(8,128)}, u32[]{:S(2)}) copy-start(f32[3,32,128]{2,1,0:T(8,128)} %choose.1.fields) | copy-start | bytes 147460

commit v2 on v1

--- a/solution.py
+++ b/solution.py
@@ -168,11 +168,11 @@
             other_out[index - 3] = row
 
 
-def choose_kernel(meta, own, swapped, own_beside, swapped_beside, out):
-    position = meta[0]
+def choose_kernel(pairs, own, swapped, own_beside, swapped_beside, out):
+    position = lax.axis_index("tm")
     odd = position % 2
     for slot in range(3):
-        offset = meta[4 + slot] - position
+        offset = pairs[0, slot] - position
         flipped = jnp.where(odd == 1, -offset, offset)
         near = jnp.where(flipped == 1, 0, jnp.where(offset == 2, 1, 2))
         third = jnp.where(odd == 1, 4, 3)
@@ -186,10 +186,10 @@
 
 
 def finish_kernel(
-    meta, fields, core_halo, chip_halo, cf_high, cf_low, lf, window, lb, cb_high, cb_low, filtered, coherence
+    fields, core_halo, chip_halo, cf_high, cf_low, lf, window, lb, cb_high, cb_low, filtered, coherence
 ):
-    side = meta[1]
-    core = meta[2]
+    side = lax.axis_index("az")
+    core = lax.axis_index("rg") % 2
     lane = lax.broadcasted_iota(jnp.int32, (1, 128), 1)
     place = lane % 32
     from_core = (place >= 16) == (core == 1)
@@ -280,9 +280,6 @@
 def per_device(slc, pairs):
     tile = slc[0]
     position = lax.axis_index("tm")
-    side = lax.axis_index("az")
-    column = lax.axis_index("rg")
-    meta = jnp.stack([position, side, column % 2, 0, pairs[0, 0], pairs[0, 1], pairs[0, 2], 0]).astype(jnp.int32)
 
     def even_pair(z, h, l, r):
         return (z ^ 1, h, l, r)
@@ -320,19 +317,20 @@
         out_shape=jax.ShapeDtypeStruct((3, 32, 128), F32),
         in_specs=[SMEM] + [VMEM] * 4,
         out_specs=VMEM,
+        compiler_params=pltpu.CompilerParams(vmem_limit_bytes=4 * 2**20),
         name="choose",
-    )(meta, own_fields, swapped, own_beside, swapped_beside)
+    )(pairs, own_fields, swapped, own_beside, swapped_beside)
 
     core_halo = moved(fields, lambda z, h, l, r: (z, h, l, r ^ 1))
     chip_halo = moved(fields, lambda z, h, l, r: (z, h, l, ((r + 1) ^ 1) - 1))
     filtered, coherence = pl.pallas_call(
         finish_kernel,
         out_shape=(jax.ShapeDtypeStruct((3, 2, 16, 32), F32), jax.ShapeDtypeStruct((3, 16, 32), F32)),
-        in_specs=[SMEM] + [VMEM] * 10,
+        in_specs=[VMEM] * 10,
         out_specs=(VMEM, VMEM),
         compiler_params=pltpu.CompilerParams(vmem_limit_bytes=24 * 2**20),
         name="finish",
-    )(meta, fields, core_halo, chip_halo, *[jnp.asarray(t) for t in tables()])
+    )(fields, core_halo, chip_halo, *[jnp.asarray(t) for t in tables()])
     return (filtered[None], coherence[None])
 
 

time: 43 us -> 38 us (0.88)
  local copies, waits for them, and re-layouts: 5.17 us -> 0.06 us
  Pallas kernels: 4.6 us -> 3.17 us
  waiting for transfers between devices: 14.1 us -> 15.1 us
  starting transfers between devices: 17.9 us -> 18.6 us
    another operation x1 -> x0, local copies, waits for them, and re-layouts: 2.5 us -> none  [per_device(): jnp.stack([position, side, column % 2, 0, pairs[0, 0], pairs[0, 1], pairs...]
    unnamed x32 -> x20, local copies, waits for them, and re-layouts: 2.06 us -> 0.06 us
    ppermute x9, waiting for transfers between devices: 14.1 us -> 15.1 us  [moved(): return lax.ppermute(value, EVERY, pairs)]
    pallas_call x1, Pallas kernels: 1.45 us -> 0.58 us  [per_device(): pl.pallas_call(choose_kernel, out_shape=jax.ShapeDtypeStruct((3, 32, 128)...]
    ppermute x9, starting transfers between devices: 17.9 us -> 18.6 us  [moved(): return lax.ppermute(value, EVERY, pairs)]
    slice x1 -> x0, local copies, waits for them, and re-layouts: 0.62 us -> none  [per_device(): pairs[0, 2]]
    pallas_call x1, Pallas kernels: 2.5 us -> 1.95 us  [per_device(): pl.pallas_call(finish_kernel, out_shape=(jax.ShapeDtypeStruct((3, 2, 16,...]
  transfers between devices with their start and end apart: 9 -> 9, of which waited for: 3 -> 5; matrix products, arithmetic and copies ran while one was open for 7% -> 0% of each run, Pallas kernels for 0% -> 0%
where the time goes in v2:
time: 38 us; the launch traced here: 37.8 us
  starting transfers between devices  18.6 us (49%)
  waiting for transfers between devices  15.1 us (40%)
  Pallas kernels  3.17 us (8%)
  between operations  0.85 us (2%)
    ppermute x9, starting transfers between devices, moved(): return lax.ppermute(value, EVERY, pairs)  18.6 us
    ppermute x9, waiting for transfers between devices, moved(): return lax.ppermute(value, EVERY, pairs)  15.1 us
    pallas_call x1, Pallas kernels, per_device(): pl.pallas_call(finish_kernel, out_shape=(jax.ShapeDtypeStruct((3, 2, 16,...  1.95 us
  transfers between devices with their start and end apart: 9, of which 5 were waited for; matrix products, arithmetic and copies ran while one was open for 0% of the time, Pallas kernels for 0%

profile of v2, /device:TPU:1, one launch (start us, length us, event | category | flops | bytes accessed | tf_op | source)
XLA Modules:
  0.0 37.8 jit_solution(2629139494508272394)
XLA Ops:
  0.6 0.7 %collective-permute-start.1 = (bf16[2,64,512]{2,1,0:T(8,128)(2,1)}, bf16[2,64,512]{2,1,0:T(8,128)(2,1)S(1)}, u32[]{:S(2)}, u32[]{:S(2)}) collective-permute-start(bf16[2,64,512]{2,1,0:T(8,128)(2,1)} %bitcast.3), channel_id=1, source_target_pairs={{32,64},{33,65},{34,66},{35,67},{36,68},{37,69},{38,70},{39,71},{4... | collective-permute-start | bytes 393224 | tf_op jit(solution)/shard_map/ppermute | solution.py:277
  1.3 5.4 %collective-permute-start.2 = (bf16[2,64,512]{2,1,0:T(8,128)(2,1)}, bf16[2,64,512]{2,1,0:T(8,128)(2,1)S(1)}, u32[]{:S(2)}, u32[]{:S(2)}) collective-permute-start(bf16[2,64,512]{2,1,0:T(8,128)(2,1)} %bitcast.4), channel_id=1, source_target_pairs={{0,32},{1,33},{2,34},{3,35},{4,36},{5,37},{6,38},{7,39},{8,40},{9,... | collective-permute-start | bytes 393224 | tf_op jit(solution)/shard_map/ppermute | solution.py:277
  6.7 2.9 %collective-permute-start = (bf16[2,64,512]{2,1,0:T(8,128)(2,1)}, bf16[2,64,512]{2,1,0:T(8,128)(2,1)S(1)}, u32[]{:S(2)}, u32[]{:S(2)}) collective-permute-start(bf16[2,64,512]{2,1,0:T(8,128)(2,1)} %bitcast.5), channel_id=1, source_target_pairs={{0,16},{1,17},{2,18},{3,19},{4,20},{5,21},{6,22},{7,23},{8,24},{9,... | collective-permute-start | bytes 393224 | tf_op jit(solution)/shard_map/ppermute | solution.py:277
  9.7 1.3 %collective-permute-start.3 = (bf16[2,64,512]{2,1,0:T(8,128)(2,1)}, bf16[2,64,512]{2,1,0:T(8,128)(2,1)S(1)}, u32[]{:S(2)}, u32[]{:S(2)}) collective-permute-start(bf16[2,64,512]{2,1,0:T(8,128)(2,1)} %bitcast.6), channel_id=1, source_target_pairs={{16,80},{17,81},{18,82},{19,83},{20,84},{21,85},{22,86},{23,87},{2... | collective-permute-start | bytes 393224 | tf_op jit(solution)/shard_map/ppermute | solution.py:277
  11.0 0.0 copy-start.2
  11.0 0.0 copy-start.3
  11.0 0.0 collective-permute-done.1
  11.0 0.0 collective-permute-done.2
  11.0 1.2 %collective-permute-done.other = bf16[2,64,512]{2,1,0:T(8,128)(2,1)S(1)} collective-permute-done((bf16[2,64,512]{2,1,0:T(8,128)(2,1)}, bf16[2,64,512]{2,1,0:T(8,128)(2,1)S(1)}, u32[]{:S(2)}, u32[]{:S(2)}) %collective-permute-start) | collective-permute-done | bytes 131104 | tf_op jit(solution)/shard_map/ppermute | solution.py:277
  12.3 10.2 %collective-permute-done.3.far = bf16[2,64,512]{2,1,0:T(8,128)(2,1)S(1)} collective-permute-done((bf16[2,64,512]{2,1,0:T(8,128)(2,1)}, bf16[2,64,512]{2,1,0:T(8,128)(2,1)S(1)}, u32[]{:S(2)}, u32[]{:S(2)}) %collective-permute-start.3) | collective-permute-done | bytes 131104 | tf_op jit(solution)/shard_map/ppermute | solution.py:277
  22.5 0.0 copy-done.2
  22.5 0.0 copy-done.3
  22.5 0.0 copy-start.9
  22.5 0.0 copy-start
  22.5 0.0 copy-start.1
  22.6 0.0 copy-start.5
  22.6 0.0 copy-start.6
  22.6 0.0 copy-start.7
  22.6 0.6 %cross.1 = (f32[3,16,128]{2,1,0:T(8,128)S(1)}, f32[3,16,128]{2,1,0:T(8,128)S(1)}) custom-call(bf16[2,64,512]{2,1,0:T(8,128)(2,1)S(1)} %bitcast.7, bf16[2,64,512]{2,1,0:T(8,128)(2,1)S(1)} %collective-permute-done.other, bf16[2,64,512]{2,1,0:T(8,128)(2,1)S(1)} %get-tuple-element.11.up, bf16[2,64,512]{2,1,0:T(8,128)(2,1)S(1)} %get-tuple-element.10.down, ...), custom_call_target="tpu_custom_call" | custom-call | tf_op jit(solution)/shard_map/cross/pallas_call | solution.py:302
  23.2 0.0 copy-start.4
  23.3 0.1 collective-permute-start.4
  23.4 0.0 copy-start.8
  23.4 0.5 %collective-permute-start.5 = (f32[3,16,128]{2,1,0:T(8,128)S(1)}, f32[3,16,128]{2,1,0:T(8,128)S(1)}, u32[]{:S(2)}, u32[]{:S(2)}) collective-permute-start(f32[3,16,128]{2,1,0:T(8,128)S(1)} %get-tuple-element.6.own), channel_id=1, source_target_pairs={{0,8},{1,9},{2,10},{3,11},{4,12},{5,13},{6,14},{7,15},{8,0},{9,1},... | collective-permute-start | bytes 73736 | tf_op jit(solution)/shard_map/ppermute | solution.py:277
  23.9 2.7 %collective-permute-start.6 = (f32[3,16,128]{2,1,0:T(8,128)S(1)}, f32[3,16,128]{2,1,0:T(8,128)S(1)}, u32[]{:S(2)}, u32[]{:S(2)}) collective-permute-start(f32[3,16,128]{2,1,0:T(8,128)S(1)} %get-tuple-element.7), channel_id=1, source_target_pairs={{0,24},{1,25},{2,26},{3,27},{4,28},{5,29},{6,30},{7,31},{8,16},{9,... | collective-permute-start | bytes 73736 | tf_op jit(solution)/shard_map/ppermute | solution.py:277
  26.6 0.9 %collective-permute-done.4.swapped = f32[3,16,128]{2,1,0:T(8,128)S(1)} collective-permute-done((f32[3,16,128]{2,1,0:T(8,128)S(1)}, f32[3,16,128]{2,1,0:T(8,128)S(1)}, u32[]{:S(2)}, u32[]{:S(2)}) %collective-permute-start.4) | collective-permute-done | bytes 24608 | tf_op jit(solution)/shard_map/ppermute | solution.py:277
  27.5 0.0 collective-permute-done.5.own_beside
  27.5 0.3 collective-permute-done.6.swapped_beside
  27.8 0.0 copy-done.9
  27.8 0.6 %choose.1.fields = f32[3,32,128]{2,1,0:T(8,128)S(1)} custom-call(s32[1,3]{1,0:T(1,128)S(1)} %copy-done.9, f32[3,16,128]{2,1,0:T(8,128)S(1)} %get-tuple-element.6.own, f32[3,16,128]{2,1,0:T(8,128)S(1)} %collective-permute-done.4.swapped, f32[3,16,128]{2,1,0:T(8,128)S(1)} %collective-permute-done.5.own_beside, ...), custom_call_target="tpu_custom_call" | custom-call | tf_op jit(solution)/shard_map/choose/pallas_call | solution.py:315
  28.4 2.0 %collective-permute-start.7 = (f32[3,32,128]{2,1,0:T(8,128)S(1)}, f32[3,32,128]{2,1,0:T(8,128)S(1)}, u32[]{:S(2)}, u32[]{:S(2)}) collective-permute-start(f32[3,32,128]{2,1,0:T(8,128)S(1)} %choose.1.fields), channel_id=1, source_target_pairs={{0,1},{1,0},{2,3},{3,2},{4,5},{5,4},{6,7},{7,6},{8,9},{9,8},{10,11... | collective-permute-start | bytes 147464 | tf_op jit(solution)/shard_map/ppermute | solution.py:277
  30.4 3.0 %collective-permute-start.8 = (f32[3,32,128]{2,1,0:T(8,128)S(1)}, f32[3,32,128]{2,1,0:T(8,128)S(1)}, u32[]{:S(2)}, u32[]{:S(2)}) collective-permute-start(f32[3,32,128]{2,1,0:T(8,128)S(1)} %choose.1.fields), channel_id=1, source_target_pairs={{1,2},{2,1},{3,4},{4,3},{5,6},{6,5},{9,10},{10,9},{11,12},{12,11},... | collective-permute-start | bytes 147464 | tf_op jit(solution)/shard_map/ppermute | solution.py:277
  33.4 0.0 collective-permute-done.7.core_halo
  33.5 2.4 %collective-permute-done.8.chip_halo = f32[3,32,128]{2,1,0:T(8,128)S(1)} collective-permute-done((f32[3,32,128]{2,1,0:T(8,128)S(1)}, f32[3,32,128]{2,1,0:T(8,128)S(1)}, u32[]{:S(2)}, u32[]{:S(2)}) %collective-permute-start.8) | collective-permute-done | bytes 49184 | tf_op jit(solution)/shard_map/ppermute | solution.py:277
  35.8 0.0 copy-done
  35.8 0.0 copy-done.1
  35.8 0.0 copy-done.5
  35.8 0.0 copy-done.6
  35.8 0.0 copy-done.7
  35.8 0.0 copy-done.4
  35.9 0.0 copy-done.8
  35.9 1.9 %finish.1 = (f32[3,2,16,32]{3,2,1,0:T(8,128)}, f32[3,16,32]{2,1,0:T(8,128)}) custom-call(f32[3,32,128]{2,1,0:T(8,128)S(1)} %choose.1.fields, f32[3,32,128]{2,1,0:T(8,128)S(1)} %collective-permute-done.7.core_halo, f32[3,32,128]{2,1,0:T(8,128)S(1)} %collective-permute-done.8.chip_halo, bf16[256,384]{1,0:T(8,128)(2,1)S(1)} %copy-done, ...), custom_call_target="tpu_custom_call" | custom-call | tf_op jit(solution)/shard_map/finish/pallas_call | solution.py:326
  (1 shorter events, 0.0 us)
Async XLA Ops:
  0.6 10.4 %collective-permute-start.1 = (bf16[2,64,512]{2,1,0:T(8,128)(2,1)}, bf16[2,64,512]{2,1,0:T(8,128)(2,1)S(1)}, u32[]{:S(2)}, u32[]{:S(2)}) collective-permute-start(bf16[2,64,512]{2,1,0:T(8,128)(2,1)} %bitcast.3), channel_id=1, source_target_pairs={{32,64},{33,65},{34,66},{35,67},{36,68},{37,69},{38,70},{39,71},{4... | collective-permute-start | bytes 393224 | tf_op jit(solution)/shard_map/ppermute | solution.py:277
  1.3 9.7 %collective-permute-start.2 = (bf16[2,64,512]{2,1,0:T(8,128)(2,1)}, bf16[2,64,512]{2,1,0:T(8,128)(2,1)S(1)}, u32[]{:S(2)}, u32[]{:S(2)}) collective-permute-start(bf16[2,64,512]{2,1,0:T(8,128)(2,1)} %bitcast.4), channel_id=1, source_target_pairs={{0,32},{1,33},{2,34},{3,35},{4,36},{5,37},{6,38},{7,39},{8,40},{9,... | collective-permute-start | bytes 393224 | tf_op jit(solution)/shard_map/ppermute | solution.py:277
  6.7 5.6 %collective-permute-start = (bf16[2,64,512]{2,1,0:T(8,128)(2,1)}, bf16[2,64,512]{2,1,0:T(8,128)(2,1)S(1)}, u32[]{:S(2)}, u32[]{:S(2)}) collective-permute-start(bf16[2,64,512]{2,1,0:T(8,128)(2,1)} %bitcast.5), channel_id=1, source_target_pairs={{0,16},{1,17},{2,18},{3,19},{4,20},{5,21},{6,22},{7,23},{8,24},{9,... | collective-permute-start | bytes 393224 | tf_op jit(solution)/shard_map/ppermute | solution.py:277
  9.7 12.9 %collective-permute-start.3 = (bf16[2,64,512]{2,1,0:T(8,128)(2,1)}, bf16[2,64,512]{2,1,0:T(8,128)(2,1)S(1)}, u32[]{:S(2)}, u32[]{:S(2)}) collective-permute-start(bf16[2,64,512]{2,1,0:T(8,128)(2,1)} %bitcast.6), channel_id=1, source_target_pairs={{16,80},{17,81},{18,82},{19,83},{20,84},{21,85},{22,86},{23,87},{2... | collective-permute-start | bytes 393224 | tf_op jit(solution)/shard_map/ppermute | solution.py:277
  11.0 11.6 %copy-start.2 = (bf16[1,2,64,512]{3,2,1,0:T(8,128)(2,1)S(1)}, bf16[1,2,64,512]{3,2,1,0:T(8,128)(2,1)}, u32[]{:S(2)}) copy-start(bf16[1,2,64,512]{3,2,1,0:T(8,128)(2,1)} %param.10) | copy-start | bytes 393220
  11.0 11.6 %copy-start.3 = (bf16[512,128]{1,0:T(8,128)(2,1)S(1)}, bf16[512,128]{1,0:T(8,128)(2,1)}, u32[]{:S(2)}) copy-start(bf16[512,128]{1,0:T(8,128)(2,1)} %constant.46.clone.look) | copy-start | bytes 393220
  22.5 5.3 %copy-start.9 = (s32[1,3]{1,0:T(1,128)S(1)}, s32[1,3]{1,0:T(1,128)}, u32[]{:S(2)}) copy-start(s32[1,3]{1,0:T(1,128)} %pairs.1) | copy-start | bytes 40
  22.5 13.3 %copy-start = (bf16[256,384]{1,0:T(8,128)(2,1)S(1)}, bf16[256,384]{1,0:T(8,128)(2,1)}, u32[]{:S(2)}) copy-start(bf16[256,384]{1,0:T(8,128)(2,1)} %constant.47.clone.cf_high) | copy-start | bytes 589828
  22.5 13.3 %copy-start.1 = (bf16[256,384]{1,0:T(8,128)(2,1)S(1)}, bf16[256,384]{1,0:T(8,128)(2,1)}, u32[]{:S(2)}) copy-start(bf16[256,384]{1,0:T(8,128)(2,1)} %constant.48.clone.cf_low) | copy-start | bytes 589828
  22.6 13.3 %copy-start.5 = (bf16[256,256]{1,0:T(8,128)(2,1)S(1)}, bf16[256,256]{1,0:T(8,128)(2,1)}, u32[]{:S(2)}) copy-start(bf16[256,256]{1,0:T(8,128)(2,1)} %constant.52.clone.cb_high) | copy-start | bytes 393220
  22.6 13.3 %copy-start.6 = (bf16[256,256]{1,0:T(8,128)(2,1)S(1)}, bf16[256,256]{1,0:T(8,128)(2,1)}, u32[]{:S(2)}) copy-start(bf16[256,256]{1,0:T(8,128)(2,1)} %constant.53.clone.cb_low) | copy-start | bytes 393220
  22.6 13.3 %copy-start.7 = (bf16[32,384]{1,0:T(8,128)(2,1)S(1)}, bf16[32,384]{1,0:T(8,128)(2,1)}, u32[]{:S(2)}) copy-start(bf16[32,384]{1,0:T(8,128)(2,1)} %constant.51.clone.lb) | copy-start | bytes 73732
  23.2 12.6 %copy-start.4 = (bf16[2,128,192]{2,1,0:T(8,128)(2,1)S(1)}, bf16[2,128,192]{2,1,0:T(8,128)(2,1)}, u32[]{:S(2)}) copy-start(bf16[2,128,192]{2,1,0:T(8,128)(2,1)} %constant.49.clone.lf) | copy-start | bytes 294916
  23.3 4.3 %collective-permute-start.4 = (f32[3,16,128]{2,1,0:T(8,128)S(1)}, f32[3,16,128]{2,1,0:T(8,128)S(1)}, u32[]{:S(2)}, u32[]{:S(2)}) collective-permute-start(f32[3,16,128]{2,1,0:T(8,128)S(1)} %get-tuple-element.7), channel_id=1, source_target_pairs={{0,16},{1,17},{2,18},{3,19},{4,20},{5,21},{6,22},{7,23},{8,24},{9,... | collective-permute-start | bytes 73736 | tf_op jit(solution)/shard_map/ppermute | solution.py:277
  23.4 12.5 %copy-start.8 = (bf16[2,16,64]{2,1,0:T(8,128)(2,1)S(1)}, bf16[2,16,64]{2,1,0:T(8,128)(2,1)}, u32[]{:S(2)}) copy-start(bf16[2,16,64]{2,1,0:T(8,128)(2,1)} %constant.50.clone.window) | copy-start | bytes 12292
  23.4 4.2 %collective-permute-start.5 = (f32[3,16,128]{2,1,0:T(8,128)S(1)}, f32[3,16,128]{2,1,0:T(8,128)S(1)}, u32[]{:S(2)}, u32[]{:S(2)}) collective-permute-start(f32[3,16,128]{2,1,0:T(8,128)S(1)} %get-tuple-element.6.own), channel_id=1, source_target_pairs={{0,8},{1,9},{2,10},{3,11},{4,12},{5,13},{6,14},{7,15},{8,0},{9,1},... | collective-permute-start | bytes 73736 | tf_op jit(solution)/shard_map/ppermute | solution.py:277
  23.9 4.0 %collective-permute-start.6 = (f32[3,16,128]{2,1,0:T(8,128)S(1)}, f32[3,16,128]{2,1,0:T(8,128)S(1)}, u32[]{:S(2)}, u32[]{:S(2)}) collective-permute-start(f32[3,16,128]{2,1,0:T(8,128)S(1)} %get-tuple-element.7), channel_id=1, source_target_pairs={{0,24},{1,25},{2,26},{3,27},{4,28},{5,29},{6,30},{7,31},{8,16},{9,... | collective-permute-start | bytes 73736 | tf_op jit(solution)/shard_map/ppermute | solution.py:277
  28.4 5.0 %collective-permute-start.7 = (f32[3,32,128]{2,1,0:T(8,128)S(1)}, f32[3,32,128]{2,1,0:T(8,128)S(1)}, u32[]{:S(2)}, u32[]{:S(2)}) collective-permute-start(f32[3,32,128]{2,1,0:T(8,128)S(1)} %choose.1.fields), channel_id=1, source_target_pairs={{0,1},{1,0},{2,3},{3,2},{4,5},{5,4},{6,7},{7,6},{8,9},{9,8},{10,11... | collective-permute-start | bytes 147464 | tf_op jit(solution)/shard_map/ppermute | solution.py:277
  30.4 5.4 %collective-permute-start.8 = (f32[3,32,128]{2,1,0:T(8,128)S(1)}, f32[3,32,128]{2,1,0:T(8,128)S(1)}, u32[]{:S(2)}, u32[]{:S(2)}) collective-permute-start(f32[3,32,128]{2,1,0:T(8,128)S(1)} %choose.1.fields), channel_id=1, source_target_pairs={{1,2},{2,1},{3,4},{4,3},{5,6},{6,5},{9,10},{10,9},{11,12},{12,11},... | collective-permute-start | bytes 147464 | tf_op jit(solution)/shard_map/ppermute | solution.py:277

commit v3 on v2

--- a/solution.py
+++ b/solution.py
@@ -131,25 +131,29 @@
     return jnp.dot(left, right, preferred_element_type=F32)
 
 
-def cross_kernel(own, other, up, down, far, look, own_out, other_out, wide, sums):
-    tiles = (own, other, up, down, far)
+def widened(tiles, wide):
     for index, tile in enumerate(tiles):
         for part in range(2):
             for chunk in range(4):
-                wide[index * 2 + part, chunk] = tile[part, :, chunk * 128 : chunk * 128 + 128].astype(F32)
-    couples = ((0, 1), (0, 2), (0, 3), (1, 2), (1, 3), (1, 4))
+                at = slice(chunk * 128, chunk * 128 + 128)
+                wide[index * 2 + part, chunk] = tile[part, :, at].astype(F32)
+
+
+def looked_records(couples, count, wide, sums, look):
+    number = len(couples)
     for chunk in range(4):
         at = slice(chunk * 128, chunk * 128 + 128)
-        totals = [None] * 17
+        totals = [None] * (2 * number + count)
         for line in range(4):
-            real = [wide[2 * i, chunk, pl.ds(line, 16, stride=4), :] for i in range(5)]
-            imag = [wide[2 * i + 1, chunk, pl.ds(line, 16, stride=4), :] for i in range(5)]
+            rows = pl.ds(line, 16, stride=4)
+            real = [wide[2 * i, chunk, rows, :] for i in range(count)]
+            imag = [wide[2 * i + 1, chunk, rows, :] for i in range(count)]
             terms = []
             for u, v in couples:
                 terms.append(real[u] * real[v] + imag[u] * imag[v])
             for u, v in couples:
                 terms.append(imag[u] * real[v] - real[u] * imag[v])
-            for u in range(5):
+            for u in range(count):
                 terms.append(real[u] * real[u] + imag[u] * imag[u])
             totals = [t if s is None else s + t for s, t in zip(totals, terms)]
         for index, total in enumerate(totals):
@@ -157,48 +161,86 @@
     high, low = halves(sums[...])
     table = look[...]
     looked = dot(high, table) + dot(low, table)
-    fields = [looked[i * 16 : i * 16 + 16] for i in range(17)]
-    far_power = [pltpu.roll(fields[12 + i], 64, 1) for i in range(5)]
-    own_power = [pltpu.roll(fields[12 + i], 96, 1) for i in range(2)]
+    fields = [looked[i * 16 : i * 16 + 16] for i in range(2 * number + count)]
+    power = fields[2 * number :]
+    records = []
     for index, (u, v) in enumerate(couples):
-        row = fields[index] + pltpu.roll(fields[6 + index], 32, 1) + far_power[v] + own_power[u]
-        if u == 0:
-            own_out[index] = row
-        else:
-            other_out[index - 3] = row
-
-
-def choose_kernel(pairs, own, swapped, own_beside, swapped_beside, out):
+        crossed = fields[index] + pltpu.roll(fields[number + index], 32, 1)
+        records.append(crossed + pltpu.roll(power[v], 64, 1) + pltpu.roll(power[u], 96, 1))
+    return records
+
+
+def cross_kernel(own, other, up, down, look, own_out, other_out, wide, sums):
+    widened((own, other, up, down), wide)
+    records = looked_records(((0, 1), (0, 2), (0, 3), (1, 2), (1, 3)), 4, wide, sums, look)
+    for index in range(3):
+        own_out[index] = records[index]
+    for index in range(2):
+        other_out[index] = records[3 + index]
+
+
+def offsets_of(pairs):
     position = lax.axis_index("tm")
-    odd = position % 2
+    odd = position % 2 == 1
+    offset = pairs[...] - position
+    return odd, jnp.where(odd, -offset, offset)
+
+
+def crossed_slots(flipped):
+    return (flipped == 3) | (flipped == -1)
+
+
+def choose_kernel(pairs, own_tile, far_tile, own, swapped, look, out, wide, sums):
+    odd, flipped = offsets_of(pairs)
+    up = jnp.where(odd, -2, 2)
+    widened((own_tile, far_tile), wide)
+    (far,) = looked_records(((0, 1),), 2, wide, sums, look)
+    third = jnp.where(odd, swapped[1], swapped[0])
+    first = jnp.where(odd, swapped[0], swapped[1])
     for slot in range(3):
-        offset = pairs[0, slot] - position
-        flipped = jnp.where(odd == 1, -offset, offset)
-        near = jnp.where(flipped == 1, 0, jnp.where(offset == 2, 1, 2))
-        third = jnp.where(odd == 1, 4, 3)
-        first = jnp.where(odd == 1, 3, 4)
-        away = jnp.where(flipped == 3, third, jnp.where(flipped == -1, first, 5)) - 3
-        is_near = (flipped == 1) | (offset == 2) | (offset == -2)
-        near = jnp.where(is_near, near, 0)
-        away = jnp.where(is_near, 0, away)
-        out[slot, 0:16] = jnp.where(is_near, own[near], swapped[away])
-        out[slot, 16:32] = jnp.where(is_near, own_beside[near], swapped_beside[away])
+        at = flipped[:, slot : slot + 1]
+        record = jnp.where(at == 1, own[0], far)
+        record = jnp.where(at == up, own[1], record)
+        record = jnp.where(at == -up, own[2], record)
+        record = jnp.where(at == 3, third, record)
+        out[slot] = jnp.where(at == -1, first, record)
 
 
 def finish_kernel(
-    fields, core_halo, chip_halo, cf_high, cf_low, lf, window, lb, cb_high, cb_low, filtered, coherence
+    pairs,
+    fields,
+    core_fields,
+    chip_fields,
+    cf_high,
+    cf_low,
+    lf,
+    window,
+    lb,
+    cb_high,
+    cb_low,
+    filtered,
+    coherence,
 ):
     side = lax.axis_index("az")
-    core = lax.axis_index("rg") % 2
+    column = lax.axis_index("rg")
+    core = column % 2
     lane = lax.broadcasted_iota(jnp.int32, (1, 128), 1)
     place = lane % 32
     from_core = (place >= 16) == (core == 1)
-    halo = jnp.where(from_core, core_halo[...].reshape(96, 128), chip_halo[...].reshape(96, 128))
+    inside = (column > 0) & (column < 7)
+
+    from_chip = jnp.where(inside, chip_fields[...].reshape(96, 128), 0.0)
+    halo = jnp.where(from_core, core_fields[...].reshape(96, 128), from_chip)
     values = jnp.concatenate([fields[...].reshape(96, 128), halo], axis=1)
     high, low = halves(values)
     table = cf_high[...]
     mixed = dot(high, table) + dot(low, table) + dot(high, cf_low[...])
-    rows = [mixed[32 * s : 32 * s + 32] for s in range(3)]
+    crossed = crossed_slots(offsets_of(pairs)[1])
+    rows = []
+    for slot in range(3):
+        first, second = mixed[16 * slot : 16 * slot + 16], mixed[48 + 16 * slot : 64 + 16 * slot]
+        turn = crossed[:, slot : slot + 1]
+        rows.append(jnp.concatenate([jnp.where(turn, second, first), jnp.where(turn, first, second)], axis=0))
     real = jnp.concatenate([r[:, 0:128] for r in rows], axis=1)
     imag = jnp.concatenate([r[:, 128:256] for r in rows], axis=1)
     sums = jnp.concatenate([r[:, 256:384] for r in rows], axis=1)
@@ -258,7 +300,6 @@
 
 
 VMEM = pl.BlockSpec(memory_space=pltpu.VMEM)
-SMEM = pl.BlockSpec(memory_space=pltpu.SMEM)
 
 
 def moved(value, where):
@@ -267,13 +308,8 @@
         for yh in range(2):
             for yl in range(2):
                 for r in range(8):
-                    target = where(z, yh, yl, r)
-                    if target is None:
-                        continue
-                    tz, th, tl, tr = target
-                    if not (0 <= tz < 8 and 0 <= tr < 8):
-                        continue
-                    pairs.append((((z * 2 + yh) * 2 + yl) * 8 + r, ((tz * 2 + th) * 2 + tl) * 8 + tr))
+                    tz, th, tl, tr = where(z, yh, yl, r)
+                    pairs.append((((z * 2 + yh) * 2 + yl) * 8 + r, ((tz % 8 * 2 + th) * 2 + tl) * 8 + tr % 8))
     return lax.ppermute(value, EVERY, pairs)
 
 
@@ -288,49 +324,61 @@
         return (((z + 1) ^ 1) - 1, h, l, r)
 
     def far_pair(z, h, l, r):
-        return (z - 2, h, l, r) if h == 0 else (z + 2, h, l, r)
-
+        return (z - 2, 1, l, r) if h == 0 else (z + 2, 0, l, r)
+
+    far = moved(tile, far_pair)
     swap_even = moved(tile, even_pair)
     swap_odd = moved(tile, odd_pair)
-    far = moved(tile, far_pair)
     other = moved(tile, lambda z, h, l, r: (z, 1 - h, l, r))
     odd_z = (position // 2) % 2 == 1
     up = jnp.where(odd_z, swap_odd, swap_even)
     down = jnp.where(odd_z, swap_even, swap_odd)
-
-    record = jax.ShapeDtypeStruct((3, 16, 128), F32)
+    look = jnp.asarray(look_table())
+
     own_fields, other_fields = pl.pallas_call(
         cross_kernel,
-        out_shape=(record, record),
-        in_specs=[VMEM] * 6,
+        out_shape=(jax.ShapeDtypeStruct((3, 16, 128), F32), jax.ShapeDtypeStruct((2, 16, 128), F32)),
+        in_specs=[VMEM] * 5,
         out_specs=(VMEM, VMEM),
-        scratch_shapes=[pltpu.VMEM((10, 4, 64, 128), F32), pltpu.VMEM((272, 512), F32)],
-        compiler_params=pltpu.CompilerParams(vmem_limit_bytes=24 * 2**20),
+        scratch_shapes=[pltpu.VMEM((8, 4, 64, 128), F32), pltpu.VMEM((224, 512), F32)],
+        compiler_params=pltpu.CompilerParams(vmem_limit_bytes=16 * 2**20),
         name="cross",
-    )(tile, other, up, down, far, jnp.asarray(look_table()))
-
-    swapped = moved(other_fields, lambda z, h, l, r: (z, 1 - h, l, r))
-    own_beside = moved(own_fields, lambda z, h, l, r: (z, h, 1 - l, r))
-    swapped_beside = moved(other_fields, lambda z, h, l, r: (z, 1 - h, 1 - l, r))
+    )(tile, other, up, down, look)
+    swapped = moved(other_fields, lambda z, h, l, r: (z, 1 - h, 1 - l, r))
     fields = pl.pallas_call(
         choose_kernel,
-        out_shape=jax.ShapeDtypeStruct((3, 32, 128), F32),
-        in_specs=[SMEM] + [VMEM] * 4,
+        out_shape=jax.ShapeDtypeStruct((3, 16, 128), F32),
+        in_specs=[VMEM] * 6,
         out_specs=VMEM,
-        compiler_params=pltpu.CompilerParams(vmem_limit_bytes=4 * 2**20),
+        scratch_shapes=[pltpu.VMEM((4, 4, 64, 128), F32), pltpu.VMEM((64, 512), F32)],
+        compiler_params=pltpu.CompilerParams(vmem_limit_bytes=16 * 2**20),
         name="choose",
-    )(pairs, own_fields, swapped, own_beside, swapped_beside)
-
-    core_halo = moved(fields, lambda z, h, l, r: (z, h, l, r ^ 1))
-    chip_halo = moved(fields, lambda z, h, l, r: (z, h, l, ((r + 1) ^ 1) - 1))
+    )(pairs, tile, far, own_fields, swapped, look)
+
+    def to_core(value):
+        return moved(value, lambda z, h, l, r: (z, h, l, r ^ 1))
+
+    def to_chip(value):
+        return moved(value, lambda z, h, l, r: (z, h, l, ((r + 1) ^ 1) - 1))
+
+    beside = moved(fields, lambda z, h, l, r: (z, h, 1 - l, r))
+    fields = jnp.concatenate([fields, beside], axis=0)
+    core_fields = to_core(fields)
+    chip_fields = to_chip(fields)
     filtered, coherence = pl.pallas_call(
         finish_kernel,
         out_shape=(jax.ShapeDtypeStruct((3, 2, 16, 32), F32), jax.ShapeDtypeStruct((3, 16, 32), F32)),
-        in_specs=[VMEM] * 10,
+        in_specs=[VMEM] * 11,
         out_specs=(VMEM, VMEM),
         compiler_params=pltpu.CompilerParams(vmem_limit_bytes=24 * 2**20),
         name="finish",
-    )(fields, core_halo, chip_halo, *[jnp.asarray(t) for t in tables()])
+    )(
+        pairs,
+        fields,
+        core_fields,
+        chip_fields,
+        *[jnp.asarray(t) for t in tables()],
+    )
     return (filtered[None], coherence[None])
 
 

time: 38 us -> 32.6 us (0.86)
  waiting for transfers between devices: 15.1 us -> 8.74 us
  starting transfers between devices: 18.6 us -> 19.8 us
    ppermute x9 -> x8, waiting for transfers between devices: 15.1 us -> 8.74 us  [moved(): return lax.ppermute(value, EVERY, pairs)]
    ppermute x9 -> x8, starting transfers between devices: 18.6 us -> 19.8 us  [moved(): return lax.ppermute(value, EVERY, pairs)]
  transfers between devices with their start and end apart: 9 -> 8, of which waited for: 5 -> 4; matrix products, arithmetic and copies ran while one was open for 0% -> 0% of each run, Pallas kernels for 0% -> 2%
where the time goes in v3:
time: 32.6 us; the launch traced here: 32.4 us
  starting transfers between devices  19.8 us (61%)
  waiting for transfers between devices  8.74 us (27%)
  Pallas kernels  2.97 us (9%)
  between operations  0.76 us (2%)
    ppermute x8, starting transfers between devices, moved(): return lax.ppermute(value, EVERY, pairs)  19.8 us
    ppermute x8, waiting for transfers between devices, moved(): return lax.ppermute(value, EVERY, pairs)  8.74 us
    pallas_call x1, Pallas kernels, per_device(): pl.pallas_call(finish_kernel, out_shape=(jax.ShapeDtypeStruct((3, 2, 16,...  1.97 us
  transfers between devices with their start and end apart: 8, of which 4 were waited for; matrix products, arithmetic and copies ran while one was open for 0% of the time, Pallas kernels for 2%

profile of v3, /device:TPU:1, one launch (start us, length us, event | category | flops | bytes accessed | tf_op | source)
XLA Modules:
  0.0 32.4 jit_solution(26116905520282838)
XLA Ops:
  0.6 2.6 %collective-permute-start.3 = (bf16[2,64,512]{2,1,0:T(8,128)(2,1)}, bf16[2,64,512]{2,1,0:T(8,128)(2,1)S(1)}, u32[]{:S(2)}, u32[]{:S(2)}) collective-permute-start(bf16[2,64,512]{2,1,0:T(8,128)(2,1)} %bitcast.3), channel_id=1, source_target_pairs={{0,32},{1,33},{2,34},{3,35},{4,36},{5,37},{6,38},{7,39},{8,40},{9,... | collective-permute-start | bytes 393224 | tf_op jit(solution)/shard_map/ppermute | solution.py:313
  3.2 4.7 %collective-permute-start.2 = (bf16[2,64,512]{2,1,0:T(8,128)(2,1)}, bf16[2,64,512]{2,1,0:T(8,128)(2,1)S(1)}, u32[]{:S(2)}, u32[]{:S(2)}) collective-permute-start(bf16[2,64,512]{2,1,0:T(8,128)(2,1)} %bitcast.4), channel_id=1, source_target_pairs={{0,224},{1,225},{2,226},{3,227},{4,228},{5,229},{6,230},{7,231},{8... | collective-permute-start | bytes 393224 | tf_op jit(solution)/shard_map/ppermute | solution.py:313
  7.8 2.9 %collective-permute-start.1 = (bf16[2,64,512]{2,1,0:T(8,128)(2,1)}, bf16[2,64,512]{2,1,0:T(8,128)(2,1)S(1)}, u32[]{:S(2)}, u32[]{:S(2)}) collective-permute-start(bf16[2,64,512]{2,1,0:T(8,128)(2,1)} %bitcast.5), channel_id=1, source_target_pairs={{0,16},{1,17},{2,18},{3,19},{4,20},{5,21},{6,22},{7,23},{8,24},{9,... | collective-permute-start | bytes 393224 | tf_op jit(solution)/shard_map/ppermute | solution.py:313
  10.8 0.9 %collective-permute-start = (bf16[2,64,512]{2,1,0:T(8,128)(2,1)}, bf16[2,64,512]{2,1,0:T(8,128)(2,1)S(1)}, u32[]{:S(2)}, u32[]{:S(2)}) collective-permute-start(bf16[2,64,512]{2,1,0:T(8,128)(2,1)} %bitcast.6), channel_id=1, source_target_pairs={{0,208},{1,209},{2,210},{3,211},{4,212},{5,213},{6,214},{7,215},{8... | collective-permute-start | bytes 393224 | tf_op jit(solution)/shard_map/ppermute | solution.py:313
  11.7 0.0 copy-start
  11.7 0.0 copy-start.1
  11.7 0.0 collective-permute-done.3
  11.7 0.0 collective-permute-done.2
  11.8 1.6 %collective-permute-done.1.other = bf16[2,64,512]{2,1,0:T(8,128)(2,1)S(1)} collective-permute-done((bf16[2,64,512]{2,1,0:T(8,128)(2,1)}, bf16[2,64,512]{2,1,0:T(8,128)(2,1)S(1)}, u32[]{:S(2)}, u32[]{:S(2)}) %collective-permute-start.1) | collective-permute-done | bytes 131104 | tf_op jit(solution)/shard_map/ppermute | solution.py:313
  13.4 0.0 copy-done
  13.4 0.0 copy-done.1
  13.4 0.0 copy-start.5
  13.4 0.0 copy-start.6
  13.4 0.7 %cross.1 = (f32[3,16,128]{2,1,0:T(8,128)S(1)}, f32[2,16,128]{2,1,0:T(8,128)S(1)}) custom-call(bf16[2,64,512]{2,1,0:T(8,128)(2,1)S(1)} %bitcast.7, bf16[2,64,512]{2,1,0:T(8,128)(2,1)S(1)} %collective-permute-done.1.other, bf16[2,64,512]{2,1,0:T(8,128)(2,1)S(1)} %get-tuple-element.11.up, bf16[2,64,512]{2,1,0:T(8,128)(2,1)S(1)} %get-tuple-element.10.down, ...), custom_call_target="tpu_custom_call" | custom-call | tf_op jit(solution)/shard_map/cross/pallas_call | solution.py:338
  14.1 0.0 copy-start.9
  14.1 2.8 %collective-permute-start.4 = (f32[2,16,128]{2,1,0:T(8,128)S(1)}, f32[2,16,128]{2,1,0:T(8,128)S(1)}, u32[]{:S(2)}, u32[]{:S(2)}) collective-permute-start(f32[2,16,128]{2,1,0:T(8,128)S(1)} %get-tuple-element.7), channel_id=1, source_target_pairs={{0,24},{1,25},{2,26},{3,27},{4,28},{5,29},{6,30},{7,31},{8,16},{9,... | collective-permute-start | bytes 49160 | tf_op jit(solution)/shard_map/ppermute | solution.py:313
  16.9 3.0 %collective-permute-done.far_tile = bf16[2,64,512]{2,1,0:T(8,128)(2,1)S(1)} collective-permute-done((bf16[2,64,512]{2,1,0:T(8,128)(2,1)}, bf16[2,64,512]{2,1,0:T(8,128)(2,1)S(1)}, u32[]{:S(2)}, u32[]{:S(2)}) %collective-permute-start) | collective-permute-done | bytes 131104 | tf_op jit(solution)/shard_map/ppermute | solution.py:313
  19.9 0.0 collective-permute-done.4.swapped
  19.9 0.0 copy-done.9
  19.9 0.0 copy-start.2
  19.9 0.0 copy-start.3
  19.9 0.0 copy-start.4
  20.0 0.3 %choose.1 = f32[3,16,128]{2,1,0:T(8,128)S(1)} custom-call(s32[1,3]{1,0:T(1,128)S(1)} %copy-done.9, bf16[2,64,512]{2,1,0:T(8,128)(2,1)S(1)} %bitcast.8, bf16[2,64,512]{2,1,0:T(8,128)(2,1)S(1)} %collective-permute-done.far_tile, f32[3,16,128]{2,1,0:T(8,128)S(1)} %get-tuple-element.6.own, f32[2,16,128]{2,1,0:T(8,128)S(1)} %collective-permute-done.4.swapped, ...), custom_call_target="tpu_custom_call" | custom-call | tf_op jit(solution)/shard_map/choose/pallas_call | solution.py:348
  20.3 0.0 copy-start.7
  20.3 0.0 copy-start.8
  20.3 0.5 %collective-permute-start.5 = (f32[3,16,128]{2,1,0:T(8,128)S(1)}, f32[3,16,128]{2,1,0:T(8,128)S(1)}, u32[]{:S(2)}, u32[]{:S(2)}) collective-permute-start(f32[3,16,128]{2,1,0:T(8,128)S(1)} %choose.1), channel_id=1, source_target_pairs={{0,8},{1,9},{2,10},{3,11},{4,12},{5,13},{6,14},{7,15},{8,0},{9,1},... | collective-permute-start | bytes 73736 | tf_op jit(solution)/shard_map/ppermute | solution.py:313
  20.8 2.3 %collective-permute-done.5 = f32[3,16,128]{2,1,0:T(8,128)S(1)} collective-permute-done((f32[3,16,128]{2,1,0:T(8,128)S(1)}, f32[3,16,128]{2,1,0:T(8,128)S(1)}, u32[]{:S(2)}, u32[]{:S(2)}) %collective-permute-start.5) | collective-permute-done | bytes 24608 | tf_op jit(solution)/shard_map/ppermute | solution.py:313
  23.1 5.5 %collective-permute-start.7 = (f32[6,16,128]{2,1,0:T(8,128)S(1)}, f32[6,16,128]{2,1,0:T(8,128)S(1)}, u32[]{:S(2)}, u32[]{:S(2)}) collective-permute-start(f32[6,16,128]{2,1,0:T(8,128)S(1)} %pad_maximum_fusion.fields), channel_id=1, source_target_pairs={{0,7},{1,2},{2,1},{3,4},{4,3},{5,6},{6,5},{7,0},{8,15},{9,10},{10,... | collective-permute-start | bytes 147464 | tf_op jit(solution)/shard_map/ppermute | solution.py:313
  28.6 0.0 collective-permute-start.6
  28.6 1.8 %collective-permute-done.7.chip_fields = f32[6,16,128]{2,1,0:T(8,128)S(1)} collective-permute-done((f32[6,16,128]{2,1,0:T(8,128)S(1)}, f32[6,16,128]{2,1,0:T(8,128)S(1)}, u32[]{:S(2)}, u32[]{:S(2)}) %collective-permute-start.7) | collective-permute-done | bytes 49184 | tf_op jit(solution)/shard_map/ppermute | solution.py:313
  30.3 0.0 collective-permute-done.6.core_fields
  30.3 0.0 copy-done.5
  30.3 0.0 copy-done.6
  30.4 0.0 copy-done.2
  30.4 0.0 copy-done.3
  30.4 0.0 copy-done.4
  30.4 0.0 copy-done.7
  30.4 0.0 copy-done.8
  30.4 2.0 %finish.1 = (f32[3,2,16,32]{3,2,1,0:T(8,128)}, f32[3,16,32]{2,1,0:T(8,128)}) custom-call(s32[1,3]{1,0:T(1,128)S(1)} %copy-done.9, f32[6,16,128]{2,1,0:T(8,128)S(1)} %pad_maximum_fusion.fields, f32[6,16,128]{2,1,0:T(8,128)S(1)} %collective-permute-done.6.core_fields, f32[6,16,128]{2,1,0:T(8,128)S(1)} %collective-permute-done.7.chip_fields, ...), custom_call_target="tpu_custom_call" | custom-call | tf_op jit(solution)/shard_map/finish/pallas_call | solution.py:368
  (2 shorter events, 0.0 us)
Async XLA Ops:
  0.6 11.1 %collective-permute-start.3 = (bf16[2,64,512]{2,1,0:T(8,128)(2,1)}, bf16[2,64,512]{2,1,0:T(8,128)(2,1)S(1)}, u32[]{:S(2)}, u32[]{:S(2)}) collective-permute-start(bf16[2,64,512]{2,1,0:T(8,128)(2,1)} %bitcast.3), channel_id=1, source_target_pairs={{0,32},{1,33},{2,34},{3,35},{4,36},{5,37},{6,38},{7,39},{8,40},{9,... | collective-permute-start | bytes 393224 | tf_op jit(solution)/shard_map/ppermute | solution.py:313
  3.2 8.5 %collective-permute-start.2 = (bf16[2,64,512]{2,1,0:T(8,128)(2,1)}, bf16[2,64,512]{2,1,0:T(8,128)(2,1)S(1)}, u32[]{:S(2)}, u32[]{:S(2)}) collective-permute-start(bf16[2,64,512]{2,1,0:T(8,128)(2,1)} %bitcast.4), channel_id=1, source_target_pairs={{0,224},{1,225},{2,226},{3,227},{4,228},{5,229},{6,230},{7,231},{8... | collective-permute-start | bytes 393224 | tf_op jit(solution)/shard_map/ppermute | solution.py:313
  7.8 5.6 %collective-permute-start.1 = (bf16[2,64,512]{2,1,0:T(8,128)(2,1)}, bf16[2,64,512]{2,1,0:T(8,128)(2,1)S(1)}, u32[]{:S(2)}, u32[]{:S(2)}) collective-permute-start(bf16[2,64,512]{2,1,0:T(8,128)(2,1)} %bitcast.5), channel_id=1, source_target_pairs={{0,16},{1,17},{2,18},{3,19},{4,20},{5,21},{6,22},{7,23},{8,24},{9,... | collective-permute-start | bytes 393224 | tf_op jit(solution)/shard_map/ppermute | solution.py:313
  10.8 9.2 %collective-permute-start = (bf16[2,64,512]{2,1,0:T(8,128)(2,1)}, bf16[2,64,512]{2,1,0:T(8,128)(2,1)S(1)}, u32[]{:S(2)}, u32[]{:S(2)}) collective-permute-start(bf16[2,64,512]{2,1,0:T(8,128)(2,1)} %bitcast.6), channel_id=1, source_target_pairs={{0,208},{1,209},{2,210},{3,211},{4,212},{5,213},{6,214},{7,215},{8... | collective-permute-start | bytes 393224 | tf_op jit(solution)/shard_map/ppermute | solution.py:313
  11.7 1.7 %copy-start = (bf16[1,2,64,512]{3,2,1,0:T(8,128)(2,1)S(1)}, bf16[1,2,64,512]{3,2,1,0:T(8,128)(2,1)}, u32[]{:S(2)}) copy-start(bf16[1,2,64,512]{3,2,1,0:T(8,128)(2,1)} %param.10) | copy-start | bytes 393220
  11.7 1.7 %copy-start.1 = (bf16[512,128]{1,0:T(8,128)(2,1)S(1)}, bf16[512,128]{1,0:T(8,128)(2,1)}, u32[]{:S(2)}) copy-start(bf16[512,128]{1,0:T(8,128)(2,1)} %constant.46.clone.look) | copy-start | bytes 393220
  13.4 16.9 %copy-start.5 = (bf16[256,256]{1,0:T(8,128)(2,1)S(1)}, bf16[256,256]{1,0:T(8,128)(2,1)}, u32[]{:S(2)}) copy-start(bf16[256,256]{1,0:T(8,128)(2,1)} %constant.52.clone.cb_high) | copy-start | bytes 393220
  13.4 16.9 %copy-start.6 = (bf16[2,128,192]{2,1,0:T(8,128)(2,1)S(1)}, bf16[2,128,192]{2,1,0:T(8,128)(2,1)}, u32[]{:S(2)}) copy-start(bf16[2,128,192]{2,1,0:T(8,128)(2,1)} %constant.49.clone.lf) | copy-start | bytes 294916
  14.1 5.9 %copy-start.9 = (s32[1,3]{1,0:T(1,128)S(1)}, s32[1,3]{1,0:T(1,128)}, u32[]{:S(2)}) copy-start(s32[1,3]{1,0:T(1,128)} %pairs.3) | copy-start | bytes 40
  14.1 5.8 %collective-permute-start.4 = (f32[2,16,128]{2,1,0:T(8,128)S(1)}, f32[2,16,128]{2,1,0:T(8,128)S(1)}, u32[]{:S(2)}, u32[]{:S(2)}) collective-permute-start(f32[2,16,128]{2,1,0:T(8,128)S(1)} %get-tuple-element.7), channel_id=1, source_target_pairs={{0,24},{1,25},{2,26},{3,27},{4,28},{5,29},{6,30},{7,31},{8,16},{9,... | collective-permute-start | bytes 49160 | tf_op jit(solution)/shard_map/ppermute | solution.py:313
  19.9 10.4 %copy-start.2 = (bf16[256,384]{1,0:T(8,128)(2,1)S(1)}, bf16[256,384]{1,0:T(8,128)(2,1)}, u32[]{:S(2)}) copy-start(bf16[256,384]{1,0:T(8,128)(2,1)} %constant.48.clone.cf_low) | copy-start | bytes 589828
  19.9 10.4 %copy-start.3 = (bf16[256,384]{1,0:T(8,128)(2,1)S(1)}, bf16[256,384]{1,0:T(8,128)(2,1)}, u32[]{:S(2)}) copy-start(bf16[256,384]{1,0:T(8,128)(2,1)} %constant.47.clone.cf_high) | copy-start | bytes 589828
  19.9 10.4 %copy-start.4 = (bf16[256,256]{1,0:T(8,128)(2,1)S(1)}, bf16[256,256]{1,0:T(8,128)(2,1)}, u32[]{:S(2)}) copy-start(bf16[256,256]{1,0:T(8,128)(2,1)} %constant.53.clone.cb_low) | copy-start | bytes 393220
  20.3 10.1 %copy-start.7 = (bf16[32,384]{1,0:T(8,128)(2,1)S(1)}, bf16[32,384]{1,0:T(8,128)(2,1)}, u32[]{:S(2)}) copy-start(bf16[32,384]{1,0:T(8,128)(2,1)} %constant.51.clone.lb) | copy-start | bytes 73732
  20.3 10.1 %copy-start.8 = (bf16[2,16,64]{2,1,0:T(8,128)(2,1)S(1)}, bf16[2,16,64]{2,1,0:T(8,128)(2,1)}, u32[]{:S(2)}) copy-start(bf16[2,16,64]{2,1,0:T(8,128)(2,1)} %constant.50.clone.window) | copy-start | bytes 12292
  20.3 2.8 %collective-permute-start.5 = (f32[3,16,128]{2,1,0:T(8,128)S(1)}, f32[3,16,128]{2,1,0:T(8,128)S(1)}, u32[]{:S(2)}, u32[]{:S(2)}) collective-permute-start(f32[3,16,128]{2,1,0:T(8,128)S(1)} %choose.1), channel_id=1, source_target_pairs={{0,8},{1,9},{2,10},{3,11},{4,12},{5,13},{6,14},{7,15},{8,0},{9,1},... | collective-permute-start | bytes 73736 | tf_op jit(solution)/shard_map/ppermute | solution.py:313
  23.1 7.2 %collective-permute-start.7 = (f32[6,16,128]{2,1,0:T(8,128)S(1)}, f32[6,16,128]{2,1,0:T(8,128)S(1)}, u32[]{:S(2)}, u32[]{:S(2)}) collective-permute-start(f32[6,16,128]{2,1,0:T(8,128)S(1)} %pad_maximum_fusion.fields), channel_id=1, source_target_pairs={{0,7},{1,2},{2,1},{3,4},{4,3},{5,6},{6,5},{7,0},{8,15},{9,10},{10,... | collective-permute-start | bytes 147464 | tf_op jit(solution)/shard_map/ppermute | solution.py:313
  28.6 1.8 %collective-permute-start.6 = (f32[6,16,128]{2,1,0:T(8,128)S(1)}, f32[6,16,128]{2,1,0:T(8,128)S(1)}, u32[]{:S(2)}, u32[]{:S(2)}) collective-permute-start(f32[6,16,128]{2,1,0:T(8,128)S(1)} %pad_maximum_fusion.fields), channel_id=1, source_target_pairs={{0,1},{1,0},{2,3},{3,2},{4,5},{5,4},{6,7},{7,6},{8,9},{9,8},{10,11... | collective-permute-start | bytes 147464 | tf_op jit(solution)/shard_map/ppermute | solution.py:313

commit v4 on v3

--- a/solution.py
+++ b/solution.py
@@ -309,7 +309,11 @@
             for yl in range(2):
                 for r in range(8):
                     tz, th, tl, tr = where(z, yh, yl, r)
-                    pairs.append((((z * 2 + yh) * 2 + yl) * 8 + r, ((tz % 8 * 2 + th) * 2 + tl) * 8 + tr % 8))
+                    if not 0 <= tz < 8:
+                        tz, th, tl, tr = z, yh, yl, r ^ 1
+                    if not 0 <= tr < 8:
+                        tz, th, tl, tr = z, yh, 1 - yl, r
+                    pairs.append((((z * 2 + yh) * 2 + yl) * 8 + r, ((tz * 2 + th) * 2 + tl) * 8 + tr))
     return lax.ppermute(value, EVERY, pairs)
 
 

time: 32.6 us -> 28.9 us (0.89)
  starting transfers between devices: 19.8 us -> 12.7 us
  waiting for transfers between devices: 8.74 us -> 12.3 us
    ppermute x8, starting transfers between devices: 19.8 us -> 12.7 us  [moved(): return lax.ppermute(value, EVERY, pairs)]
    ppermute x8, waiting for transfers between devices: 8.74 us -> 12.3 us  [moved(): return lax.ppermute(value, EVERY, pairs)]
where the time goes in v4:
time: 28.9 us; the launch traced here: 28.8 us
  starting transfers between devices  12.7 us (44%)
  waiting for transfers between devices  12.3 us (43%)
  Pallas kernels  2.96 us (10%)
  between operations  0.74 us (3%)
    ppermute x8, starting transfers between devices, moved(): return lax.ppermute(value, EVERY, pairs)  12.7 us
    ppermute x8, waiting for transfers between devices, moved(): return lax.ppermute(value, EVERY, pairs)  12.3 us
    pallas_call x1, Pallas kernels, per_device(): pl.pallas_call(finish_kernel, out_shape=(jax.ShapeDtypeStruct((3, 2, 16,...  1.96 us
    pallas_call x1, Pallas kernels, per_device(): pl.pallas_call(cross_kernel, out_shape=(jax.ShapeDtypeStruct((3, 16, 128)...  0.65 us
  transfers between devices with their start and end apart: 8, of which 4 were waited for; matrix products, arithmetic and copies ran while one was open for 0% of the time, Pallas kernels for 2%

profile of v4, /device:TPU:1, one launch (start us, length us, event | category | flops | bytes accessed | tf_op | source)
XLA Modules:
  0.0 28.8 jit_solution(6132976315587226653)
XLA Ops:
  0.6 2.6 %collective-permute-start.3 = (bf16[2,64,512]{2,1,0:T(8,128)(2,1)}, bf16[2,64,512]{2,1,0:T(8,128)(2,1)S(1)}, u32[]{:S(2)}, u32[]{:S(2)}) collective-permute-start(bf16[2,64,512]{2,1,0:T(8,128)(2,1)} %bitcast.3), channel_id=1, source_target_pairs={{0,32},{1,33},{2,34},{3,35},{4,36},{5,37},{6,38},{7,39},{8,40},{9,... | collective-permute-start | bytes 393224 | tf_op jit(solution)/shard_map/ppermute | solution.py:317
  3.2 1.0 %collective-permute-start.2 = (bf16[2,64,512]{2,1,0:T(8,128)(2,1)}, bf16[2,64,512]{2,1,0:T(8,128)(2,1)S(1)}, u32[]{:S(2)}, u32[]{:S(2)}) collective-permute-start(bf16[2,64,512]{2,1,0:T(8,128)(2,1)} %bitcast.4), channel_id=1, source_target_pairs={{0,1},{1,0},{2,3},{3,2},{4,5},{5,4},{6,7},{7,6},{8,9},{9,8},{10,11... | collective-permute-start | bytes 393224 | tf_op jit(solution)/shard_map/ppermute | solution.py:317
  4.1 2.9 %collective-permute-start.1 = (bf16[2,64,512]{2,1,0:T(8,128)(2,1)}, bf16[2,64,512]{2,1,0:T(8,128)(2,1)S(1)}, u32[]{:S(2)}, u32[]{:S(2)}) collective-permute-start(bf16[2,64,512]{2,1,0:T(8,128)(2,1)} %bitcast.5), channel_id=1, source_target_pairs={{0,16},{1,17},{2,18},{3,19},{4,20},{5,21},{6,22},{7,23},{8,24},{9,... | collective-permute-start | bytes 393224 | tf_op jit(solution)/shard_map/ppermute | solution.py:317
  7.1 0.3 collective-permute-start
  7.3 0.0 copy-start
  7.3 0.0 copy-start.1
  7.3 0.0 collective-permute-done.3
  7.3 0.0 collective-permute-done.2
  7.4 5.6 %collective-permute-done.1.other = bf16[2,64,512]{2,1,0:T(8,128)(2,1)S(1)} collective-permute-done((bf16[2,64,512]{2,1,0:T(8,128)(2,1)}, bf16[2,64,512]{2,1,0:T(8,128)(2,1)S(1)}, u32[]{:S(2)}, u32[]{:S(2)}) %collective-permute-start.1) | collective-permute-done | bytes 131104 | tf_op jit(solution)/shard_map/ppermute | solution.py:317
  13.0 0.0 copy-done
  13.0 0.0 copy-done.1
  13.0 0.0 copy-start.5
  13.0 0.0 copy-start.6
  13.0 0.7 %cross.1 = (f32[3,16,128]{2,1,0:T(8,128)S(1)}, f32[2,16,128]{2,1,0:T(8,128)S(1)}) custom-call(bf16[2,64,512]{2,1,0:T(8,128)(2,1)S(1)} %bitcast.7, bf16[2,64,512]{2,1,0:T(8,128)(2,1)S(1)} %collective-permute-done.1.other, bf16[2,64,512]{2,1,0:T(8,128)(2,1)S(1)} %get-tuple-element.11.up, bf16[2,64,512]{2,1,0:T(8,128)(2,1)S(1)} %get-tuple-element.10.down, ...), custom_call_target="tpu_custom_call" | custom-call | tf_op jit(solution)/shard_map/cross/pallas_call | solution.py:342
  13.6 0.0 copy-start.9
  13.6 0.8 %collective-permute-start.4 = (f32[2,16,128]{2,1,0:T(8,128)S(1)}, f32[2,16,128]{2,1,0:T(8,128)S(1)}, u32[]{:S(2)}, u32[]{:S(2)}) collective-permute-start(f32[2,16,128]{2,1,0:T(8,128)S(1)} %get-tuple-element.7), channel_id=1, source_target_pairs={{0,24},{1,25},{2,26},{3,27},{4,28},{5,29},{6,30},{7,31},{8,16},{9,... | collective-permute-start | bytes 49160 | tf_op jit(solution)/shard_map/ppermute | solution.py:317
  14.5 0.0 collective-permute-done.far_tile
  14.5 3.0 %collective-permute-done.4.swapped = f32[2,16,128]{2,1,0:T(8,128)S(1)} collective-permute-done((f32[2,16,128]{2,1,0:T(8,128)S(1)}, f32[2,16,128]{2,1,0:T(8,128)S(1)}, u32[]{:S(2)}, u32[]{:S(2)}) %collective-permute-start.4) | collective-permute-done | bytes 16416 | tf_op jit(solution)/shard_map/ppermute | solution.py:317
  17.5 0.0 copy-done.9
  17.5 0.0 copy-start.2
  17.5 0.0 copy-start.3
  17.5 0.0 copy-start.4
  17.5 0.3 %choose.1 = f32[3,16,128]{2,1,0:T(8,128)S(1)} custom-call(s32[1,3]{1,0:T(1,128)S(1)} %copy-done.9, bf16[2,64,512]{2,1,0:T(8,128)(2,1)S(1)} %bitcast.8, bf16[2,64,512]{2,1,0:T(8,128)(2,1)S(1)} %collective-permute-done.far_tile, f32[3,16,128]{2,1,0:T(8,128)S(1)} %get-tuple-element.6.own, f32[2,16,128]{2,1,0:T(8,128)S(1)} %collective-permute-done.4.swapped, ...), custom_call_target="tpu_custom_call" | custom-call | tf_op jit(solution)/shard_map/choose/pallas_call | solution.py:352
  17.9 0.0 copy-start.7
  17.9 0.0 copy-start.8
  17.9 0.8 %collective-permute-start.5 = (f32[3,16,128]{2,1,0:T(8,128)S(1)}, f32[3,16,128]{2,1,0:T(8,128)S(1)}, u32[]{:S(2)}, u32[]{:S(2)}) collective-permute-start(f32[3,16,128]{2,1,0:T(8,128)S(1)} %choose.1), channel_id=1, source_target_pairs={{0,8},{1,9},{2,10},{3,11},{4,12},{5,13},{6,14},{7,15},{8,0},{9,1},... | collective-permute-start | bytes 73736 | tf_op jit(solution)/shard_map/ppermute | solution.py:317
  18.8 1.9 %collective-permute-done.5 = f32[3,16,128]{2,1,0:T(8,128)S(1)} collective-permute-done((f32[3,16,128]{2,1,0:T(8,128)S(1)}, f32[3,16,128]{2,1,0:T(8,128)S(1)}, u32[]{:S(2)}, u32[]{:S(2)}) %collective-permute-start.5) | collective-permute-done | bytes 24608 | tf_op jit(solution)/shard_map/ppermute | solution.py:317
  20.7 4.3 %collective-permute-start.7 = (f32[6,16,128]{2,1,0:T(8,128)S(1)}, f32[6,16,128]{2,1,0:T(8,128)S(1)}, u32[]{:S(2)}, u32[]{:S(2)}) collective-permute-start(f32[6,16,128]{2,1,0:T(8,128)S(1)} %pad_maximum_fusion.fields), channel_id=1, source_target_pairs={{0,8},{1,2},{2,1},{3,4},{4,3},{5,6},{6,5},{7,15},{8,0},{9,10},{10,... | collective-permute-start | bytes 147464 | tf_op jit(solution)/shard_map/ppermute | solution.py:317
  25.0 0.0 collective-permute-start.6
  25.0 1.8 %collective-permute-done.7.chip_fields = f32[6,16,128]{2,1,0:T(8,128)S(1)} collective-permute-done((f32[6,16,128]{2,1,0:T(8,128)S(1)}, f32[6,16,128]{2,1,0:T(8,128)S(1)}, u32[]{:S(2)}, u32[]{:S(2)}) %collective-permute-start.7) | collective-permute-done | bytes 49184 | tf_op jit(solution)/shard_map/ppermute | solution.py:317
  26.8 0.0 collective-permute-done.6.core_fields
  26.8 0.0 copy-done.5
  26.8 0.0 copy-done.6
  26.8 0.0 copy-done.2
  26.8 0.0 copy-done.3
  26.8 0.0 copy-done.4
  26.8 0.0 copy-done.7
  26.8 0.0 copy-done.8
  26.9 2.0 %finish.1 = (f32[3,2,16,32]{3,2,1,0:T(8,128)}, f32[3,16,32]{2,1,0:T(8,128)}) custom-call(s32[1,3]{1,0:T(1,128)S(1)} %copy-done.9, f32[6,16,128]{2,1,0:T(8,128)S(1)} %pad_maximum_fusion.fields, f32[6,16,128]{2,1,0:T(8,128)S(1)} %collective-permute-done.6.core_fields, f32[6,16,128]{2,1,0:T(8,128)S(1)} %collective-permute-done.7.chip_fields, ...), custom_call_target="tpu_custom_call" | custom-call | tf_op jit(solution)/shard_map/finish/pallas_call | solution.py:372
  (2 shorter events, 0.0 us)
Async XLA Ops:
  0.6 6.7 %collective-permute-start.3 = (bf16[2,64,512]{2,1,0:T(8,128)(2,1)}, bf16[2,64,512]{2,1,0:T(8,128)(2,1)S(1)}, u32[]{:S(2)}, u32[]{:S(2)}) collective-permute-start(bf16[2,64,512]{2,1,0:T(8,128)(2,1)} %bitcast.3), channel_id=1, source_target_pairs={{0,32},{1,33},{2,34},{3,35},{4,36},{5,37},{6,38},{7,39},{8,40},{9,... | collective-permute-start | bytes 393224 | tf_op jit(solution)/shard_map/ppermute | solution.py:317
  3.2 4.2 %collective-permute-start.2 = (bf16[2,64,512]{2,1,0:T(8,128)(2,1)}, bf16[2,64,512]{2,1,0:T(8,128)(2,1)S(1)}, u32[]{:S(2)}, u32[]{:S(2)}) collective-permute-start(bf16[2,64,512]{2,1,0:T(8,128)(2,1)} %bitcast.4), channel_id=1, source_target_pairs={{0,1},{1,0},{2,3},{3,2},{4,5},{5,4},{6,7},{7,6},{8,9},{9,8},{10,11... | collective-permute-start | bytes 393224 | tf_op jit(solution)/shard_map/ppermute | solution.py:317
  4.1 8.8 %collective-permute-start.1 = (bf16[2,64,512]{2,1,0:T(8,128)(2,1)}, bf16[2,64,512]{2,1,0:T(8,128)(2,1)S(1)}, u32[]{:S(2)}, u32[]{:S(2)}) collective-permute-start(bf16[2,64,512]{2,1,0:T(8,128)(2,1)} %bitcast.5), channel_id=1, source_target_pairs={{0,16},{1,17},{2,18},{3,19},{4,20},{5,21},{6,22},{7,23},{8,24},{9,... | collective-permute-start | bytes 393224 | tf_op jit(solution)/shard_map/ppermute | solution.py:317
  7.1 7.4 %collective-permute-start = (bf16[2,64,512]{2,1,0:T(8,128)(2,1)}, bf16[2,64,512]{2,1,0:T(8,128)(2,1)S(1)}, u32[]{:S(2)}, u32[]{:S(2)}) collective-permute-start(bf16[2,64,512]{2,1,0:T(8,128)(2,1)} %bitcast.6), channel_id=1, source_target_pairs={{0,1},{1,0},{2,3},{3,2},{4,5},{5,4},{6,7},{7,6},{8,9},{9,8},{10,11... | collective-permute-start | bytes 393224 | tf_op jit(solution)/shard_map/ppermute | solution.py:317
  7.3 5.6 %copy-start = (bf16[1,2,64,512]{3,2,1,0:T(8,128)(2,1)S(1)}, bf16[1,2,64,512]{3,2,1,0:T(8,128)(2,1)}, u32[]{:S(2)}) copy-start(bf16[1,2,64,512]{3,2,1,0:T(8,128)(2,1)} %param.10) | copy-start | bytes 393220
  7.3 5.6 %copy-start.1 = (bf16[512,128]{1,0:T(8,128)(2,1)S(1)}, bf16[512,128]{1,0:T(8,128)(2,1)}, u32[]{:S(2)}) copy-start(bf16[512,128]{1,0:T(8,128)(2,1)} %constant.46.clone.look) | copy-start | bytes 393220
  13.0 13.8 %copy-start.5 = (bf16[256,256]{1,0:T(8,128)(2,1)S(1)}, bf16[256,256]{1,0:T(8,128)(2,1)}, u32[]{:S(2)}) copy-start(bf16[256,256]{1,0:T(8,128)(2,1)} %constant.52.clone.cb_high) | copy-start | bytes 393220
  13.0 13.8 %copy-start.6 = (bf16[2,128,192]{2,1,0:T(8,128)(2,1)S(1)}, bf16[2,128,192]{2,1,0:T(8,128)(2,1)}, u32[]{:S(2)}) copy-start(bf16[2,128,192]{2,1,0:T(8,128)(2,1)} %constant.49.clone.lf) | copy-start | bytes 294916
  13.6 3.9 %copy-start.9 = (s32[1,3]{1,0:T(1,128)S(1)}, s32[1,3]{1,0:T(1,128)}, u32[]{:S(2)}) copy-start(s32[1,3]{1,0:T(1,128)} %pairs.3) | copy-start | bytes 40
  13.6 3.9 %collective-permute-start.4 = (f32[2,16,128]{2,1,0:T(8,128)S(1)}, f32[2,16,128]{2,1,0:T(8,128)S(1)}, u32[]{:S(2)}, u32[]{:S(2)}) collective-permute-start(f32[2,16,128]{2,1,0:T(8,128)S(1)} %get-tuple-element.7), channel_id=1, source_target_pairs={{0,24},{1,25},{2,26},{3,27},{4,28},{5,29},{6,30},{7,31},{8,16},{9,... | collective-permute-start | bytes 49160 | tf_op jit(solution)/shard_map/ppermute | solution.py:317
  17.5 9.3 %copy-start.2 = (bf16[256,384]{1,0:T(8,128)(2,1)S(1)}, bf16[256,384]{1,0:T(8,128)(2,1)}, u32[]{:S(2)}) copy-start(bf16[256,384]{1,0:T(8,128)(2,1)} %constant.48.clone.cf_low) | copy-start | bytes 589828
  17.5 9.3 %copy-start.3 = (bf16[256,384]{1,0:T(8,128)(2,1)S(1)}, bf16[256,384]{1,0:T(8,128)(2,1)}, u32[]{:S(2)}) copy-start(bf16[256,384]{1,0:T(8,128)(2,1)} %constant.47.clone.cf_high) | copy-start | bytes 589828
  17.5 9.3 %copy-start.4 = (bf16[256,256]{1,0:T(8,128)(2,1)S(1)}, bf16[256,256]{1,0:T(8,128)(2,1)}, u32[]{:S(2)}) copy-start(bf16[256,256]{1,0:T(8,128)(2,1)} %constant.53.clone.cb_low) | copy-start | bytes 393220
  17.9 8.9 %copy-start.7 = (bf16[32,384]{1,0:T(8,128)(2,1)S(1)}, bf16[32,384]{1,0:T(8,128)(2,1)}, u32[]{:S(2)}) copy-start(bf16[32,384]{1,0:T(8,128)(2,1)} %constant.51.clone.lb) | copy-start | bytes 73732
  17.9 8.9 %copy-start.8 = (bf16[2,16,64]{2,1,0:T(8,128)(2,1)S(1)}, bf16[2,16,64]{2,1,0:T(8,128)(2,1)}, u32[]{:S(2)}) copy-start(bf16[2,16,64]{2,1,0:T(8,128)(2,1)} %constant.50.clone.window) | copy-start | bytes 12292
  17.9 2.8 %collective-permute-start.5 = (f32[3,16,128]{2,1,0:T(8,128)S(1)}, f32[3,16,128]{2,1,0:T(8,128)S(1)}, u32[]{:S(2)}, u32[]{:S(2)}) collective-permute-start(f32[3,16,128]{2,1,0:T(8,128)S(1)} %choose.1), channel_id=1, source_target_pairs={{0,8},{1,9},{2,10},{3,11},{4,12},{5,13},{6,14},{7,15},{8,0},{9,1},... | collective-permute-start | bytes 73736 | tf_op jit(solution)/shard_map/ppermute | solution.py:317
  20.7 6.1 %collective-permute-start.7 = (f32[6,16,128]{2,1,0:T(8,128)S(1)}, f32[6,16,128]{2,1,0:T(8,128)S(1)}, u32[]{:S(2)}, u32[]{:S(2)}) collective-permute-start(f32[6,16,128]{2,1,0:T(8,128)S(1)} %pad_maximum_fusion.fields), channel_id=1, source_target_pairs={{0,8},{1,2},{2,1},{3,4},{4,3},{5,6},{6,5},{7,15},{8,0},{9,10},{10,... | collective-permute-start | bytes 147464 | tf_op jit(solution)/shard_map/ppermute | solution.py:317
  25.0 1.8 %collective-permute-start.6 = (f32[6,16,128]{2,1,0:T(8,128)S(1)}, f32[6,16,128]{2,1,0:T(8,128)S(1)}, u32[]{:S(2)}, u32[]{:S(2)}) collective-permute-start(f32[6,16,128]{2,1,0:T(8,128)S(1)} %pad_maximum_fusion.fields), channel_id=1, source_target_pairs={{0,1},{1,0},{2,3},{3,2},{4,5},{5,4},{6,7},{7,6},{8,9},{9,8},{10,11... | collective-permute-start | bytes 147464 | tf_op jit(solution)/shard_map/ppermute | solution.py:317

commit v5 on v4

--- a/solution.py
+++ b/solution.py
@@ -265,8 +265,8 @@
             block = block + turned(block, 1) + turned(block, -1)
             smoothed.append(block / 9.0)
     largest = jnp.concatenate([jnp.max(b, axis=0, keepdims=True) for b in smoothed] + [jnp.zeros((2, 128), F32)], axis=0)
-    for by in (1, 2, 4, 8, 16):
-        largest = jnp.maximum(largest, turned(largest, by))
+    groups = [jnp.max(jnp.where(lane // 32 == g, largest, 0.0), axis=1, keepdims=True) for g in range(3)]
+    largest = jnp.where(lane < 32, groups[0], jnp.where(lane < 64, groups[1], groups[2]))
     scale = 1.0 / (jnp.sqrt(largest) + 1e-06)
     weights = [jnp.sqrt(b) * scale[i : i + 1] for i, b in enumerate(smoothed)]
     weights = jnp.concatenate(

time: 28.9 us -> 28.6 us (0.990)
  no operation moved by 1% of the time
where the time goes in v5:
time: 28.6 us
  starting transfers between devices  12.7 us (44%)
  waiting for transfers between devices  12.3 us (43%)
  Pallas kernels  2.7 us (9%)
  between operations  0.74 us (3%)
    ppermute x8, starting transfers between devices, moved(): return lax.ppermute(value, EVERY, pairs)  12.7 us
    ppermute x8, waiting for transfers between devices, moved(): return lax.ppermute(value, EVERY, pairs)  12.3 us
    pallas_call x1, Pallas kernels, per_device(): pl.pallas_call(finish_kernel, out_shape=(jax.ShapeDtypeStruct((3, 2, 16,...  1.7 us
    pallas_call x1, Pallas kernels, per_device(): pl.pallas_call(cross_kernel, out_shape=(jax.ShapeDtypeStruct((3, 16, 128)...  0.65 us
  transfers between devices with their start and end apart: 8, of which 4 were waited for; matrix products, arithmetic and copies ran while one was open for 0% of the time, Pallas kernels for 2%

profile of v5, /device:TPU:1, one launch (start us, length us, event | category | flops | bytes accessed | tf_op | source)
XLA Modules:
  0.0 28.6 jit_solution(15443973945200151741)
XLA Ops:
  0.6 2.6 %collective-permute-start.3 = (bf16[2,64,512]{2,1,0:T(8,128)(2,1)}, bf16[2,64,512]{2,1,0:T(8,128)(2,1)S(1)}, u32[]{:S(2)}, u32[]{:S(2)}) collective-permute-start(bf16[2,64,512]{2,1,0:T(8,128)(2,1)} %bitcast.3), channel_id=1, source_target_pairs={{0,32},{1,33},{2,34},{3,35},{4,36},{5,37},{6,38},{7,39},{8,40},{9,... | collective-permute-start | bytes 393224 | tf_op jit(solution)/shard_map/ppermute | solution.py:317
  3.2 1.0 %collective-permute-start.2 = (bf16[2,64,512]{2,1,0:T(8,128)(2,1)}, bf16[2,64,512]{2,1,0:T(8,128)(2,1)S(1)}, u32[]{:S(2)}, u32[]{:S(2)}) collective-permute-start(bf16[2,64,512]{2,1,0:T(8,128)(2,1)} %bitcast.4), channel_id=1, source_target_pairs={{0,1},{1,0},{2,3},{3,2},{4,5},{5,4},{6,7},{7,6},{8,9},{9,8},{10,11... | collective-permute-start | bytes 393224 | tf_op jit(solution)/shard_map/ppermute | solution.py:317
  4.1 2.9 %collective-permute-start.1 = (bf16[2,64,512]{2,1,0:T(8,128)(2,1)}, bf16[2,64,512]{2,1,0:T(8,128)(2,1)S(1)}, u32[]{:S(2)}, u32[]{:S(2)}) collective-permute-start(bf16[2,64,512]{2,1,0:T(8,128)(2,1)} %bitcast.5), channel_id=1, source_target_pairs={{0,16},{1,17},{2,18},{3,19},{4,20},{5,21},{6,22},{7,23},{8,24},{9,... | collective-permute-start | bytes 393224 | tf_op jit(solution)/shard_map/ppermute | solution.py:317
  7.1 0.3 collective-permute-start
  7.3 0.0 copy-start
  7.3 0.0 copy-start.1
  7.3 0.0 collective-permute-done.3
  7.3 0.0 collective-permute-done.2
  7.4 5.6 %collective-permute-done.1.other = bf16[2,64,512]{2,1,0:T(8,128)(2,1)S(1)} collective-permute-done((bf16[2,64,512]{2,1,0:T(8,128)(2,1)}, bf16[2,64,512]{2,1,0:T(8,128)(2,1)S(1)}, u32[]{:S(2)}, u32[]{:S(2)}) %collective-permute-start.1) | collective-permute-done | bytes 131104 | tf_op jit(solution)/shard_map/ppermute | solution.py:317
  13.0 0.0 copy-done
  13.0 0.0 copy-done.1
  13.0 0.0 copy-start.5
  13.0 0.0 copy-start.6
  13.0 0.7 %cross.1 = (f32[3,16,128]{2,1,0:T(8,128)S(1)}, f32[2,16,128]{2,1,0:T(8,128)S(1)}) custom-call(bf16[2,64,512]{2,1,0:T(8,128)(2,1)S(1)} %bitcast.7, bf16[2,64,512]{2,1,0:T(8,128)(2,1)S(1)} %collective-permute-done.1.other, bf16[2,64,512]{2,1,0:T(8,128)(2,1)S(1)} %get-tuple-element.11.up, bf16[2,64,512]{2,1,0:T(8,128)(2,1)S(1)} %get-tuple-element.10.down, ...), custom_call_target="tpu_custom_call" | custom-call | tf_op jit(solution)/shard_map/cross/pallas_call | solution.py:342
  13.6 0.0 copy-start.9
  13.6 0.8 %collective-permute-start.4 = (f32[2,16,128]{2,1,0:T(8,128)S(1)}, f32[2,16,128]{2,1,0:T(8,128)S(1)}, u32[]{:S(2)}, u32[]{:S(2)}) collective-permute-start(f32[2,16,128]{2,1,0:T(8,128)S(1)} %get-tuple-element.7), channel_id=1, source_target_pairs={{0,24},{1,25},{2,26},{3,27},{4,28},{5,29},{6,30},{7,31},{8,16},{9,... | collective-permute-start | bytes 49160 | tf_op jit(solution)/shard_map/ppermute | solution.py:317
  14.5 0.0 collective-permute-done.far_tile
  14.5 3.0 %collective-permute-done.4.swapped = f32[2,16,128]{2,1,0:T(8,128)S(1)} collective-permute-done((f32[2,16,128]{2,1,0:T(8,128)S(1)}, f32[2,16,128]{2,1,0:T(8,128)S(1)}, u32[]{:S(2)}, u32[]{:S(2)}) %collective-permute-start.4) | collective-permute-done | bytes 16416 | tf_op jit(solution)/shard_map/ppermute | solution.py:317
  17.5 0.0 copy-done.9
  17.5 0.0 copy-start.2
  17.5 0.0 copy-start.3
  17.5 0.0 copy-start.4
  17.5 0.3 %choose.1 = f32[3,16,128]{2,1,0:T(8,128)S(1)} custom-call(s32[1,3]{1,0:T(1,128)S(1)} %copy-done.9, bf16[2,64,512]{2,1,0:T(8,128)(2,1)S(1)} %bitcast.8, bf16[2,64,512]{2,1,0:T(8,128)(2,1)S(1)} %collective-permute-done.far_tile, f32[3,16,128]{2,1,0:T(8,128)S(1)} %get-tuple-element.6.own, f32[2,16,128]{2,1,0:T(8,128)S(1)} %collective-permute-done.4.swapped, ...), custom_call_target="tpu_custom_call" | custom-call | tf_op jit(solution)/shard_map/choose/pallas_call | solution.py:352
  17.9 0.0 copy-start.7
  17.9 0.0 copy-start.8
  17.9 0.8 %collective-permute-start.5 = (f32[3,16,128]{2,1,0:T(8,128)S(1)}, f32[3,16,128]{2,1,0:T(8,128)S(1)}, u32[]{:S(2)}, u32[]{:S(2)}) collective-permute-start(f32[3,16,128]{2,1,0:T(8,128)S(1)} %choose.1), channel_id=1, source_target_pairs={{0,8},{1,9},{2,10},{3,11},{4,12},{5,13},{6,14},{7,15},{8,0},{9,1},... | collective-permute-start | bytes 73736 | tf_op jit(solution)/shard_map/ppermute | solution.py:317
  18.8 1.9 %collective-permute-done.5 = f32[3,16,128]{2,1,0:T(8,128)S(1)} collective-permute-done((f32[3,16,128]{2,1,0:T(8,128)S(1)}, f32[3,16,128]{2,1,0:T(8,128)S(1)}, u32[]{:S(2)}, u32[]{:S(2)}) %collective-permute-start.5) | collective-permute-done | bytes 24608 | tf_op jit(solution)/shard_map/ppermute | solution.py:317
  20.7 4.3 %collective-permute-start.7 = (f32[6,16,128]{2,1,0:T(8,128)S(1)}, f32[6,16,128]{2,1,0:T(8,128)S(1)}, u32[]{:S(2)}, u32[]{:S(2)}) collective-permute-start(f32[6,16,128]{2,1,0:T(8,128)S(1)} %pad_maximum_fusion.fields), channel_id=1, source_target_pairs={{0,8},{1,2},{2,1},{3,4},{4,3},{5,6},{6,5},{7,15},{8,0},{9,10},{10,... | collective-permute-start | bytes 147464 | tf_op jit(solution)/shard_map/ppermute | solution.py:317
  25.0 0.0 collective-permute-start.6
  25.0 1.8 %collective-permute-done.7.chip_fields = f32[6,16,128]{2,1,0:T(8,128)S(1)} collective-permute-done((f32[6,16,128]{2,1,0:T(8,128)S(1)}, f32[6,16,128]{2,1,0:T(8,128)S(1)}, u32[]{:S(2)}, u32[]{:S(2)}) %collective-permute-start.7) | collective-permute-done | bytes 49184 | tf_op jit(solution)/shard_map/ppermute | solution.py:317
  26.8 0.0 collective-permute-done.6.core_fields
  26.8 0.0 copy-done.5
  26.8 0.0 copy-done.6
  26.8 0.0 copy-done.2
  26.8 0.0 copy-done.3
  26.8 0.0 copy-done.4
  26.8 0.0 copy-done.7
  26.8 0.0 copy-done.8
  26.9 1.7 %finish.1 = (f32[3,2,16,32]{3,2,1,0:T(8,128)}, f32[3,16,32]{2,1,0:T(8,128)}) custom-call(s32[1,3]{1,0:T(1,128)S(1)} %copy-done.9, f32[6,16,128]{2,1,0:T(8,128)S(1)} %pad_maximum_fusion.fields, f32[6,16,128]{2,1,0:T(8,128)S(1)} %collective-permute-done.6.core_fields, f32[6,16,128]{2,1,0:T(8,128)S(1)} %collective-permute-done.7.chip_fields, ...), custom_call_target="tpu_custom_call" | custom-call | tf_op jit(solution)/shard_map/finish/pallas_call | solution.py:372
  (2 shorter events, 0.0 us)
Async XLA Ops:
  0.6 6.7 %collective-permute-start.3 = (bf16[2,64,512]{2,1,0:T(8,128)(2,1)}, bf16[2,64,512]{2,1,0:T(8,128)(2,1)S(1)}, u32[]{:S(2)}, u32[]{:S(2)}) collective-permute-start(bf16[2,64,512]{2,1,0:T(8,128)(2,1)} %bitcast.3), channel_id=1, source_target_pairs={{0,32},{1,33},{2,34},{3,35},{4,36},{5,37},{6,38},{7,39},{8,40},{9,... | collective-permute-start | bytes 393224 | tf_op jit(solution)/shard_map/ppermute | solution.py:317
  3.2 4.2 %collective-permute-start.2 = (bf16[2,64,512]{2,1,0:T(8,128)(2,1)}, bf16[2,64,512]{2,1,0:T(8,128)(2,1)S(1)}, u32[]{:S(2)}, u32[]{:S(2)}) collective-permute-start(bf16[2,64,512]{2,1,0:T(8,128)(2,1)} %bitcast.4), channel_id=1, source_target_pairs={{0,1},{1,0},{2,3},{3,2},{4,5},{5,4},{6,7},{7,6},{8,9},{9,8},{10,11... | collective-permute-start | bytes 393224 | tf_op jit(solution)/shard_map/ppermute | solution.py:317
  4.1 8.8 %collective-permute-start.1 = (bf16[2,64,512]{2,1,0:T(8,128)(2,1)}, bf16[2,64,512]{2,1,0:T(8,128)(2,1)S(1)}, u32[]{:S(2)}, u32[]{:S(2)}) collective-permute-start(bf16[2,64,512]{2,1,0:T(8,128)(2,1)} %bitcast.5), channel_id=1, source_target_pairs={{0,16},{1,17},{2,18},{3,19},{4,20},{5,21},{6,22},{7,23},{8,24},{9,... | collective-permute-start | bytes 393224 | tf_op jit(solution)/shard_map/ppermute | solution.py:317
  7.1 7.4 %collective-permute-start = (bf16[2,64,512]{2,1,0:T(8,128)(2,1)}, bf16[2,64,512]{2,1,0:T(8,128)(2,1)S(1)}, u32[]{:S(2)}, u32[]{:S(2)}) collective-permute-start(bf16[2,64,512]{2,1,0:T(8,128)(2,1)} %bitcast.6), channel_id=1, source_target_pairs={{0,1},{1,0},{2,3},{3,2},{4,5},{5,4},{6,7},{7,6},{8,9},{9,8},{10,11... | collective-permute-start | bytes 393224 | tf_op jit(solution)/shard_map/ppermute | solution.py:317
  7.3 5.6 %copy-start = (bf16[1,2,64,512]{3,2,1,0:T(8,128)(2,1)S(1)}, bf16[1,2,64,512]{3,2,1,0:T(8,128)(2,1)}, u32[]{:S(2)}) copy-start(bf16[1,2,64,512]{3,2,1,0:T(8,128)(2,1)} %param.10) | copy-start | bytes 393220
  7.3 5.6 %copy-start.1 = (bf16[512,128]{1,0:T(8,128)(2,1)S(1)}, bf16[512,128]{1,0:T(8,128)(2,1)}, u32[]{:S(2)}) copy-start(bf16[512,128]{1,0:T(8,128)(2,1)} %constant.46.clone.look) | copy-start | bytes 393220
  13.0 13.8 %copy-start.5 = (bf16[256,256]{1,0:T(8,128)(2,1)S(1)}, bf16[256,256]{1,0:T(8,128)(2,1)}, u32[]{:S(2)}) copy-start(bf16[256,256]{1,0:T(8,128)(2,1)} %constant.52.clone.cb_high) | copy-start | bytes 393220
  13.0 13.8 %copy-start.6 = (bf16[2,128,192]{2,1,0:T(8,128)(2,1)S(1)}, bf16[2,128,192]{2,1,0:T(8,128)(2,1)}, u32[]{:S(2)}) copy-start(bf16[2,128,192]{2,1,0:T(8,128)(2,1)} %constant.49.clone.lf) | copy-start | bytes 294916
  13.6 3.9 %copy-start.9 = (s32[1,3]{1,0:T(1,128)S(1)}, s32[1,3]{1,0:T(1,128)}, u32[]{:S(2)}) copy-start(s32[1,3]{1,0:T(1,128)} %pairs.3) | copy-start | bytes 40
  13.6 3.9 %collective-permute-start.4 = (f32[2,16,128]{2,1,0:T(8,128)S(1)}, f32[2,16,128]{2,1,0:T(8,128)S(1)}, u32[]{:S(2)}, u32[]{:S(2)}) collective-permute-start(f32[2,16,128]{2,1,0:T(8,128)S(1)} %get-tuple-element.7), channel_id=1, source_target_pairs={{0,24},{1,25},{2,26},{3,27},{4,28},{5,29},{6,30},{7,31},{8,16},{9,... | collective-permute-start | bytes 49160 | tf_op jit(solution)/shard_map/ppermute | solution.py:317
  17.5 9.3 %copy-start.2 = (bf16[256,384]{1,0:T(8,128)(2,1)S(1)}, bf16[256,384]{1,0:T(8,128)(2,1)}, u32[]{:S(2)}) copy-start(bf16[256,384]{1,0:T(8,128)(2,1)} %constant.48.clone.cf_low) | copy-start | bytes 589828
  17.5 9.3 %copy-start.3 = (bf16[256,384]{1,0:T(8,128)(2,1)S(1)}, bf16[256,384]{1,0:T(8,128)(2,1)}, u32[]{:S(2)}) copy-start(bf16[256,384]{1,0:T(8,128)(2,1)} %constant.47.clone.cf_high) | copy-start | bytes 589828
  17.5 9.3 %copy-start.4 = (bf16[256,256]{1,0:T(8,128)(2,1)S(1)}, bf16[256,256]{1,0:T(8,128)(2,1)}, u32[]{:S(2)}) copy-start(bf16[256,256]{1,0:T(8,128)(2,1)} %constant.53.clone.cb_low) | copy-start | bytes 393220
  17.9 8.9 %copy-start.7 = (bf16[32,384]{1,0:T(8,128)(2,1)S(1)}, bf16[32,384]{1,0:T(8,128)(2,1)}, u32[]{:S(2)}) copy-start(bf16[32,384]{1,0:T(8,128)(2,1)} %constant.51.clone.lb) | copy-start | bytes 73732
  17.9 8.9 %copy-start.8 = (bf16[2,16,64]{2,1,0:T(8,128)(2,1)S(1)}, bf16[2,16,64]{2,1,0:T(8,128)(2,1)}, u32[]{:S(2)}) copy-start(bf16[2,16,64]{2,1,0:T(8,128)(2,1)} %constant.50.clone.window) | copy-start | bytes 12292
  17.9 2.8 %collective-permute-start.5 = (f32[3,16,128]{2,1,0:T(8,128)S(1)}, f32[3,16,128]{2,1,0:T(8,128)S(1)}, u32[]{:S(2)}, u32[]{:S(2)}) collective-permute-start(f32[3,16,128]{2,1,0:T(8,128)S(1)} %choose.1), channel_id=1, source_target_pairs={{0,8},{1,9},{2,10},{3,11},{4,12},{5,13},{6,14},{7,15},{8,0},{9,1},... | collective-permute-start | bytes 73736 | tf_op jit(solution)/shard_map/ppermute | solution.py:317
  20.7 6.1 %collective-permute-start.7 = (f32[6,16,128]{2,1,0:T(8,128)S(1)}, f32[6,16,128]{2,1,0:T(8,128)S(1)}, u32[]{:S(2)}, u32[]{:S(2)}) collective-permute-start(f32[6,16,128]{2,1,0:T(8,128)S(1)} %pad_maximum_fusion.fields), channel_id=1, source_target_pairs={{0,8},{1,2},{2,1},{3,4},{4,3},{5,6},{6,5},{7,15},{8,0},{9,10},{10,... | collective-permute-start | bytes 147464 | tf_op jit(solution)/shard_map/ppermute | solution.py:317
  25.0 1.8 %collective-permute-start.6 = (f32[6,16,128]{2,1,0:T(8,128)S(1)}, f32[6,16,128]{2,1,0:T(8,128)S(1)}, u32[]{:S(2)}, u32[]{:S(2)}) collective-permute-start(f32[6,16,128]{2,1,0:T(8,128)S(1)} %pad_maximum_fusion.fields), channel_id=1, source_target_pairs={{0,1},{1,0},{2,3},{3,2},{4,5},{5,4},{6,7},{7,6},{8,9},{9,8},{10,11... | collective-permute-start | bytes 147464 | tf_op jit(solution)/shard_map/ppermute | solution.py:317

commit v6 on v5

--- a/solution.py
+++ b/solution.py
@@ -139,11 +139,11 @@
                 wide[index * 2 + part, chunk] = tile[part, :, at].astype(F32)
 
 
-def looked_records(couples, count, wide, sums, look):
-    number = len(couples)
+def looked_fields(couples, powers, count, wide, sums, look):
+    number = 2 * len(couples) + len(powers)
     for chunk in range(4):
         at = slice(chunk * 128, chunk * 128 + 128)
-        totals = [None] * (2 * number + count)
+        totals = [None] * number
         for line in range(4):
             rows = pl.ds(line, 16, stride=4)
             real = [wide[2 * i, chunk, rows, :] for i in range(count)]
@@ -153,7 +153,7 @@
                 terms.append(real[u] * real[v] + imag[u] * imag[v])
             for u, v in couples:
                 terms.append(imag[u] * real[v] - real[u] * imag[v])
-            for u in range(count):
+            for u in powers:
                 terms.append(real[u] * real[u] + imag[u] * imag[u])
             totals = [t if s is None else s + t for s, t in zip(totals, terms)]
         for index, total in enumerate(totals):
@@ -161,22 +161,31 @@
     high, low = halves(sums[...])
     table = look[...]
     looked = dot(high, table) + dot(low, table)
-    fields = [looked[i * 16 : i * 16 + 16] for i in range(2 * number + count)]
-    power = fields[2 * number :]
-    records = []
-    for index, (u, v) in enumerate(couples):
-        crossed = fields[index] + pltpu.roll(fields[number + index], 32, 1)
-        records.append(crossed + pltpu.roll(power[v], 64, 1) + pltpu.roll(power[u], 96, 1))
-    return records
-
-
-def cross_kernel(own, other, up, down, look, own_out, other_out, wide, sums):
+    return [looked[i * 16 : i * 16 + 16] for i in range(number)]
+
+
+def record(real, imag, far_power, own_power):
+    crossed = real + pltpu.roll(imag, 32, 1)
+    return crossed + pltpu.roll(far_power, 64, 1) + pltpu.roll(own_power, 96, 1)
+
+
+def cross_kernel(own, other, up, down, look, own_out, other_out, powers, wide, sums):
     widened((own, other, up, down), wide)
-    records = looked_records(((0, 1), (0, 2), (0, 3), (1, 2), (1, 3)), 4, wide, sums, look)
+    couples = ((0, 1), (0, 2), (0, 3), (1, 2), (1, 3))
+    fields = looked_fields(couples, (0, 1, 2, 3), 4, wide, sums, look)
+    power = fields[10:14]
+    records = [record(fields[i], fields[5 + i], power[v], power[u]) for i, (u, v) in enumerate(couples)]
     for index in range(3):
         own_out[index] = records[index]
     for index in range(2):
         other_out[index] = records[3 + index]
+    powers[...] = power[0]
+
+
+def far_kernel(own, far, powers, look, out, wide, sums):
+    widened((own, far), wide)
+    fields = looked_fields(((0, 1),), (1,), 2, wide, sums, look)
+    out[...] = record(fields[0], fields[1], fields[2], powers[...])
 
 
 def offsets_of(pairs):
@@ -190,27 +199,28 @@
     return (flipped == 3) | (flipped == -1)
 
 
-def choose_kernel(pairs, own_tile, far_tile, own, swapped, look, out, wide, sums):
+def choose_kernel(pairs, own, far, swapped, out):
     odd, flipped = offsets_of(pairs)
     up = jnp.where(odd, -2, 2)
-    widened((own_tile, far_tile), wide)
-    (far,) = looked_records(((0, 1),), 2, wide, sums, look)
     third = jnp.where(odd, swapped[1], swapped[0])
     first = jnp.where(odd, swapped[0], swapped[1])
     for slot in range(3):
         at = flipped[:, slot : slot + 1]
-        record = jnp.where(at == 1, own[0], far)
-        record = jnp.where(at == up, own[1], record)
-        record = jnp.where(at == -up, own[2], record)
-        record = jnp.where(at == 3, third, record)
-        out[slot] = jnp.where(at == -1, first, record)
+        chosen = jnp.where(at == 1, own[0], far[...])
+        chosen = jnp.where(at == up, own[1], chosen)
+        chosen = jnp.where(at == -up, own[2], chosen)
+        chosen = jnp.where(at == 3, third, chosen)
+        out[slot] = jnp.where(at == -1, first, chosen)
 
 
 def finish_kernel(
     pairs,
     fields,
-    core_fields,
-    chip_fields,
+    chip_beside,
+    chip,
+    core_beside,
+    beside,
+    core,
     cf_high,
     cf_low,
     lf,
@@ -222,16 +232,18 @@
     coherence,
 ):
     side = lax.axis_index("az")
-    column = lax.axis_index("rg")
-    core = column % 2
     lane = lax.broadcasted_iota(jnp.int32, (1, 128), 1)
     place = lane % 32
-    from_core = (place >= 16) == (core == 1)
+    column = lax.axis_index("rg")
+    from_core = (place >= 16) == (column % 2 == 1)
     inside = (column > 0) & (column < 7)
 
-    from_chip = jnp.where(inside, chip_fields[...].reshape(96, 128), 0.0)
-    halo = jnp.where(from_core, core_fields[...].reshape(96, 128), from_chip)
-    values = jnp.concatenate([fields[...].reshape(96, 128), halo], axis=1)
+    def both(near, away):
+        return jnp.concatenate([near[...].reshape(48, 128), away[...].reshape(48, 128)], axis=0)
+
+    from_chip = jnp.where(inside, both(chip, chip_beside), 0.0)
+    halo = jnp.where(from_core, both(core, core_beside), from_chip)
+    values = jnp.concatenate([both(fields, beside), halo], axis=1)
     high, low = halves(values)
     table = cf_high[...]
     mixed = dot(high, table) + dot(low, table) + dot(high, cf_low[...])
@@ -334,53 +346,61 @@
     swap_even = moved(tile, even_pair)
     swap_odd = moved(tile, odd_pair)
     other = moved(tile, lambda z, h, l, r: (z, 1 - h, l, r))
-    odd_z = (position // 2) % 2 == 1
-    up = jnp.where(odd_z, swap_odd, swap_even)
-    down = jnp.where(odd_z, swap_even, swap_odd)
+    even_z = (position // 2) % 2 == 0
+    up = jnp.where(even_z, swap_even, swap_odd)
+    down = jnp.where(even_z, swap_odd, swap_even)
     look = jnp.asarray(look_table())
 
-    own_fields, other_fields = pl.pallas_call(
-        cross_kernel,
-        out_shape=(jax.ShapeDtypeStruct((3, 16, 128), F32), jax.ShapeDtypeStruct((2, 16, 128), F32)),
-        in_specs=[VMEM] * 5,
-        out_specs=(VMEM, VMEM),
-        scratch_shapes=[pltpu.VMEM((8, 4, 64, 128), F32), pltpu.VMEM((224, 512), F32)],
-        compiler_params=pltpu.CompilerParams(vmem_limit_bytes=16 * 2**20),
-        name="cross",
-    )(tile, other, up, down, look)
+    def looked(kernel, name, shapes, tiles, fields, operands):
+        return pl.pallas_call(
+            kernel,
+            out_shape=[jax.ShapeDtypeStruct(shape, F32) for shape in shapes],
+            in_specs=[VMEM] * len(operands),
+            out_specs=[VMEM] * len(shapes),
+            scratch_shapes=[pltpu.VMEM((2 * tiles, 4, 64, 128), F32), pltpu.VMEM((16 * fields, 512), F32)],
+            compiler_params=pltpu.CompilerParams(vmem_limit_bytes=16 * 2**20),
+            name=name,
+        )(*operands)
+
+    own_fields, other_fields, powers = looked(
+        cross_kernel, "cross", ((3, 16, 128), (2, 16, 128), (16, 128)), 4, 14, (tile, other, up, down, look)
+    )
     swapped = moved(other_fields, lambda z, h, l, r: (z, 1 - h, 1 - l, r))
+    (away,) = looked(far_kernel, "far", ((16, 128),), 2, 3, (tile, far, powers, look))
     fields = pl.pallas_call(
         choose_kernel,
         out_shape=jax.ShapeDtypeStruct((3, 16, 128), F32),
-        in_specs=[VMEM] * 6,
+        in_specs=[VMEM] * 4,
         out_specs=VMEM,
-        scratch_shapes=[pltpu.VMEM((4, 4, 64, 128), F32), pltpu.VMEM((64, 512), F32)],
-        compiler_params=pltpu.CompilerParams(vmem_limit_bytes=16 * 2**20),
+        compiler_params=pltpu.CompilerParams(vmem_limit_bytes=4 * 2**20),
         name="choose",
-    )(pairs, tile, far, own_fields, swapped, look)
-
-    def to_core(value):
-        return moved(value, lambda z, h, l, r: (z, h, l, r ^ 1))
-
-    def to_chip(value):
-        return moved(value, lambda z, h, l, r: (z, h, l, ((r + 1) ^ 1) - 1))
-
-    beside = moved(fields, lambda z, h, l, r: (z, h, 1 - l, r))
-    fields = jnp.concatenate([fields, beside], axis=0)
-    core_fields = to_core(fields)
-    chip_fields = to_chip(fields)
+    )(pairs, own_fields, away, swapped)
+
+    def chip_of(r):
+        return ((r + 1) ^ 1) - 1
+
+    halos = dict(
+        beside=moved(fields, lambda z, h, l, r: (z, h, 1 - l, r)),
+        core=moved(fields, lambda z, h, l, r: (z, h, l, r ^ 1)),
+        chip=moved(fields, lambda z, h, l, r: (z, h, l, chip_of(r))),
+        core_beside=moved(fields, lambda z, h, l, r: (z, h, 1 - l, r ^ 1)),
+        chip_beside=moved(fields, lambda z, h, l, r: (z, h, 1 - l, chip_of(r))),
+    )
     filtered, coherence = pl.pallas_call(
         finish_kernel,
         out_shape=(jax.ShapeDtypeStruct((3, 2, 16, 32), F32), jax.ShapeDtypeStruct((3, 16, 32), F32)),
-        in_specs=[VMEM] * 11,
+        in_specs=[VMEM] * 14,
         out_specs=(VMEM, VMEM),
         compiler_params=pltpu.CompilerParams(vmem_limit_bytes=24 * 2**20),
         name="finish",
     )(
         pairs,
         fields,
-        core_fields,
-        chip_fields,
+        halos["chip_beside"],
+        halos["chip"],
+        halos["core_beside"],
+        halos["beside"],
+        halos["core"],
         *[jnp.asarray(t) for t in tables()],
     )
     return (filtered[None], coherence[None])

time: 28.6 us -> 27.1 us (0.948); the launches traced: 28.6 us -> 26.6 us
  waiting for transfers between devices: 12.3 us -> 9.94 us
  starting transfers between devices: 12.7 us -> 13.1 us
    ppermute x8 -> x10, waiting for transfers between devices: 12.3 us -> 9.94 us  [moved(): return lax.ppermute(value, EVERY, pairs)]
    ppermute x8 -> x10, starting transfers between devices: 12.7 us -> 13.1 us  [moved(): return lax.ppermute(value, EVERY, pairs)]
    pallas_call x1 -> x2, Pallas kernels: 0.65 us -> 0.96 us  [looked(): pl.pallas_call(kernel, out_shape=[jax.ShapeDtypeStruct(shape, F32) for sh...]
  transfers between devices with their start and end apart: 8 -> 10, of which waited for: 4 -> 5; matrix products, arithmetic and copies ran while one was open for 0% -> 0% of each run, Pallas kernels for 2% -> 4%
where the time goes in v6:
time: 27.1 us; the launch traced here: 26.6 us
  starting transfers between devices  13.1 us (48%)
  waiting for transfers between devices  9.94 us (37%)
  Pallas kernels  2.76 us (10%)
  between operations  0.73 us (3%)
    ppermute x10, starting transfers between devices, moved(): return lax.ppermute(value, EVERY, pairs)  13.1 us
    ppermute x10, waiting for transfers between devices, moved(): return lax.ppermute(value, EVERY, pairs)  9.94 us
    pallas_call x1, Pallas kernels, per_device(): pl.pallas_call(finish_kernel, out_shape=(jax.ShapeDtypeStruct((3, 2, 16,...  1.7 us
    pallas_call x2, Pallas kernels, looked(): pl.pallas_call(kernel, out_shape=[jax.ShapeDtypeStruct(shape, F32) for sh...  0.96 us
  transfers between devices with their start and end apart: 10, of which 5 were waited for; matrix products, arithmetic and copies ran while one was open for 0% of the time, Pallas kernels for 4%

profile of v6, /device:TPU:1, one launch (start us, length us, event | category | flops | bytes accessed | tf_op | source)
XLA Modules:
  0.0 26.6 jit_solution(2780405499352015217)
XLA Ops:
  0.6 2.6 %collective-permute-start.1 = (bf16[2,64,512]{2,1,0:T(8,128)(2,1)}, bf16[2,64,512]{2,1,0:T(8,128)(2,1)S(1)}, u32[]{:S(2)}, u32[]{:S(2)}) collective-permute-start(bf16[2,64,512]{2,1,0:T(8,128)(2,1)} %bitcast.3), channel_id=1, source_target_pairs={{0,32},{1,33},{2,34},{3,35},{4,36},{5,37},{6,38},{7,39},{8,40},{9,... | collective-permute-start | bytes 393224 | tf_op jit(solution)/shard_map/ppermute | solution.py:329
  3.2 1.0 %collective-permute-start.2 = (bf16[2,64,512]{2,1,0:T(8,128)(2,1)}, bf16[2,64,512]{2,1,0:T(8,128)(2,1)S(1)}, u32[]{:S(2)}, u32[]{:S(2)}) collective-permute-start(bf16[2,64,512]{2,1,0:T(8,128)(2,1)} %bitcast.4), channel_id=1, source_target_pairs={{0,1},{1,0},{2,3},{3,2},{4,5},{5,4},{6,7},{7,6},{8,9},{9,8},{10,11... | collective-permute-start | bytes 393224 | tf_op jit(solution)/shard_map/ppermute | solution.py:329
  4.1 2.9 %collective-permute-start = (bf16[2,64,512]{2,1,0:T(8,128)(2,1)}, bf16[2,64,512]{2,1,0:T(8,128)(2,1)S(1)}, u32[]{:S(2)}, u32[]{:S(2)}) collective-permute-start(bf16[2,64,512]{2,1,0:T(8,128)(2,1)} %bitcast.5), channel_id=1, source_target_pairs={{0,16},{1,17},{2,18},{3,19},{4,20},{5,21},{6,22},{7,23},{8,24},{9,... | collective-permute-start | bytes 393224 | tf_op jit(solution)/shard_map/ppermute | solution.py:329
  7.1 0.3 %collective-permute-start.3 = (bf16[2,64,512]{2,1,0:T(8,128)(2,1)}, bf16[2,64,512]{2,1,0:T(8,128)(2,1)S(1)}, u32[]{:S(2)}, u32[]{:S(2)}) collective-permute-start(bf16[2,64,512]{2,1,0:T(8,128)(2,1)} %bitcast.6), channel_id=1, source_target_pairs={{0,1},{1,0},{2,3},{3,2},{4,5},{5,4},{6,7},{7,6},{8,9},{9,8},{10,11... | collective-permute-start | bytes 393224 | tf_op jit(solution)/shard_map/ppermute | solution.py:329
  7.3 0.0 copy-start
  7.3 0.0 copy-start.1
  7.3 0.0 collective-permute-done.1
  7.3 0.0 collective-permute-done.2
  7.4 5.6 %collective-permute-done.other = bf16[2,64,512]{2,1,0:T(8,128)(2,1)S(1)} collective-permute-done((bf16[2,64,512]{2,1,0:T(8,128)(2,1)}, bf16[2,64,512]{2,1,0:T(8,128)(2,1)S(1)}, u32[]{:S(2)}, u32[]{:S(2)}) %collective-permute-start) | collective-permute-done | bytes 131104 | tf_op jit(solution)/shard_map/ppermute | solution.py:329
  13.0 0.0 copy-done
  13.0 0.0 copy-done.1
  13.0 0.0 copy-start.4
  13.0 0.0 copy-start.5
  13.0 0.0 copy-start.6
  13.0 0.7 %cross.1 = (f32[3,16,128]{2,1,0:T(8,128)S(1)}, f32[2,16,128]{2,1,0:T(8,128)S(1)}, f32[16,128]{1,0:T(8,128)S(1)}) custom-call(bf16[2,64,512]{2,1,0:T(8,128)(2,1)S(1)} %bitcast.7, bf16[2,64,512]{2,1,0:T(8,128)(2,1)S(1)} %collective-permute-done.other, bf16[2,64,512]{2,1,0:T(8,128)(2,1)S(1)} %get-tuple-element.13.up, ...), custom_call_target="tpu_custom_call" | custom-call | tf_op jit(solution)/shard_map/cross/pallas_call | solution.py:355
  13.6 0.8 %collective-permute-start.4 = (f32[2,16,128]{2,1,0:T(8,128)S(1)}, f32[2,16,128]{2,1,0:T(8,128)S(1)}, u32[]{:S(2)}, u32[]{:S(2)}) collective-permute-start(f32[2,16,128]{2,1,0:T(8,128)S(1)} %get-tuple-element.9), channel_id=1, source_target_pairs={{0,24},{1,25},{2,26},{3,27},{4,28},{5,29},{6,30},{7,31},{8,16},{9,... | collective-permute-start | bytes 49160 | tf_op jit(solution)/shard_map/ppermute | solution.py:329
  14.5 0.0 collective-permute-done.3.far
  14.5 0.0 copy-start.2
  14.5 0.0 copy-start.3
  14.5 0.3 %far.1 = f32[16,128]{1,0:T(8,128)S(1)} custom-call(bf16[2,64,512]{2,1,0:T(8,128)(2,1)S(1)} %bitcast.8, bf16[2,64,512]{2,1,0:T(8,128)(2,1)S(1)} %collective-permute-done.3.far, f32[16,128]{1,0:T(8,128)S(1)} %get-tuple-element.8.powers, bf16[512,128]{1,0:T(8,128)(2,1)S(1)} %copy-done.1), custom_call_target="tpu_custom_call" | custom-call | tf_op jit(solution)/shard_map/far/pallas_call | solution.py:355
  14.8 0.0 copy-start.9
  14.8 2.7 %collective-permute-done.4.swapped = f32[2,16,128]{2,1,0:T(8,128)S(1)} collective-permute-done((f32[2,16,128]{2,1,0:T(8,128)S(1)}, f32[2,16,128]{2,1,0:T(8,128)S(1)}, u32[]{:S(2)}, u32[]{:S(2)}) %collective-permute-start.4) | collective-permute-done | bytes 16416 | tf_op jit(solution)/shard_map/ppermute | solution.py:329
  17.5 0.0 copy-done.9
  17.5 0.0 copy-start.7
  17.5 0.0 copy-start.8
  17.5 0.1 choose.1.fields
  17.6 3.3 %collective-permute-start.5 = (f32[3,16,128]{2,1,0:T(8,128)S(1)}, f32[3,16,128]{2,1,0:T(8,128)S(1)}, u32[]{:S(2)}, u32[]{:S(2)}) collective-permute-start(f32[3,16,128]{2,1,0:T(8,128)S(1)} %choose.1.fields), channel_id=1, source_target_pairs={{0,8},{1,10},{2,9},{3,12},{4,11},{5,14},{6,13},{7,15},{8,0},{9,2},... | collective-permute-start | bytes 73736 | tf_op jit(solution)/shard_map/ppermute | solution.py:329
  21.0 0.1 collective-permute-start.6
  21.0 1.0 %collective-permute-start.7 = (f32[3,16,128]{2,1,0:T(8,128)S(1)}, f32[3,16,128]{2,1,0:T(8,128)S(1)}, u32[]{:S(2)}, u32[]{:S(2)}) collective-permute-start(f32[3,16,128]{2,1,0:T(8,128)S(1)} %choose.1.fields), channel_id=1, source_target_pairs={{0,9},{1,8},{2,11},{3,10},{4,13},{5,12},{6,15},{7,14},{8,1},{9,0},... | collective-permute-start | bytes 73736 | tf_op jit(solution)/shard_map/ppermute | solution.py:329
  22.1 1.1 %collective-permute-start.8 = (f32[3,16,128]{2,1,0:T(8,128)S(1)}, f32[3,16,128]{2,1,0:T(8,128)S(1)}, u32[]{:S(2)}, u32[]{:S(2)}) collective-permute-start(f32[3,16,128]{2,1,0:T(8,128)S(1)} %choose.1.fields), channel_id=1, source_target_pairs={{0,8},{1,9},{2,10},{3,11},{4,12},{5,13},{6,14},{7,15},{8,0},{9,1},... | collective-permute-start | bytes 73736 | tf_op jit(solution)/shard_map/ppermute | solution.py:329
  23.2 0.0 collective-permute-start.9
  23.2 0.0 collective-permute-done.5.chip_beside
  23.2 1.3 %collective-permute-done.6.chip = f32[3,16,128]{2,1,0:T(8,128)S(1)} collective-permute-done((f32[3,16,128]{2,1,0:T(8,128)S(1)}, f32[3,16,128]{2,1,0:T(8,128)S(1)}, u32[]{:S(2)}, u32[]{:S(2)}) %collective-permute-start.6) | collective-permute-done | bytes 24608 | tf_op jit(solution)/shard_map/ppermute | solution.py:329
  24.5 0.2 collective-permute-done.7.core_beside
  24.7 0.1 collective-permute-done.8.beside
  24.8 0.0 collective-permute-done.9.core
  24.8 0.0 copy-done.4
  24.8 0.0 copy-done.5
  24.8 0.0 copy-done.6
  24.8 0.0 copy-done.2
  24.8 0.0 copy-done.3
  24.9 0.0 copy-done.7
  24.9 0.0 copy-done.8
  24.9 1.7 %finish.1 = (f32[3,2,16,32]{3,2,1,0:T(8,128)}, f32[3,16,32]{2,1,0:T(8,128)}) custom-call(s32[1,3]{1,0:T(1,128)S(1)} %copy-done.9, f32[3,16,128]{2,1,0:T(8,128)S(1)} %choose.1.fields, f32[3,16,128]{2,1,0:T(8,128)S(1)} %collective-permute-done.5.chip_beside, f32[3,16,128]{2,1,0:T(8,128)S(1)} %collective-permute-done.6.chip, ...), custom_call_target="tpu_custom_call" | custom-call | tf_op jit(solution)/shard_map/finish/pallas_call | solution.py:389
  (1 shorter events, 0.0 us)
Async XLA Ops:
  0.6 6.7 %collective-permute-start.1 = (bf16[2,64,512]{2,1,0:T(8,128)(2,1)}, bf16[2,64,512]{2,1,0:T(8,128)(2,1)S(1)}, u32[]{:S(2)}, u32[]{:S(2)}) collective-permute-start(bf16[2,64,512]{2,1,0:T(8,128)(2,1)} %bitcast.3), channel_id=1, source_target_pairs={{0,32},{1,33},{2,34},{3,35},{4,36},{5,37},{6,38},{7,39},{8,40},{9,... | collective-permute-start | bytes 393224 | tf_op jit(solution)/shard_map/ppermute | solution.py:329
  3.2 4.2 %collective-permute-start.2 = (bf16[2,64,512]{2,1,0:T(8,128)(2,1)}, bf16[2,64,512]{2,1,0:T(8,128)(2,1)S(1)}, u32[]{:S(2)}, u32[]{:S(2)}) collective-permute-start(bf16[2,64,512]{2,1,0:T(8,128)(2,1)} %bitcast.4), channel_id=1, source_target_pairs={{0,1},{1,0},{2,3},{3,2},{4,5},{5,4},{6,7},{7,6},{8,9},{9,8},{10,11... | collective-permute-start | bytes 393224 | tf_op jit(solution)/shard_map/ppermute | solution.py:329
  4.1 8.8 %collective-permute-start = (bf16[2,64,512]{2,1,0:T(8,128)(2,1)}, bf16[2,64,512]{2,1,0:T(8,128)(2,1)S(1)}, u32[]{:S(2)}, u32[]{:S(2)}) collective-permute-start(bf16[2,64,512]{2,1,0:T(8,128)(2,1)} %bitcast.5), channel_id=1, source_target_pairs={{0,16},{1,17},{2,18},{3,19},{4,20},{5,21},{6,22},{7,23},{8,24},{9,... | collective-permute-start | bytes 393224 | tf_op jit(solution)/shard_map/ppermute | solution.py:329
  7.1 7.4 %collective-permute-start.3 = (bf16[2,64,512]{2,1,0:T(8,128)(2,1)}, bf16[2,64,512]{2,1,0:T(8,128)(2,1)S(1)}, u32[]{:S(2)}, u32[]{:S(2)}) collective-permute-start(bf16[2,64,512]{2,1,0:T(8,128)(2,1)} %bitcast.6), channel_id=1, source_target_pairs={{0,1},{1,0},{2,3},{3,2},{4,5},{5,4},{6,7},{7,6},{8,9},{9,8},{10,11... | collective-permute-start | bytes 393224 | tf_op jit(solution)/shard_map/ppermute | solution.py:329
  7.3 5.6 %copy-start = (bf16[1,2,64,512]{3,2,1,0:T(8,128)(2,1)S(1)}, bf16[1,2,64,512]{3,2,1,0:T(8,128)(2,1)}, u32[]{:S(2)}) copy-start(bf16[1,2,64,512]{3,2,1,0:T(8,128)(2,1)} %param.10) | copy-start | bytes 393220
  7.3 5.6 %copy-start.1 = (bf16[512,128]{1,0:T(8,128)(2,1)S(1)}, bf16[512,128]{1,0:T(8,128)(2,1)}, u32[]{:S(2)}) copy-start(bf16[512,128]{1,0:T(8,128)(2,1)} %constant.46.clone.look) | copy-start | bytes 393220
  13.0 11.9 %copy-start.4 = (bf16[2,128,192]{2,1,0:T(8,128)(2,1)S(1)}, bf16[2,128,192]{2,1,0:T(8,128)(2,1)}, u32[]{:S(2)}) copy-start(bf16[2,128,192]{2,1,0:T(8,128)(2,1)} %constant.49.clone.lf) | copy-start | bytes 294916
  13.0 11.9 %copy-start.5 = (bf16[256,256]{1,0:T(8,128)(2,1)S(1)}, bf16[256,256]{1,0:T(8,128)(2,1)}, u32[]{:S(2)}) copy-start(bf16[256,256]{1,0:T(8,128)(2,1)} %constant.52.clone.cb_high) | copy-start | bytes 393220
  13.0 11.9 %copy-start.6 = (bf16[256,256]{1,0:T(8,128)(2,1)S(1)}, bf16[256,256]{1,0:T(8,128)(2,1)}, u32[]{:S(2)}) copy-start(bf16[256,256]{1,0:T(8,128)(2,1)} %constant.53.clone.cb_low) | copy-start | bytes 393220
  13.6 3.9 %collective-permute-start.4 = (f32[2,16,128]{2,1,0:T(8,128)S(1)}, f32[2,16,128]{2,1,0:T(8,128)S(1)}, u32[]{:S(2)}, u32[]{:S(2)}) collective-permute-start(f32[2,16,128]{2,1,0:T(8,128)S(1)} %get-tuple-element.9), channel_id=1, source_target_pairs={{0,24},{1,25},{2,26},{3,27},{4,28},{5,29},{6,30},{7,31},{8,16},{9,... | collective-permute-start | bytes 49160 | tf_op jit(solution)/shard_map/ppermute | solution.py:329
  14.5 10.3 %copy-start.2 = (bf16[256,384]{1,0:T(8,128)(2,1)S(1)}, bf16[256,384]{1,0:T(8,128)(2,1)}, u32[]{:S(2)}) copy-start(bf16[256,384]{1,0:T(8,128)(2,1)} %constant.47.clone.cf_high) | copy-start | bytes 589828
  14.5 10.4 %copy-start.3 = (bf16[256,384]{1,0:T(8,128)(2,1)S(1)}, bf16[256,384]{1,0:T(8,128)(2,1)}, u32[]{:S(2)}) copy-start(bf16[256,384]{1,0:T(8,128)(2,1)} %constant.48.clone.cf_low) | copy-start | bytes 589828
  14.8 2.7 %copy-start.9 = (s32[1,3]{1,0:T(1,128)S(1)}, s32[1,3]{1,0:T(1,128)}, u32[]{:S(2)}) copy-start(s32[1,3]{1,0:T(1,128)} %pairs.3) | copy-start | bytes 40
  17.5 7.3 %copy-start.7 = (bf16[32,384]{1,0:T(8,128)(2,1)S(1)}, bf16[32,384]{1,0:T(8,128)(2,1)}, u32[]{:S(2)}) copy-start(bf16[32,384]{1,0:T(8,128)(2,1)} %constant.51.clone.lb) | copy-start | bytes 73732
  17.5 7.3 %copy-start.8 = (bf16[2,16,64]{2,1,0:T(8,128)(2,1)S(1)}, bf16[2,16,64]{2,1,0:T(8,128)(2,1)}, u32[]{:S(2)}) copy-start(bf16[2,16,64]{2,1,0:T(8,128)(2,1)} %constant.50.clone.window) | copy-start | bytes 12292
  17.6 5.5 %collective-permute-start.5 = (f32[3,16,128]{2,1,0:T(8,128)S(1)}, f32[3,16,128]{2,1,0:T(8,128)S(1)}, u32[]{:S(2)}, u32[]{:S(2)}) collective-permute-start(f32[3,16,128]{2,1,0:T(8,128)S(1)} %choose.1.fields), channel_id=1, source_target_pairs={{0,8},{1,10},{2,9},{3,12},{4,11},{5,14},{6,13},{7,15},{8,0},{9,2},... | collective-permute-start | bytes 73736 | tf_op jit(solution)/shard_map/ppermute | solution.py:329
  21.0 3.5 %collective-permute-start.6 = (f32[3,16,128]{2,1,0:T(8,128)S(1)}, f32[3,16,128]{2,1,0:T(8,128)S(1)}, u32[]{:S(2)}, u32[]{:S(2)}) collective-permute-start(f32[3,16,128]{2,1,0:T(8,128)S(1)} %choose.1.fields), channel_id=1, source_target_pairs={{0,8},{1,2},{2,1},{3,4},{4,3},{5,6},{6,5},{7,15},{8,0},{9,10},{10,... | collective-permute-start | bytes 73736 | tf_op jit(solution)/shard_map/ppermute | solution.py:329
  21.0 3.7 %collective-permute-start.7 = (f32[3,16,128]{2,1,0:T(8,128)S(1)}, f32[3,16,128]{2,1,0:T(8,128)S(1)}, u32[]{:S(2)}, u32[]{:S(2)}) collective-permute-start(f32[3,16,128]{2,1,0:T(8,128)S(1)} %choose.1.fields), channel_id=1, source_target_pairs={{0,9},{1,8},{2,11},{3,10},{4,13},{5,12},{6,15},{7,14},{8,1},{9,0},... | collective-permute-start | bytes 73736 | tf_op jit(solution)/shard_map/ppermute | solution.py:329
  22.1 2.8 %collective-permute-start.8 = (f32[3,16,128]{2,1,0:T(8,128)S(1)}, f32[3,16,128]{2,1,0:T(8,128)S(1)}, u32[]{:S(2)}, u32[]{:S(2)}) collective-permute-start(f32[3,16,128]{2,1,0:T(8,128)S(1)} %choose.1.fields), channel_id=1, source_target_pairs={{0,8},{1,9},{2,10},{3,11},{4,12},{5,13},{6,14},{7,15},{8,0},{9,1},... | collective-permute-start | bytes 73736 | tf_op jit(solution)/shard_map/ppermute | solution.py:329
  23.2 1.6 %collective-permute-start.9 = (f32[3,16,128]{2,1,0:T(8,128)S(1)}, f32[3,16,128]{2,1,0:T(8,128)S(1)}, u32[]{:S(2)}, u32[]{:S(2)}) collective-permute-start(f32[3,16,128]{2,1,0:T(8,128)S(1)} %choose.1.fields), channel_id=1, source_target_pairs={{0,1},{1,0},{2,3},{3,2},{4,5},{5,4},{6,7},{7,6},{8,9},{9,8},{10,11... | collective-permute-start | bytes 73736 | tf_op jit(solution)/shard_map/ppermute | solution.py:329

commit v7 on v6

--- a/solution.py
+++ b/solution.py
@@ -169,7 +169,7 @@
     return crossed + pltpu.roll(far_power, 64, 1) + pltpu.roll(own_power, 96, 1)
 
 
-def cross_kernel(own, other, up, down, look, own_out, other_out, powers, wide, sums):
+def cross_kernel(own, up, down, other, look, own_out, other_out, powers, wide, sums):
     widened((own, other, up, down), wide)
     couples = ((0, 1), (0, 2), (0, 3), (1, 2), (1, 3))
     fields = looked_fields(couples, (0, 1, 2, 3), 4, wide, sums, look)
@@ -216,8 +216,8 @@
 def finish_kernel(
     pairs,
     fields,
+    chip,
     chip_beside,
-    chip,
     core_beside,
     beside,
     core,
@@ -246,16 +246,19 @@
     values = jnp.concatenate([both(fields, beside), halo], axis=1)
     high, low = halves(values)
     table = cf_high[...]
-    mixed = dot(high, table) + dot(low, table) + dot(high, cf_low[...])
+    mixed = dot(high, table) + dot(low, table)
+    spread = mixed[:, 0:256] + dot(high, cf_low[:, 0:256])
     crossed = crossed_slots(offsets_of(pairs)[1])
-    rows = []
-    for slot in range(3):
-        first, second = mixed[16 * slot : 16 * slot + 16], mixed[48 + 16 * slot : 64 + 16 * slot]
-        turn = crossed[:, slot : slot + 1]
-        rows.append(jnp.concatenate([jnp.where(turn, second, first), jnp.where(turn, first, second)], axis=0))
-    real = jnp.concatenate([r[:, 0:128] for r in rows], axis=1)
-    imag = jnp.concatenate([r[:, 128:256] for r in rows], axis=1)
-    sums = jnp.concatenate([r[:, 256:384] for r in rows], axis=1)
+
+    def by_slot(values):
+        rows = []
+        for slot in range(3):
+            first, second = values[16 * slot : 16 * slot + 16], values[48 + 16 * slot : 64 + 16 * slot]
+            turn = crossed[:, slot : slot + 1]
+            rows.append(jnp.concatenate([jnp.where(turn, second, first), jnp.where(turn, first, second)], axis=0))
+        return jnp.concatenate(rows, axis=1)
+
+    real, imag, sums = by_slot(spread[:, 0:128]), by_slot(spread[:, 128:256]), by_slot(mixed[:, 256:384])
     high, low = halves(jnp.concatenate([real, imag], axis=0))
     spectrum = dot(lf[side], jnp.concatenate([high, low, high], axis=0))
     spec_real, spec_imag = spectrum[0:64], spectrum[64:128]
@@ -275,11 +278,11 @@
             block = power[32 * patch : 32 * patch + 32, 128 * slot : 128 * slot + 128]
             block = block + pltpu.roll(block, 1, 0) + pltpu.roll(block, 31, 0)
             block = block + turned(block, 1) + turned(block, -1)
-            smoothed.append(block / 9.0)
+            smoothed.append(block)
     largest = jnp.concatenate([jnp.max(b, axis=0, keepdims=True) for b in smoothed] + [jnp.zeros((2, 128), F32)], axis=0)
     groups = [jnp.max(jnp.where(lane // 32 == g, largest, 0.0), axis=1, keepdims=True) for g in range(3)]
     largest = jnp.where(lane < 32, groups[0], jnp.where(lane < 64, groups[1], groups[2]))
-    scale = 1.0 / (jnp.sqrt(largest) + 1e-06)
+    scale = 1.0 / (jnp.sqrt(largest) + 3e-06)
     weights = [jnp.sqrt(b) * scale[i : i + 1] for i, b in enumerate(smoothed)]
     weights = jnp.concatenate(
         [jnp.concatenate(weights[0:3], axis=1), jnp.concatenate(weights[3:6], axis=1)], axis=0
@@ -363,7 +366,7 @@
         )(*operands)
 
     own_fields, other_fields, powers = looked(
-        cross_kernel, "cross", ((3, 16, 128), (2, 16, 128), (16, 128)), 4, 14, (tile, other, up, down, look)
+        cross_kernel, "cross", ((3, 16, 128), (2, 16, 128), (16, 128)), 4, 14, (tile, up, down, other, look)
     )
     swapped = moved(other_fields, lambda z, h, l, r: (z, 1 - h, 1 - l, r))
     (away,) = looked(far_kernel, "far", ((16, 128),), 2, 3, (tile, far, powers, look))
@@ -396,8 +399,8 @@
     )(
         pairs,
         fields,
+        halos["chip"],
         halos["chip_beside"],
-        halos["chip"],
         halos["core_beside"],
         halos["beside"],
         halos["core"],

time: 27.1 us -> 27 us (level); the launches traced: 26.6 us -> 26.9 us
    ppermute x10, waiting for transfers between devices: 9.94 us -> 10.2 us  [moved(): return lax.ppermute(value, EVERY, pairs)]
  transfers between devices with their start and end apart: 10 -> 10, of which waited for: 5 -> 3; matrix products, arithmetic and copies ran while one was open for 0% -> 0% of each run, Pallas kernels for 4% -> 4%
where the time goes in v7:
time: 27 us; the launch traced here: 26.9 us
  starting transfers between devices  13.1 us (49%)
  waiting for transfers between devices  10.2 us (38%)
  Pallas kernels  2.73 us (10%)
  between operations  0.74 us (3%)
    ppermute x10, starting transfers between devices, moved(): return lax.ppermute(value, EVERY, pairs)  13.1 us
    ppermute x10, waiting for transfers between devices, moved(): return lax.ppermute(value, EVERY, pairs)  10.2 us
    pallas_call x1, Pallas kernels, per_device(): pl.pallas_call(finish_kernel, out_shape=(jax.ShapeDtypeStruct((3, 2, 16,...  1.67 us
    pallas_call x2, Pallas kernels, looked(): pl.pallas_call(kernel, out_shape=[jax.ShapeDtypeStruct(shape, F32) for sh...  0.96 us
  transfers between devices with their start and end apart: 10, of which 3 were waited for; matrix products, arithmetic and copies ran while one was open for 0% of the time, Pallas kernels for 4%

profile of v7, /device:TPU:1, one launch (start us, length us, event | category | flops | bytes accessed | tf_op | source)
XLA Modules:
  0.0 26.9 jit_solution(5084507200268187169)
XLA Ops:
  0.6 2.6 %collective-permute-start = (bf16[2,64,512]{2,1,0:T(8,128)(2,1)}, bf16[2,64,512]{2,1,0:T(8,128)(2,1)S(1)}, u32[]{:S(2)}, u32[]{:S(2)}) collective-permute-start(bf16[2,64,512]{2,1,0:T(8,128)(2,1)} %bitcast.3), channel_id=1, source_target_pairs={{0,32},{1,33},{2,34},{3,35},{4,36},{5,37},{6,38},{7,39},{8,40},{9,... | collective-permute-start | bytes 393224 | tf_op jit(solution)/shard_map/ppermute | solution.py:332
  3.2 1.0 %collective-permute-start.1 = (bf16[2,64,512]{2,1,0:T(8,128)(2,1)}, bf16[2,64,512]{2,1,0:T(8,128)(2,1)S(1)}, u32[]{:S(2)}, u32[]{:S(2)}) collective-permute-start(bf16[2,64,512]{2,1,0:T(8,128)(2,1)} %bitcast.4), channel_id=1, source_target_pairs={{0,1},{1,0},{2,3},{3,2},{4,5},{5,4},{6,7},{7,6},{8,9},{9,8},{10,11... | collective-permute-start | bytes 393224 | tf_op jit(solution)/shard_map/ppermute | solution.py:332
  4.1 2.9 %collective-permute-start.2 = (bf16[2,64,512]{2,1,0:T(8,128)(2,1)}, bf16[2,64,512]{2,1,0:T(8,128)(2,1)S(1)}, u32[]{:S(2)}, u32[]{:S(2)}) collective-permute-start(bf16[2,64,512]{2,1,0:T(8,128)(2,1)} %bitcast.5), channel_id=1, source_target_pairs={{0,16},{1,17},{2,18},{3,19},{4,20},{5,21},{6,22},{7,23},{8,24},{9,... | collective-permute-start | bytes 393224 | tf_op jit(solution)/shard_map/ppermute | solution.py:332
  7.1 0.3 %collective-permute-start.3 = (bf16[2,64,512]{2,1,0:T(8,128)(2,1)}, bf16[2,64,512]{2,1,0:T(8,128)(2,1)S(1)}, u32[]{:S(2)}, u32[]{:S(2)}) collective-permute-start(bf16[2,64,512]{2,1,0:T(8,128)(2,1)} %bitcast.6), channel_id=1, source_target_pairs={{0,1},{1,0},{2,3},{3,2},{4,5},{5,4},{6,7},{7,6},{8,9},{9,8},{10,11... | collective-permute-start | bytes 393224 | tf_op jit(solution)/shard_map/ppermute | solution.py:332
  7.3 0.0 copy-start
  7.3 0.0 copy-start.1
  7.3 0.0 collective-permute-done
  7.3 0.0 collective-permute-done.1
  7.4 5.6 %collective-permute-done.2.other = bf16[2,64,512]{2,1,0:T(8,128)(2,1)S(1)} collective-permute-done((bf16[2,64,512]{2,1,0:T(8,128)(2,1)}, bf16[2,64,512]{2,1,0:T(8,128)(2,1)S(1)}, u32[]{:S(2)}, u32[]{:S(2)}) %collective-permute-start.2) | collective-permute-done | bytes 131104 | tf_op jit(solution)/shard_map/ppermute | solution.py:332
  13.0 0.0 copy-done
  13.0 0.0 copy-done.1
  13.0 0.0 copy-start.4
  13.0 0.0 copy-start.5
  13.0 0.0 copy-start.6
  13.0 0.7 %cross.1 = (f32[3,16,128]{2,1,0:T(8,128)S(1)}, f32[2,16,128]{2,1,0:T(8,128)S(1)}, f32[16,128]{1,0:T(8,128)S(1)}) custom-call(bf16[2,64,512]{2,1,0:T(8,128)(2,1)S(1)} %bitcast.7, bf16[2,64,512]{2,1,0:T(8,128)(2,1)S(1)} %get-tuple-element.13.up, bf16[2,64,512]{2,1,0:T(8,128)(2,1)S(1)} %get-tuple-element.12.down, ...), custom_call_target="tpu_custom_call" | custom-call | tf_op jit(solution)/shard_map/cross/pallas_call | solution.py:358
  13.6 0.8 %collective-permute-start.4 = (f32[2,16,128]{2,1,0:T(8,128)S(1)}, f32[2,16,128]{2,1,0:T(8,128)S(1)}, u32[]{:S(2)}, u32[]{:S(2)}) collective-permute-start(f32[2,16,128]{2,1,0:T(8,128)S(1)} %get-tuple-element.9), channel_id=1, source_target_pairs={{0,24},{1,25},{2,26},{3,27},{4,28},{5,29},{6,30},{7,31},{8,16},{9,... | collective-permute-start | bytes 49160 | tf_op jit(solution)/shard_map/ppermute | solution.py:332
  14.5 0.0 collective-permute-done.3.far
  14.5 0.0 copy-start.2
  14.5 0.0 copy-start.3
  14.5 0.3 %far.1 = f32[16,128]{1,0:T(8,128)S(1)} custom-call(bf16[2,64,512]{2,1,0:T(8,128)(2,1)S(1)} %bitcast.8, bf16[2,64,512]{2,1,0:T(8,128)(2,1)S(1)} %collective-permute-done.3.far, f32[16,128]{1,0:T(8,128)S(1)} %get-tuple-element.8.powers, bf16[512,128]{1,0:T(8,128)(2,1)S(1)} %copy-done.1), custom_call_target="tpu_custom_call" | custom-call | tf_op jit(solution)/shard_map/far/pallas_call | solution.py:358
  14.8 0.0 copy-start.9
  14.8 2.7 %collective-permute-done.4.swapped = f32[2,16,128]{2,1,0:T(8,128)S(1)} collective-permute-done((f32[2,16,128]{2,1,0:T(8,128)S(1)}, f32[2,16,128]{2,1,0:T(8,128)S(1)}, u32[]{:S(2)}, u32[]{:S(2)}) %collective-permute-start.4) | collective-permute-done | bytes 16416 | tf_op jit(solution)/shard_map/ppermute | solution.py:332
  17.5 0.0 copy-done.9
  17.5 0.0 copy-start.7
  17.5 0.0 copy-start.8
  17.5 0.1 choose.1.fields
  17.6 3.3 %collective-permute-start.5 = (f32[3,16,128]{2,1,0:T(8,128)S(1)}, f32[3,16,128]{2,1,0:T(8,128)S(1)}, u32[]{:S(2)}, u32[]{:S(2)}) collective-permute-start(f32[3,16,128]{2,1,0:T(8,128)S(1)} %choose.1.fields), channel_id=1, source_target_pairs={{0,8},{1,2},{2,1},{3,4},{4,3},{5,6},{6,5},{7,15},{8,0},{9,10},{10,... | collective-permute-start | bytes 73736 | tf_op jit(solution)/shard_map/ppermute | solution.py:332
  20.9 0.1 collective-permute-start.6
  21.1 1.0 %collective-permute-start.7 = (f32[3,16,128]{2,1,0:T(8,128)S(1)}, f32[3,16,128]{2,1,0:T(8,128)S(1)}, u32[]{:S(2)}, u32[]{:S(2)}) collective-permute-start(f32[3,16,128]{2,1,0:T(8,128)S(1)} %choose.1.fields), channel_id=1, source_target_pairs={{0,9},{1,8},{2,11},{3,10},{4,13},{5,12},{6,15},{7,14},{8,1},{9,0},... | collective-permute-start | bytes 73736 | tf_op jit(solution)/shard_map/ppermute | solution.py:332
  22.1 1.1 %collective-permute-start.8 = (f32[3,16,128]{2,1,0:T(8,128)S(1)}, f32[3,16,128]{2,1,0:T(8,128)S(1)}, u32[]{:S(2)}, u32[]{:S(2)}) collective-permute-start(f32[3,16,128]{2,1,0:T(8,128)S(1)} %choose.1.fields), channel_id=1, source_target_pairs={{0,8},{1,9},{2,10},{3,11},{4,12},{5,13},{6,14},{7,15},{8,0},{9,1},... | collective-permute-start | bytes 73736 | tf_op jit(solution)/shard_map/ppermute | solution.py:332
  23.2 0.0 collective-permute-start.9
  23.2 0.0 collective-permute-done.5.chip
  23.2 1.9 %collective-permute-done.6.chip_beside = f32[3,16,128]{2,1,0:T(8,128)S(1)} collective-permute-done((f32[3,16,128]{2,1,0:T(8,128)S(1)}, f32[3,16,128]{2,1,0:T(8,128)S(1)}, u32[]{:S(2)}, u32[]{:S(2)}) %collective-permute-start.6) | collective-permute-done | bytes 24608 | tf_op jit(solution)/shard_map/ppermute | solution.py:332
  25.1 0.0 collective-permute-done.7.core_beside
  25.1 0.0 collective-permute-done.8.beside
  25.1 0.0 collective-permute-done.9.core
  25.1 0.0 copy-done.4
  25.1 0.0 copy-done.5
  25.1 0.0 copy-done.6
  25.1 0.0 copy-done.2
  25.1 0.0 copy-done.3
  25.2 0.0 copy-done.7
  25.2 0.0 copy-done.8
  25.2 1.7 %finish.1 = (f32[3,2,16,32]{3,2,1,0:T(8,128)}, f32[3,16,32]{2,1,0:T(8,128)}) custom-call(s32[1,3]{1,0:T(1,128)S(1)} %copy-done.9, f32[3,16,128]{2,1,0:T(8,128)S(1)} %choose.1.fields, f32[3,16,128]{2,1,0:T(8,128)S(1)} %collective-permute-done.5.chip, f32[3,16,128]{2,1,0:T(8,128)S(1)} %collective-permute-done.6.chip_beside, ...), custom_call_target="tpu_custom_call" | custom-call | tf_op jit(solution)/shard_map/finish/pallas_call | solution.py:392
  (1 shorter events, 0.0 us)
Async XLA Ops:
  0.6 6.7 %collective-permute-start = (bf16[2,64,512]{2,1,0:T(8,128)(2,1)}, bf16[2,64,512]{2,1,0:T(8,128)(2,1)S(1)}, u32[]{:S(2)}, u32[]{:S(2)}) collective-permute-start(bf16[2,64,512]{2,1,0:T(8,128)(2,1)} %bitcast.3), channel_id=1, source_target_pairs={{0,32},{1,33},{2,34},{3,35},{4,36},{5,37},{6,38},{7,39},{8,40},{9,... | collective-permute-start | bytes 393224 | tf_op jit(solution)/shard_map/ppermute | solution.py:332
  3.2 4.2 %collective-permute-start.1 = (bf16[2,64,512]{2,1,0:T(8,128)(2,1)}, bf16[2,64,512]{2,1,0:T(8,128)(2,1)S(1)}, u32[]{:S(2)}, u32[]{:S(2)}) collective-permute-start(bf16[2,64,512]{2,1,0:T(8,128)(2,1)} %bitcast.4), channel_id=1, source_target_pairs={{0,1},{1,0},{2,3},{3,2},{4,5},{5,4},{6,7},{7,6},{8,9},{9,8},{10,11... | collective-permute-start | bytes 393224 | tf_op jit(solution)/shard_map/ppermute | solution.py:332
  4.1 8.8 %collective-permute-start.2 = (bf16[2,64,512]{2,1,0:T(8,128)(2,1)}, bf16[2,64,512]{2,1,0:T(8,128)(2,1)S(1)}, u32[]{:S(2)}, u32[]{:S(2)}) collective-permute-start(bf16[2,64,512]{2,1,0:T(8,128)(2,1)} %bitcast.5), channel_id=1, source_target_pairs={{0,16},{1,17},{2,18},{3,19},{4,20},{5,21},{6,22},{7,23},{8,24},{9,... | collective-permute-start | bytes 393224 | tf_op jit(solution)/shard_map/ppermute | solution.py:332
  7.1 7.4 %collective-permute-start.3 = (bf16[2,64,512]{2,1,0:T(8,128)(2,1)}, bf16[2,64,512]{2,1,0:T(8,128)(2,1)S(1)}, u32[]{:S(2)}, u32[]{:S(2)}) collective-permute-start(bf16[2,64,512]{2,1,0:T(8,128)(2,1)} %bitcast.6), channel_id=1, source_target_pairs={{0,1},{1,0},{2,3},{3,2},{4,5},{5,4},{6,7},{7,6},{8,9},{9,8},{10,11... | collective-permute-start | bytes 393224 | tf_op jit(solution)/shard_map/ppermute | solution.py:332
  7.3 5.6 %copy-start = (bf16[1,2,64,512]{3,2,1,0:T(8,128)(2,1)S(1)}, bf16[1,2,64,512]{3,2,1,0:T(8,128)(2,1)}, u32[]{:S(2)}) copy-start(bf16[1,2,64,512]{3,2,1,0:T(8,128)(2,1)} %param.10) | copy-start | bytes 393220
  7.3 5.6 %copy-start.1 = (bf16[512,128]{1,0:T(8,128)(2,1)S(1)}, bf16[512,128]{1,0:T(8,128)(2,1)}, u32[]{:S(2)}) copy-start(bf16[512,128]{1,0:T(8,128)(2,1)} %constant.46.clone.look) | copy-start | bytes 393220
  13.0 12.1 %copy-start.4 = (bf16[2,128,192]{2,1,0:T(8,128)(2,1)S(1)}, bf16[2,128,192]{2,1,0:T(8,128)(2,1)}, u32[]{:S(2)}) copy-start(bf16[2,128,192]{2,1,0:T(8,128)(2,1)} %constant.49.clone.lf) | copy-start | bytes 294916
  13.0 12.2 %copy-start.5 = (bf16[256,256]{1,0:T(8,128)(2,1)S(1)}, bf16[256,256]{1,0:T(8,128)(2,1)}, u32[]{:S(2)}) copy-start(bf16[256,256]{1,0:T(8,128)(2,1)} %constant.52.clone.cb_high) | copy-start | bytes 393220
  13.0 12.2 %copy-start.6 = (bf16[256,256]{1,0:T(8,128)(2,1)S(1)}, bf16[256,256]{1,0:T(8,128)(2,1)}, u32[]{:S(2)}) copy-start(bf16[256,256]{1,0:T(8,128)(2,1)} %constant.53.clone.cb_low) | copy-start | bytes 393220
  13.6 3.9 %collective-permute-start.4 = (f32[2,16,128]{2,1,0:T(8,128)S(1)}, f32[2,16,128]{2,1,0:T(8,128)S(1)}, u32[]{:S(2)}, u32[]{:S(2)}) collective-permute-start(f32[2,16,128]{2,1,0:T(8,128)S(1)} %get-tuple-element.9), channel_id=1, source_target_pairs={{0,24},{1,25},{2,26},{3,27},{4,28},{5,29},{6,30},{7,31},{8,16},{9,... | collective-permute-start | bytes 49160 | tf_op jit(solution)/shard_map/ppermute | solution.py:332
  14.5 10.6 %copy-start.2 = (bf16[256,384]{1,0:T(8,128)(2,1)S(1)}, bf16[256,384]{1,0:T(8,128)(2,1)}, u32[]{:S(2)}) copy-start(bf16[256,384]{1,0:T(8,128)(2,1)} %constant.47.clone.cf_high) | copy-start | bytes 589828
  14.5 10.7 %copy-start.3 = (bf16[256,384]{1,0:T(8,128)(2,1)S(1)}, bf16[256,384]{1,0:T(8,128)(2,1)}, u32[]{:S(2)}) copy-start(bf16[256,384]{1,0:T(8,128)(2,1)} %constant.48.clone.cf_low) | copy-start | bytes 589828
  14.8 2.7 %copy-start.9 = (s32[1,3]{1,0:T(1,128)S(1)}, s32[1,3]{1,0:T(1,128)}, u32[]{:S(2)}) copy-start(s32[1,3]{1,0:T(1,128)} %pairs.3) | copy-start | bytes 40
  17.5 7.6 %copy-start.7 = (bf16[32,384]{1,0:T(8,128)(2,1)S(1)}, bf16[32,384]{1,0:T(8,128)(2,1)}, u32[]{:S(2)}) copy-start(bf16[32,384]{1,0:T(8,128)(2,1)} %constant.51.clone.lb) | copy-start | bytes 73732
  17.5 7.6 %copy-start.8 = (bf16[2,16,64]{2,1,0:T(8,128)(2,1)S(1)}, bf16[2,16,64]{2,1,0:T(8,128)(2,1)}, u32[]{:S(2)}) copy-start(bf16[2,16,64]{2,1,0:T(8,128)(2,1)} %constant.50.clone.window) | copy-start | bytes 12292
  17.6 5.6 %collective-permute-start.5 = (f32[3,16,128]{2,1,0:T(8,128)S(1)}, f32[3,16,128]{2,1,0:T(8,128)S(1)}, u32[]{:S(2)}, u32[]{:S(2)}) collective-permute-start(f32[3,16,128]{2,1,0:T(8,128)S(1)} %choose.1.fields), channel_id=1, source_target_pairs={{0,8},{1,2},{2,1},{3,4},{4,3},{5,6},{6,5},{7,15},{8,0},{9,10},{10,... | collective-permute-start | bytes 73736 | tf_op jit(solution)/shard_map/ppermute | solution.py:332
  20.9 4.2 %collective-permute-start.6 = (f32[3,16,128]{2,1,0:T(8,128)S(1)}, f32[3,16,128]{2,1,0:T(8,128)S(1)}, u32[]{:S(2)}, u32[]{:S(2)}) collective-permute-start(f32[3,16,128]{2,1,0:T(8,128)S(1)} %choose.1.fields), channel_id=1, source_target_pairs={{0,8},{1,10},{2,9},{3,12},{4,11},{5,14},{6,13},{7,15},{8,0},{9,2},... | collective-permute-start | bytes 73736 | tf_op jit(solution)/shard_map/ppermute | solution.py:332
  21.1 4.0 %collective-permute-start.7 = (f32[3,16,128]{2,1,0:T(8,128)S(1)}, f32[3,16,128]{2,1,0:T(8,128)S(1)}, u32[]{:S(2)}, u32[]{:S(2)}) collective-permute-start(f32[3,16,128]{2,1,0:T(8,128)S(1)} %choose.1.fields), channel_id=1, source_target_pairs={{0,9},{1,8},{2,11},{3,10},{4,13},{5,12},{6,15},{7,14},{8,1},{9,0},... | collective-permute-start | bytes 73736 | tf_op jit(solution)/shard_map/ppermute | solution.py:332
  22.1 3.0 %collective-permute-start.8 = (f32[3,16,128]{2,1,0:T(8,128)S(1)}, f32[3,16,128]{2,1,0:T(8,128)S(1)}, u32[]{:S(2)}, u32[]{:S(2)}) collective-permute-start(f32[3,16,128]{2,1,0:T(8,128)S(1)} %choose.1.fields), channel_id=1, source_target_pairs={{0,8},{1,9},{2,10},{3,11},{4,12},{5,13},{6,14},{7,15},{8,0},{9,1},... | collective-permute-start | bytes 73736 | tf_op jit(solution)/shard_map/ppermute | solution.py:332
  23.2 1.9 %collective-permute-start.9 = (f32[3,16,128]{2,1,0:T(8,128)S(1)}, f32[3,16,128]{2,1,0:T(8,128)S(1)}, u32[]{:S(2)}, u32[]{:S(2)}) collective-permute-start(f32[3,16,128]{2,1,0:T(8,128)S(1)} %choose.1.fields), channel_id=1, source_target_pairs={{0,1},{1,0},{2,3},{3,2},{4,5},{5,4},{6,7},{7,6},{8,9},{9,8},{10,11... | collective-permute-start | bytes 73736 | tf_op jit(solution)/shard_map/ppermute | solution.py:332

commit v8 on v7

--- a/solution.py
+++ b/solution.py
@@ -169,17 +169,22 @@
     return crossed + pltpu.roll(far_power, 64, 1) + pltpu.roll(own_power, 96, 1)
 
 
-def cross_kernel(own, up, down, other, look, own_out, other_out, powers, wide, sums):
+def line_kernel(own, up, down, look, out, powers, wide, sums):
+    widened((own, up, down), wide)
+    fields = looked_fields(((0, 1), (0, 2)), (0, 1, 2), 3, wide, sums, look)
+    for index in range(2):
+        out[index] = record(fields[index], fields[2 + index], fields[5 + index], fields[4])
+    for index in range(3):
+        powers[index] = fields[4 + index]
+
+
+def cross_kernel(own, other, up, down, powers, look, near, other_out, power, wide, sums):
     widened((own, other, up, down), wide)
-    couples = ((0, 1), (0, 2), (0, 3), (1, 2), (1, 3))
-    fields = looked_fields(couples, (0, 1, 2, 3), 4, wide, sums, look)
-    power = fields[10:14]
-    records = [record(fields[i], fields[5 + i], power[v], power[u]) for i, (u, v) in enumerate(couples)]
-    for index in range(3):
-        own_out[index] = records[index]
+    fields = looked_fields(((0, 1), (1, 2), (1, 3)), (1,), 4, wide, sums, look)
+    near[...] = record(fields[0], fields[3], fields[6], powers[0])
     for index in range(2):
-        other_out[index] = records[3 + index]
-    powers[...] = power[0]
+        other_out[index] = record(fields[1 + index], fields[4 + index], powers[1 + index], fields[6])
+    power[...] = powers[0]
 
 
 def far_kernel(own, far, powers, look, out, wide, sums):
@@ -199,16 +204,16 @@
     return (flipped == 3) | (flipped == -1)
 
 
-def choose_kernel(pairs, own, far, swapped, out):
+def choose_kernel(pairs, near, beyond, far, swapped, out):
     odd, flipped = offsets_of(pairs)
     up = jnp.where(odd, -2, 2)
     third = jnp.where(odd, swapped[1], swapped[0])
     first = jnp.where(odd, swapped[0], swapped[1])
     for slot in range(3):
         at = flipped[:, slot : slot + 1]
-        chosen = jnp.where(at == 1, own[0], far[...])
-        chosen = jnp.where(at == up, own[1], chosen)
-        chosen = jnp.where(at == -up, own[2], chosen)
+        chosen = jnp.where(at == 1, near[...], far[...])
+        chosen = jnp.where(at == up, beyond[0], chosen)
+        chosen = jnp.where(at == -up, beyond[1], chosen)
         chosen = jnp.where(at == 3, third, chosen)
         out[slot] = jnp.where(at == -1, first, chosen)
 
@@ -216,8 +221,8 @@
 def finish_kernel(
     pairs,
     fields,
+    chip_beside,
     chip,
-    chip_beside,
     core_beside,
     beside,
     core,
@@ -365,19 +370,25 @@
             name=name,
         )(*operands)
 
-    own_fields, other_fields, powers = looked(
-        cross_kernel, "cross", ((3, 16, 128), (2, 16, 128), (16, 128)), 4, 14, (tile, up, down, other, look)
+    beyond, line_powers = looked(line_kernel, "line", ((2, 16, 128), (3, 16, 128)), 3, 7, (tile, up, down, look))
+    near, other_fields, powers = looked(
+        cross_kernel,
+        "cross",
+        ((16, 128), (2, 16, 128), (16, 128)),
+        4,
+        7,
+        (tile, other, up, down, line_powers, look),
     )
     swapped = moved(other_fields, lambda z, h, l, r: (z, 1 - h, 1 - l, r))
     (away,) = looked(far_kernel, "far", ((16, 128),), 2, 3, (tile, far, powers, look))
     fields = pl.pallas_call(
         choose_kernel,
         out_shape=jax.ShapeDtypeStruct((3, 16, 128), F32),
-        in_specs=[VMEM] * 4,
+        in_specs=[VMEM] * 5,
         out_specs=VMEM,
         compiler_params=pltpu.CompilerParams(vmem_limit_bytes=4 * 2**20),
         name="choose",
-    )(pairs, own_fields, away, swapped)
+    )(pairs, near, beyond, away, swapped)
 
     def chip_of(r):
         return ((r + 1) ^ 1) - 1
@@ -399,8 +410,8 @@
     )(
         pairs,
         fields,
+        halos["chip_beside"],
         halos["chip"],
-        halos["chip_beside"],
         halos["core_beside"],
         halos["beside"],
         halos["core"],

time: 27 us -> 27.5 us (1.019); the launches traced: 26.9 us -> 27 us
  waiting for transfers between devices: 10.2 us -> 8.57 us
  local copies, waits for them, and re-layouts: 0.04 us -> 1.61 us
    ppermute x10, waiting for transfers between devices: 10.2 us -> 8.57 us  [moved(): return lax.ppermute(value, EVERY, pairs)]
    unnamed x20, local copies, waits for them, and re-layouts: 0.04 us -> 1.61 us
    pallas_call x2 -> x3, Pallas kernels: 0.96 us -> 1.22 us  [looked(): pl.pallas_call(kernel, out_shape=[jax.ShapeDtypeStruct(shape, F32) for sh...]
  transfers between devices with their start and end apart: 10 -> 10, of which waited for: 3 -> 5; matrix products, arithmetic and copies ran while one was open for 0% -> 0% of each run, Pallas kernels for 4% -> 5%
where the time goes in v8:
time: 27.5 us; the launch traced here: 27 us
  starting transfers between devices  13.1 us (48%)
  waiting for transfers between devices  8.57 us (31%)
  Pallas kernels  2.99 us (11%)
  local copies, waits for them, and re-layouts  1.61 us (6%)
  between operations  0.72 us (3%)
    ppermute x10, starting transfers between devices, moved(): return lax.ppermute(value, EVERY, pairs)  13.1 us
    ppermute x10, waiting for transfers between devices, moved(): return lax.ppermute(value, EVERY, pairs)  8.57 us
    pallas_call x1, Pallas kernels, per_device(): pl.pallas_call(finish_kernel, out_shape=(jax.ShapeDtypeStruct((3, 2, 16,...  1.67 us
    unnamed x20, local copies, waits for them, and re-layouts  1.61 us
    pallas_call x3, Pallas kernels, looked(): pl.pallas_call(kernel, out_shape=[jax.ShapeDtypeStruct(shape, F32) for sh...  1.22 us
  transfers between devices with their start and end apart: 10, of which 5 were waited for; matrix products, arithmetic and copies ran while one was open for 0% of the time, Pallas kernels for 5%

profile of v8, /device:TPU:1, one launch (start us, length us, event | category | flops | bytes accessed | tf_op | source)
XLA Modules:
  0.0 27.0 jit_solution(18102148249851593986)
XLA Ops:
  0.6 2.6 %collective-permute-start.1 = (bf16[2,64,512]{2,1,0:T(8,128)(2,1)}, bf16[2,64,512]{2,1,0:T(8,128)(2,1)S(1)}, u32[]{:S(2)}, u32[]{:S(2)}) collective-permute-start(bf16[2,64,512]{2,1,0:T(8,128)(2,1)} %bitcast.3), channel_id=1, source_target_pairs={{0,32},{1,33},{2,34},{3,35},{4,36},{5,37},{6,38},{7,39},{8,40},{9,... | collective-permute-start | bytes 393224 | tf_op jit(solution)/shard_map/ppermute | solution.py:337
  3.2 1.0 %collective-permute-start.2 = (bf16[2,64,512]{2,1,0:T(8,128)(2,1)}, bf16[2,64,512]{2,1,0:T(8,128)(2,1)S(1)}, u32[]{:S(2)}, u32[]{:S(2)}) collective-permute-start(bf16[2,64,512]{2,1,0:T(8,128)(2,1)} %bitcast.4), channel_id=1, source_target_pairs={{0,1},{1,0},{2,3},{3,2},{4,5},{5,4},{6,7},{7,6},{8,9},{9,8},{10,11... | collective-permute-start | bytes 393224 | tf_op jit(solution)/shard_map/ppermute | solution.py:337
  4.1 2.9 %collective-permute-start = (bf16[2,64,512]{2,1,0:T(8,128)(2,1)}, bf16[2,64,512]{2,1,0:T(8,128)(2,1)S(1)}, u32[]{:S(2)}, u32[]{:S(2)}) collective-permute-start(bf16[2,64,512]{2,1,0:T(8,128)(2,1)} %bitcast.5), channel_id=1, source_target_pairs={{0,16},{1,17},{2,18},{3,19},{4,20},{5,21},{6,22},{7,23},{8,24},{9,... | collective-permute-start | bytes 393224 | tf_op jit(solution)/shard_map/ppermute | solution.py:337
  7.1 0.3 %collective-permute-start.3 = (bf16[2,64,512]{2,1,0:T(8,128)(2,1)}, bf16[2,64,512]{2,1,0:T(8,128)(2,1)S(1)}, u32[]{:S(2)}, u32[]{:S(2)}) collective-permute-start(bf16[2,64,512]{2,1,0:T(8,128)(2,1)} %bitcast.6), channel_id=1, source_target_pairs={{0,1},{1,0},{2,3},{3,2},{4,5},{5,4},{6,7},{7,6},{8,9},{9,8},{10,11... | collective-permute-start | bytes 393224 | tf_op jit(solution)/shard_map/ppermute | solution.py:337
  7.3 0.0 copy-start
  7.3 0.0 copy-start.1
  7.3 0.0 collective-permute-done.1
  7.3 0.0 collective-permute-done.2
  7.4 0.9 %copy-done = bf16[1,2,64,512]{3,2,1,0:T(8,128)(2,1)S(1)} copy-done((bf16[1,2,64,512]{3,2,1,0:T(8,128)(2,1)S(1)}, bf16[1,2,64,512]{3,2,1,0:T(8,128)(2,1)}, u32[]{:S(2)}) %copy-start) | copy-done | bytes 131096
  8.2 0.1 copy-done.1
  8.3 0.4 %line.1 = (f32[2,16,128]{2,1,0:T(8,128)S(1)}, f32[3,16,128]{2,1,0:T(8,128)S(1)}) custom-call(bf16[2,64,512]{2,1,0:T(8,128)(2,1)S(1)} %bitcast.7, bf16[2,64,512]{2,1,0:T(8,128)(2,1)S(1)} %get-tuple-element.17.up, bf16[2,64,512]{2,1,0:T(8,128)(2,1)S(1)} %get-tuple-element.16.down, bf16[512,128]{1,0:T(8,128)(2,1)S(1)} %copy-done.1), custom_call_target="tpu_custom_call" | custom-call | tf_op jit(solution)/shard_map/line/pallas_call | solution.py:363
  8.8 4.2 %collective-permute-done.other = bf16[2,64,512]{2,1,0:T(8,128)(2,1)S(1)} collective-permute-done((bf16[2,64,512]{2,1,0:T(8,128)(2,1)}, bf16[2,64,512]{2,1,0:T(8,128)(2,1)S(1)}, u32[]{:S(2)}, u32[]{:S(2)}) %collective-permute-start) | collective-permute-done | bytes 131104 | tf_op jit(solution)/shard_map/ppermute | solution.py:337
  13.0 0.0 copy-start.4
  13.0 0.0 copy-start.5
  13.0 0.0 copy-start.6
  13.0 0.5 %cross.1 = (f32[16,128]{1,0:T(8,128)S(1)}, f32[2,16,128]{2,1,0:T(8,128)S(1)}, f32[16,128]{1,0:T(8,128)S(1)}) custom-call(bf16[2,64,512]{2,1,0:T(8,128)(2,1)S(1)} %bitcast.8, bf16[2,64,512]{2,1,0:T(8,128)(2,1)S(1)} %collective-permute-done.other, bf16[2,64,512]{2,1,0:T(8,128)(2,1)S(1)} %get-tuple-element.17.up, ...), custom_call_target="tpu_custom_call" | custom-call | tf_op jit(solution)/shard_map/cross/pallas_call | solution.py:363
  13.4 0.8 %collective-permute-start.4 = (f32[2,16,128]{2,1,0:T(8,128)S(1)}, f32[2,16,128]{2,1,0:T(8,128)S(1)}, u32[]{:S(2)}, u32[]{:S(2)}) collective-permute-start(f32[2,16,128]{2,1,0:T(8,128)S(1)} %get-tuple-element.13), channel_id=1, source_target_pairs={{0,24},{1,25},{2,26},{3,27},{4,28},{5,29},{6,30},{7,31},{8,16},{9,... | collective-permute-start | bytes 49160 | tf_op jit(solution)/shard_map/ppermute | solution.py:337
  14.3 0.0 collective-permute-done.3.far
  14.3 0.0 copy-start.2
  14.3 0.0 copy-start.3
  14.3 0.3 %far.1 = f32[16,128]{1,0:T(8,128)S(1)} custom-call(bf16[2,64,512]{2,1,0:T(8,128)(2,1)S(1)} %bitcast.9, bf16[2,64,512]{2,1,0:T(8,128)(2,1)S(1)} %collective-permute-done.3.far, f32[16,128]{1,0:T(8,128)S(1)} %get-tuple-element.12.powers, bf16[512,128]{1,0:T(8,128)(2,1)S(1)} %copy-done.1), custom_call_target="tpu_custom_call" | custom-call | tf_op jit(solution)/shard_map/far/pallas_call | solution.py:363
  14.6 2.7 %collective-permute-done.4.swapped = f32[2,16,128]{2,1,0:T(8,128)S(1)} collective-permute-done((f32[2,16,128]{2,1,0:T(8,128)S(1)}, f32[2,16,128]{2,1,0:T(8,128)S(1)}, u32[]{:S(2)}, u32[]{:S(2)}) %collective-permute-start.4) | collective-permute-done | bytes 16416 | tf_op jit(solution)/shard_map/ppermute | solution.py:337
  17.3 0.0 copy-start.9
  17.3 0.7 %copy-done.9 = s32[1,3]{1,0:T(1,128)S(1)} copy-done((s32[1,3]{1,0:T(1,128)S(1)}, s32[1,3]{1,0:T(1,128)}, u32[]{:S(2)}) %copy-start.9) | copy-done | bytes 36
  18.0 0.0 copy-start.7
  18.0 0.0 copy-start.8
  18.0 0.1 choose.1.fields
  18.1 3.3 %collective-permute-start.5 = (f32[3,16,128]{2,1,0:T(8,128)S(1)}, f32[3,16,128]{2,1,0:T(8,128)S(1)}, u32[]{:S(2)}, u32[]{:S(2)}) collective-permute-start(f32[3,16,128]{2,1,0:T(8,128)S(1)} %choose.1.fields), channel_id=1, source_target_pairs={{0,8},{1,10},{2,9},{3,12},{4,11},{5,14},{6,13},{7,15},{8,0},{9,2},... | collective-permute-start | bytes 73736 | tf_op jit(solution)/shard_map/ppermute | solution.py:337
  21.4 0.1 collective-permute-start.6
  21.5 1.0 %collective-permute-start.7 = (f32[3,16,128]{2,1,0:T(8,128)S(1)}, f32[3,16,128]{2,1,0:T(8,128)S(1)}, u32[]{:S(2)}, u32[]{:S(2)}) collective-permute-start(f32[3,16,128]{2,1,0:T(8,128)S(1)} %choose.1.fields), channel_id=1, source_target_pairs={{0,9},{1,8},{2,11},{3,10},{4,13},{5,12},{6,15},{7,14},{8,1},{9,0},... | collective-permute-start | bytes 73736 | tf_op jit(solution)/shard_map/ppermute | solution.py:337
  22.5 1.1 %collective-permute-start.8 = (f32[3,16,128]{2,1,0:T(8,128)S(1)}, f32[3,16,128]{2,1,0:T(8,128)S(1)}, u32[]{:S(2)}, u32[]{:S(2)}) collective-permute-start(f32[3,16,128]{2,1,0:T(8,128)S(1)} %choose.1.fields), channel_id=1, source_target_pairs={{0,8},{1,9},{2,10},{3,11},{4,12},{5,13},{6,14},{7,15},{8,0},{9,1},... | collective-permute-start | bytes 73736 | tf_op jit(solution)/shard_map/ppermute | solution.py:337
  23.6 0.0 collective-permute-start.9
  23.6 0.0 collective-permute-done.5.chip_beside
  23.6 1.3 %collective-permute-done.6.chip = f32[3,16,128]{2,1,0:T(8,128)S(1)} collective-permute-done((f32[3,16,128]{2,1,0:T(8,128)S(1)}, f32[3,16,128]{2,1,0:T(8,128)S(1)}, u32[]{:S(2)}, u32[]{:S(2)}) %collective-permute-start.6) | collective-permute-done | bytes 24608 | tf_op jit(solution)/shard_map/ppermute | solution.py:337
  24.9 0.2 collective-permute-done.7.core_beside
  25.1 0.1 collective-permute-done.8.beside
  25.3 0.0 collective-permute-done.9.core
  25.3 0.0 copy-done.4
  25.3 0.0 copy-done.5
  25.3 0.0 copy-done.6
  25.3 0.0 copy-done.2
  25.3 0.0 copy-done.3
  25.3 0.0 copy-done.7
  25.3 0.0 copy-done.8
  25.3 1.7 %finish.1 = (f32[3,2,16,32]{3,2,1,0:T(8,128)}, f32[3,16,32]{2,1,0:T(8,128)}) custom-call(s32[1,3]{1,0:T(1,128)S(1)} %copy-done.9, f32[3,16,128]{2,1,0:T(8,128)S(1)} %choose.1.fields, f32[3,16,128]{2,1,0:T(8,128)S(1)} %collective-permute-done.5.chip_beside, f32[3,16,128]{2,1,0:T(8,128)S(1)} %collective-permute-done.6.chip, ...), custom_call_target="tpu_custom_call" | custom-call | tf_op jit(solution)/shard_map/finish/pallas_call | solution.py:403
  (1 shorter events, 0.0 us)
Async XLA Ops:
  0.6 6.7 %collective-permute-start.1 = (bf16[2,64,512]{2,1,0:T(8,128)(2,1)}, bf16[2,64,512]{2,1,0:T(8,128)(2,1)S(1)}, u32[]{:S(2)}, u32[]{:S(2)}) collective-permute-start(bf16[2,64,512]{2,1,0:T(8,128)(2,1)} %bitcast.3), channel_id=1, source_target_pairs={{0,32},{1,33},{2,34},{3,35},{4,36},{5,37},{6,38},{7,39},{8,40},{9,... | collective-permute-start | bytes 393224 | tf_op jit(solution)/shard_map/ppermute | solution.py:337
  3.2 4.2 %collective-permute-start.2 = (bf16[2,64,512]{2,1,0:T(8,128)(2,1)}, bf16[2,64,512]{2,1,0:T(8,128)(2,1)S(1)}, u32[]{:S(2)}, u32[]{:S(2)}) collective-permute-start(bf16[2,64,512]{2,1,0:T(8,128)(2,1)} %bitcast.4), channel_id=1, source_target_pairs={{0,1},{1,0},{2,3},{3,2},{4,5},{5,4},{6,7},{7,6},{8,9},{9,8},{10,11... | collective-permute-start | bytes 393224 | tf_op jit(solution)/shard_map/ppermute | solution.py:337
  4.1 8.8 %collective-permute-start = (bf16[2,64,512]{2,1,0:T(8,128)(2,1)}, bf16[2,64,512]{2,1,0:T(8,128)(2,1)S(1)}, u32[]{:S(2)}, u32[]{:S(2)}) collective-permute-start(bf16[2,64,512]{2,1,0:T(8,128)(2,1)} %bitcast.5), channel_id=1, source_target_pairs={{0,16},{1,17},{2,18},{3,19},{4,20},{5,21},{6,22},{7,23},{8,24},{9,... | collective-permute-start | bytes 393224 | tf_op jit(solution)/shard_map/ppermute | solution.py:337
  7.1 7.2 %collective-permute-start.3 = (bf16[2,64,512]{2,1,0:T(8,128)(2,1)}, bf16[2,64,512]{2,1,0:T(8,128)(2,1)S(1)}, u32[]{:S(2)}, u32[]{:S(2)}) collective-permute-start(bf16[2,64,512]{2,1,0:T(8,128)(2,1)} %bitcast.6), channel_id=1, source_target_pairs={{0,1},{1,0},{2,3},{3,2},{4,5},{5,4},{6,7},{7,6},{8,9},{9,8},{10,11... | collective-permute-start | bytes 393224 | tf_op jit(solution)/shard_map/ppermute | solution.py:337
  7.3 0.9 %copy-start = (bf16[1,2,64,512]{3,2,1,0:T(8,128)(2,1)S(1)}, bf16[1,2,64,512]{3,2,1,0:T(8,128)(2,1)}, u32[]{:S(2)}) copy-start(bf16[1,2,64,512]{3,2,1,0:T(8,128)(2,1)} %param.10) | copy-start | bytes 393220
  7.3 1.0 %copy-start.1 = (bf16[512,128]{1,0:T(8,128)(2,1)S(1)}, bf16[512,128]{1,0:T(8,128)(2,1)}, u32[]{:S(2)}) copy-start(bf16[512,128]{1,0:T(8,128)(2,1)} %constant.46.clone.look) | copy-start | bytes 393220
  13.0 12.3 %copy-start.4 = (bf16[2,128,192]{2,1,0:T(8,128)(2,1)S(1)}, bf16[2,128,192]{2,1,0:T(8,128)(2,1)}, u32[]{:S(2)}) copy-start(bf16[2,128,192]{2,1,0:T(8,128)(2,1)} %constant.49.clone.lf) | copy-start | bytes 294916
  13.0 12.3 %copy-start.5 = (bf16[256,256]{1,0:T(8,128)(2,1)S(1)}, bf16[256,256]{1,0:T(8,128)(2,1)}, u32[]{:S(2)}) copy-start(bf16[256,256]{1,0:T(8,128)(2,1)} %constant.52.clone.cb_high) | copy-start | bytes 393220
  13.0 12.3 %copy-start.6 = (bf16[256,256]{1,0:T(8,128)(2,1)S(1)}, bf16[256,256]{1,0:T(8,128)(2,1)}, u32[]{:S(2)}) copy-start(bf16[256,256]{1,0:T(8,128)(2,1)} %constant.53.clone.cb_low) | copy-start | bytes 393220
  13.4 3.9 %collective-permute-start.4 = (f32[2,16,128]{2,1,0:T(8,128)S(1)}, f32[2,16,128]{2,1,0:T(8,128)S(1)}, u32[]{:S(2)}, u32[]{:S(2)}) collective-permute-start(f32[2,16,128]{2,1,0:T(8,128)S(1)} %get-tuple-element.13), channel_id=1, source_target_pairs={{0,24},{1,25},{2,26},{3,27},{4,28},{5,29},{6,30},{7,31},{8,16},{9,... | collective-permute-start | bytes 49160 | tf_op jit(solution)/shard_map/ppermute | solution.py:337
  14.3 11.0 %copy-start.2 = (bf16[256,384]{1,0:T(8,128)(2,1)S(1)}, bf16[256,384]{1,0:T(8,128)(2,1)}, u32[]{:S(2)}) copy-start(bf16[256,384]{1,0:T(8,128)(2,1)} %constant.47.clone.cf_high) | copy-start | bytes 589828
  14.3 11.0 %copy-start.3 = (bf16[256,384]{1,0:T(8,128)(2,1)S(1)}, bf16[256,384]{1,0:T(8,128)(2,1)}, u32[]{:S(2)}) copy-start(bf16[256,384]{1,0:T(8,128)(2,1)} %constant.48.clone.cf_low) | copy-start | bytes 589828
  17.3 0.7 %copy-start.9 = (s32[1,3]{1,0:T(1,128)S(1)}, s32[1,3]{1,0:T(1,128)}, u32[]{:S(2)}) copy-start(s32[1,3]{1,0:T(1,128)} %pairs.3) | copy-start | bytes 40
  18.0 7.3 %copy-start.7 = (bf16[32,384]{1,0:T(8,128)(2,1)S(1)}, bf16[32,384]{1,0:T(8,128)(2,1)}, u32[]{:S(2)}) copy-start(bf16[32,384]{1,0:T(8,128)(2,1)} %constant.51.clone.lb) | copy-start | bytes 73732
  18.0 7.3 %copy-start.8 = (bf16[2,16,64]{2,1,0:T(8,128)(2,1)S(1)}, bf16[2,16,64]{2,1,0:T(8,128)(2,1)}, u32[]{:S(2)}) copy-start(bf16[2,16,64]{2,1,0:T(8,128)(2,1)} %constant.50.clone.window) | copy-start | bytes 12292
  18.1 5.5 %collective-permute-start.5 = (f32[3,16,128]{2,1,0:T(8,128)S(1)}, f32[3,16,128]{2,1,0:T(8,128)S(1)}, u32[]{:S(2)}, u32[]{:S(2)}) collective-permute-start(f32[3,16,128]{2,1,0:T(8,128)S(1)} %choose.1.fields), channel_id=1, source_target_pairs={{0,8},{1,10},{2,9},{3,12},{4,11},{5,14},{6,13},{7,15},{8,0},{9,2},... | collective-permute-start | bytes 73736 | tf_op jit(solution)/shard_map/ppermute | solution.py:337
  21.4 3.5 %collective-permute-start.6 = (f32[3,16,128]{2,1,0:T(8,128)S(1)}, f32[3,16,128]{2,1,0:T(8,128)S(1)}, u32[]{:S(2)}, u32[]{:S(2)}) collective-permute-start(f32[3,16,128]{2,1,0:T(8,128)S(1)} %choose.1.fields), channel_id=1, source_target_pairs={{0,8},{1,2},{2,1},{3,4},{4,3},{5,6},{6,5},{7,15},{8,0},{9,10},{10,... | collective-permute-start | bytes 73736 | tf_op jit(solution)/shard_map/ppermute | solution.py:337
  21.5 3.7 %collective-permute-start.7 = (f32[3,16,128]{2,1,0:T(8,128)S(1)}, f32[3,16,128]{2,1,0:T(8,128)S(1)}, u32[]{:S(2)}, u32[]{:S(2)}) collective-permute-start(f32[3,16,128]{2,1,0:T(8,128)S(1)} %choose.1.fields), channel_id=1, source_target_pairs={{0,9},{1,8},{2,11},{3,10},{4,13},{5,12},{6,15},{7,14},{8,1},{9,0},... | collective-permute-start | bytes 73736 | tf_op jit(solution)/shard_map/ppermute | solution.py:337
  22.5 2.8 %collective-permute-start.8 = (f32[3,16,128]{2,1,0:T(8,128)S(1)}, f32[3,16,128]{2,1,0:T(8,128)S(1)}, u32[]{:S(2)}, u32[]{:S(2)}) collective-permute-start(f32[3,16,128]{2,1,0:T(8,128)S(1)} %choose.1.fields), channel_id=1, source_target_pairs={{0,8},{1,9},{2,10},{3,11},{4,12},{5,13},{6,14},{7,15},{8,0},{9,1},... | collective-permute-start | bytes 73736 | tf_op jit(solution)/shard_map/ppermute | solution.py:337
  23.6 1.6 %collective-permute-start.9 = (f32[3,16,128]{2,1,0:T(8,128)S(1)}, f32[3,16,128]{2,1,0:T(8,128)S(1)}, u32[]{:S(2)}, u32[]{:S(2)}) collective-permute-start(f32[3,16,128]{2,1,0:T(8,128)S(1)} %choose.1.fields), channel_id=1, source_target_pairs={{0,1},{1,0},{2,3},{3,2},{4,5},{5,4},{6,7},{7,6},{8,9},{9,8},{10,11... | collective-permute-start | bytes 73736 | tf_op jit(solution)/shard_map/ppermute | solution.py:337
